TPU v7x, 256 devices: a whole 4x4x8 slice. The times are simulated.
256 devices in a mesh: section: 16 (over y, x), dp: 16 (over z, core).
Axes of the slice: x: 4, y: 4, z: 8, core: 2. Of those that a mesh axis runs over, the one named last changes fastest.
Arguments:
- hidden_acts: bfloat16 [16, 2048, 28672], P('section', 'dp'), may hold values from -6 to 6
- resid_stream: bfloat16 [16, 2048, 8192], P('section', 'dp'), may hold values from -6 to 6
- norm_scale: float32 [16, 8192], P('section'), may hold values from -1 to 1
- out_grad: bfloat16 [2048, 8192], P('dp'), may hold values from -6 to 6
- lengths: int32 [32], P('dp'), may hold values from 1 to 64, 1792 in all
- proj_in: bfloat16 [16, 64, 28672], P('section'), may hold values from -0.03125 to 0.03125
- proj_out: bfloat16 [16, 64, 8192], P('section'), may hold values from -0.0625 to 0.0625
- queries: bfloat16 [16, 512, 4096], P('section', 'dp'), may hold values from -0.09375 to 0.09375
Outputs:
- scores: float32 [32, 512], P(None, 'dp')
- in_grads: bfloat16 [16, 2048, 8192], P('section', 'dp')
Inputs may be any that keep to these rules, and one draw needn't show every extreme that they name: Some sequence has exactly 64 live tokens; the lengths sum to 1792.
All inputs are finite; a program needn't handle non-finite values. No bound on the sum of `lengths` on one device may be relied on, other than what follows from the above.
Results may differ from a plain program's by a relative error of at most 0.012.
Values may be sent and summed in bfloat16 or wider, within the bound.
No kernel may reach another device: no remote copies, remote signals or barrier semaphores. Data moves between devices by JAX's collectives and lax.ppermute only.
A program may use at most 64 MiB of HBM per device.

v0:
```python
import jax
import jax.numpy as jnp
from jax import lax
from jax.sharding import PartitionSpec as P


def passed_along(value, axis, steps):
    count = lax.axis_size(axis)
    first, last = (max(0, -steps), min(count, count - steps))
    return lax.ppermute(value, axis, [(source, source + steps) for source in range(first, last)])


def chain_back(grad_rows, resid_rows, norm_gain):
    grad_f32 = grad_rows.astype(jnp.float32)
    resid_f32 = resid_rows.astype(jnp.float32)
    inv_rms = lax.rsqrt(jnp.mean(resid_f32 * resid_f32, axis=-1, keepdims=True) + 1e-05)
    weighted = grad_f32 * norm_gain
    inner_mean = jnp.mean(weighted * resid_f32, axis=-1, keepdims=True)
    result = grad_f32 + inv_rms * weighted - resid_f32 * (inv_rms * inv_rms * inv_rms) * inner_mean
    return result.astype(jnp.bfloat16)


def shards(hidden_acts, resid_stream, norm_scale, out_grad, lengths, proj_in, proj_out, queries):
    tok_rows, features = out_grad.shape
    examples = lengths.shape[0]
    seq_len = tok_rows // examples
    rank_size = proj_in.shape[1]
    sections = lax.axis_size("section")
    section_index = lax.axis_index("section")
    resid_rows = resid_stream[0]
    norm_gain = norm_scale[0]
    positions = jnp.arange(seq_len, dtype=jnp.int32)
    live_mask = (positions[None, :] < lengths[:, None]).reshape(tok_rows, 1)
    start_grad = jnp.where(live_mask, out_grad, jnp.zeros_like(out_grad))

    def advance(turn_index, carry):
        incoming, held_grad = carry
        active_section = sections - 1 - turn_index
        held_grad = jnp.where(section_index == active_section, incoming, held_grad)
        passed = passed_along(chain_back(incoming, resid_rows, norm_gain), "section", -1)
        return (passed, held_grad)

    incoming, held_grad = lax.fori_loop(0, sections - 1, advance, (start_grad, start_grad))
    held_grad = jnp.where(section_index == 0, incoming, held_grad)
    in_grad = chain_back(held_grad, resid_rows, norm_gain)
    side_in = jnp.einsum(
        "tf,rf->tr", hidden_acts[0], proj_in[0], preferred_element_type=jnp.float32
    ).astype(jnp.bfloat16)
    side_out = jnp.einsum(
        "td,rd->tr", held_grad, proj_out[0], preferred_element_type=jnp.float32
    ).astype(jnp.bfloat16)
    outer = jnp.einsum(
        "eto,eti->eoi",
        side_out.reshape(examples, seq_len, rank_size),
        side_in.reshape(examples, seq_len, rank_size),
        preferred_element_type=jnp.float32,
    )
    example_grads = outer.reshape(examples, rank_size * rank_size).astype(jnp.bfloat16)
    gathered = lax.all_gather(example_grads, "dp", axis=0, tiled=True)
    partial_value = jnp.einsum(
        "ek,qk->eq", gathered, queries[0], preferred_element_type=jnp.float32
    )
    grads_f32 = gathered.astype(jnp.float32)
    squares = jnp.sum(grads_f32 * grads_f32, axis=1)
    summed, squares = lax.psum((partial_value, squares), "section")
    scores = summed / jnp.sqrt(squares / (sections * rank_size * rank_size) + 1e-06)[:, None]
    return (scores, in_grad[None])


def solution(mesh):
    in_specs = (
        P("section", "dp", None),
        P("section", "dp", None),
        P("section", None),
        P("dp", None),
        P("dp"),
        P("section", None, None),
        P("section", None, None),
        P("section", "dp", None),
    )
    out_specs = (P(None, "dp"), P("section", "dp", None))
    return jax.shard_map(shards, mesh=mesh, in_specs=in_specs, out_specs=out_specs, check_vma=False)
```

profile of v0, /device:TPU:1, one launch (start us, length us, event | category | flops | bytes accessed | tf_op | source)
XLA Modules:
  0.0 893.7 jit_solution(13319103283085233230)
XLA Ops:
  4.7 771.2 %while.15 = (s32[]{:T(128)}, bf16[128,8192]{1,0:T(8,128)(2,1)S(1)}, bf16[128,8192]{1,0:T(8,128)(2,1)}, bf16[128,8192]{1,0:T(8,128)(2,1)}, f32[1,8192]{1,0:T(1,128)S(1)}, /*index=5*/s32[]{:T(128)}, s32[]{:T(128)}, s32[]{:T(128)}) while((s32[]{:T(128)}, bf16[128,8192]{1,0:T(8,128)(2,1)S(1)}, bf16[128,8192]{1,0:T(8,128)(2,1)}, ...), condition=%wide.region_3.4_spmd, body=%wide.region_0.3_spmd.sunk | while | flops 17826176 | bytes 37819564 | solution.py:43
  7.5 3.0 fusion.31
  11.8 3.1 broadcast_select_fusion.5
  14.9 42.8 %collective-permute-done = bf16[128,8192]{1,0:T(8,128)(2,1)} collective-permute-done((bf16[128,8192]{1,0:T(8,128)(2,1)}, bf16[128,8192]{1,0:T(8,128)(2,1)}, u32[]{:S(2)}, u32[]{:S(2)}) %collective-permute-start) | collective-permute-done | bytes 2097184 | tf_op jit(solution)/shard_map/while/body/eval_jaxpr/ppermute | solution.py:10
  62.1 3.0 fusion.31
  66.4 3.1 broadcast_select_fusion.5
  69.5 45.4 %collective-permute-done = bf16[128,8192]{1,0:T(8,128)(2,1)} collective-permute-done((bf16[128,8192]{1,0:T(8,128)(2,1)}, bf16[128,8192]{1,0:T(8,128)(2,1)}, u32[]{:S(2)}, u32[]{:S(2)}) %collective-permute-start) | collective-permute-done | bytes 2097184 | tf_op jit(solution)/shard_map/while/body/eval_jaxpr/ppermute | solution.py:10
  123.6 3.1 broadcast_select_fusion.5
  126.7 42.4 %collective-permute-done = bf16[128,8192]{1,0:T(8,128)(2,1)} collective-permute-done((bf16[128,8192]{1,0:T(8,128)(2,1)}, bf16[128,8192]{1,0:T(8,128)(2,1)}, u32[]{:S(2)}, u32[]{:S(2)}) %collective-permute-start) | collective-permute-done | bytes 2097184 | tf_op jit(solution)/shard_map/while/body/eval_jaxpr/ppermute | solution.py:10
  173.6 3.0 fusion.31
  177.8 3.1 broadcast_select_fusion.5
  181.0 44.5 %collective-permute-done = bf16[128,8192]{1,0:T(8,128)(2,1)} collective-permute-done((bf16[128,8192]{1,0:T(8,128)(2,1)}, bf16[128,8192]{1,0:T(8,128)(2,1)}, u32[]{:S(2)}, u32[]{:S(2)}) %collective-permute-start) | collective-permute-done | bytes 2097184 | tf_op jit(solution)/shard_map/while/body/eval_jaxpr/ppermute | solution.py:10
  229.9 3.0 fusion.31
  234.2 3.1 broadcast_select_fusion.5
  237.3 42.7 %collective-permute-done = bf16[128,8192]{1,0:T(8,128)(2,1)} collective-permute-done((bf16[128,8192]{1,0:T(8,128)(2,1)}, bf16[128,8192]{1,0:T(8,128)(2,1)}, u32[]{:S(2)}, u32[]{:S(2)}) %collective-permute-start) | collective-permute-done | bytes 2097184 | tf_op jit(solution)/shard_map/while/body/eval_jaxpr/ppermute | solution.py:10
  284.4 3.0 fusion.31
  288.7 3.1 broadcast_select_fusion.5
  291.8 41.8 %collective-permute-done = bf16[128,8192]{1,0:T(8,128)(2,1)} collective-permute-done((bf16[128,8192]{1,0:T(8,128)(2,1)}, bf16[128,8192]{1,0:T(8,128)(2,1)}, u32[]{:S(2)}, u32[]{:S(2)}) %collective-permute-start) | collective-permute-done | bytes 2097184 | tf_op jit(solution)/shard_map/while/body/eval_jaxpr/ppermute | solution.py:10
  338.0 3.0 fusion.31
  342.2 3.1 broadcast_select_fusion.5
  345.4 40.8 %collective-permute-done = bf16[128,8192]{1,0:T(8,128)(2,1)} collective-permute-done((bf16[128,8192]{1,0:T(8,128)(2,1)}, bf16[128,8192]{1,0:T(8,128)(2,1)}, u32[]{:S(2)}, u32[]{:S(2)}) %collective-permute-start) | collective-permute-done | bytes 2097184 | tf_op jit(solution)/shard_map/while/body/eval_jaxpr/ppermute | solution.py:10
  390.6 3.0 fusion.31
  394.9 3.1 broadcast_select_fusion.5
  398.0 39.9 %collective-permute-done = bf16[128,8192]{1,0:T(8,128)(2,1)} collective-permute-done((bf16[128,8192]{1,0:T(8,128)(2,1)}, bf16[128,8192]{1,0:T(8,128)(2,1)}, u32[]{:S(2)}, u32[]{:S(2)}) %collective-permute-start) | collective-permute-done | bytes 2097184 | tf_op jit(solution)/shard_map/while/body/eval_jaxpr/ppermute | solution.py:10
  442.4 3.0 fusion.31
  446.6 3.1 broadcast_select_fusion.5
  449.8 39.0 %collective-permute-done = bf16[128,8192]{1,0:T(8,128)(2,1)} collective-permute-done((bf16[128,8192]{1,0:T(8,128)(2,1)}, bf16[128,8192]{1,0:T(8,128)(2,1)}, u32[]{:S(2)}, u32[]{:S(2)}) %collective-permute-start) | collective-permute-done | bytes 2097184 | tf_op jit(solution)/shard_map/while/body/eval_jaxpr/ppermute | solution.py:10
  493.2 3.0 fusion.31
  497.4 3.1 broadcast_select_fusion.5
  500.6 38.1 %collective-permute-done = bf16[128,8192]{1,0:T(8,128)(2,1)} collective-permute-done((bf16[128,8192]{1,0:T(8,128)(2,1)}, bf16[128,8192]{1,0:T(8,128)(2,1)}, u32[]{:S(2)}, u32[]{:S(2)}) %collective-permute-start) | collective-permute-done | bytes 2097184 | tf_op jit(solution)/shard_map/while/body/eval_jaxpr/ppermute | solution.py:10
  543.1 3.0 fusion.31
  547.3 3.1 broadcast_select_fusion.5
  550.5 37.2 %collective-permute-done = bf16[128,8192]{1,0:T(8,128)(2,1)} collective-permute-done((bf16[128,8192]{1,0:T(8,128)(2,1)}, bf16[128,8192]{1,0:T(8,128)(2,1)}, u32[]{:S(2)}, u32[]{:S(2)}) %collective-permute-start) | collective-permute-done | bytes 2097184 | tf_op jit(solution)/shard_map/while/body/eval_jaxpr/ppermute | solution.py:10
  592.0 3.0 fusion.31
  596.3 3.1 broadcast_select_fusion.5
  599.5 36.2 %collective-permute-done = bf16[128,8192]{1,0:T(8,128)(2,1)} collective-permute-done((bf16[128,8192]{1,0:T(8,128)(2,1)}, bf16[128,8192]{1,0:T(8,128)(2,1)}, u32[]{:S(2)}, u32[]{:S(2)}) %collective-permute-start) | collective-permute-done | bytes 2097184 | tf_op jit(solution)/shard_map/while/body/eval_jaxpr/ppermute | solution.py:10
  644.4 3.1 broadcast_select_fusion.5
  647.5 35.3 %collective-permute-done = bf16[128,8192]{1,0:T(8,128)(2,1)} collective-permute-done((bf16[128,8192]{1,0:T(8,128)(2,1)}, bf16[128,8192]{1,0:T(8,128)(2,1)}, u32[]{:S(2)}, u32[]{:S(2)}) %collective-permute-start) | collective-permute-done | bytes 2097184 | tf_op jit(solution)/shard_map/while/body/eval_jaxpr/ppermute | solution.py:10
  687.2 3.0 fusion.31
  691.5 3.1 broadcast_select_fusion.5
  694.6 34.4 %collective-permute-done = bf16[128,8192]{1,0:T(8,128)(2,1)} collective-permute-done((bf16[128,8192]{1,0:T(8,128)(2,1)}, bf16[128,8192]{1,0:T(8,128)(2,1)}, u32[]{:S(2)}, u32[]{:S(2)}) %collective-permute-start) | collective-permute-done | bytes 2097184 | tf_op jit(solution)/shard_map/while/body/eval_jaxpr/ppermute | solution.py:10
  737.7 3.1 broadcast_select_fusion.5
  740.8 33.5 %collective-permute-done = bf16[128,8192]{1,0:T(8,128)(2,1)} collective-permute-done((bf16[128,8192]{1,0:T(8,128)(2,1)}, bf16[128,8192]{1,0:T(8,128)(2,1)}, u32[]{:S(2)}, u32[]{:S(2)}) %collective-permute-start) | collective-permute-done | bytes 2097184 | tf_op jit(solution)/shard_map/while/body/eval_jaxpr/ppermute | solution.py:10
  775.9 3.1 fusion.11
  781.3 6.9 fusion.16
  788.6 35.5 %all-gather = bf16[16,2,4096]{2,1,0:T(2,128)(2,1)} all-gather(bf16[1,2,4096]{2,1,0:T(2,128)(2,1)S(1)} %reshape.73), channel_id=1, replica_groups=mesh['section'=16,'dp'=16] {'dp'}, dimensions={0}, use_global_device_ids=true | all-gather | bytes 278528 | tf_op jit(solution)/shard_map/all_gather | solution.py:59
  826.5 61.9 %all-reduce = (f32[32,32]{1,0:T(8,128)S(1)}, f32[32]{0:T(128)S(1)}) all-reduce(f32[32,32]{1,0:T(8,128)S(1)} %fusion.22, f32[32]{0:T(128)S(1)} %multiply_reduce_fusion), channel_id=1, replica_groups=mesh['section'=16,'dp'=16] {'section'}, use_global_device_ids=true, to_apply=%region_4.5 | all-reduce | flops 1056 | bytes 8448 | tf_op jit(solution)/shard_map/psum | solution.py:65
  889.2 4.5 fusion.15
  (117 shorter events, 103.9 us)
Async XLA Ops:
  0.6 779.7 %copy-start = (bf16[1,64,8192]{2,1,0:T(8,128)(2,1)S(1)}, bf16[1,64,8192]{2,1,0:T(8,128)(2,1)}, u32[]{:S(2)}) copy-start(bf16[1,64,8192]{2,1,0:T(8,128)(2,1)} %param.16) | copy-start | bytes 3145732
  1.5 3.1 copy-start.4
  4.7 2.8 copy-start.1
  10.5 47.3 %collective-permute-start = (bf16[128,8192]{1,0:T(8,128)(2,1)}, bf16[128,8192]{1,0:T(8,128)(2,1)}, u32[]{:S(2)}, u32[]{:S(2)}) collective-permute-start(bf16[128,8192]{1,0:T(8,128)(2,1)} %fusion.31), channel_id=1, source_target_pairs={{16,0},{32,16},{48,32},{64,48},{80,64},{96,80},{112,96},{128,112},... | collective-permute-start | bytes 6291464 | tf_op jit(solution)/shard_map/while/body/eval_jaxpr/ppermute | solution.py:10
  59.3 2.8 copy-start.1
  65.1 49.8 %collective-permute-start = (bf16[128,8192]{1,0:T(8,128)(2,1)}, bf16[128,8192]{1,0:T(8,128)(2,1)}, u32[]{:S(2)}, u32[]{:S(2)}) collective-permute-start(bf16[128,8192]{1,0:T(8,128)(2,1)} %fusion.31), channel_id=1, source_target_pairs={{16,0},{32,16},{48,32},{64,48},{80,64},{96,80},{112,96},{128,112},... | collective-permute-start | bytes 6291464 | tf_op jit(solution)/shard_map/while/body/eval_jaxpr/ppermute | solution.py:10
  116.5 2.8 copy-start.1
  122.3 46.9 %collective-permute-start = (bf16[128,8192]{1,0:T(8,128)(2,1)}, bf16[128,8192]{1,0:T(8,128)(2,1)}, u32[]{:S(2)}, u32[]{:S(2)}) collective-permute-start(bf16[128,8192]{1,0:T(8,128)(2,1)} %fusion.31), channel_id=1, source_target_pairs={{16,0},{32,16},{48,32},{64,48},{80,64},{96,80},{112,96},{128,112},... | collective-permute-start | bytes 6291464 | tf_op jit(solution)/shard_map/while/body/eval_jaxpr/ppermute | solution.py:10
  170.7 2.8 copy-start.1
  176.5 48.9 %collective-permute-start = (bf16[128,8192]{1,0:T(8,128)(2,1)}, bf16[128,8192]{1,0:T(8,128)(2,1)}, u32[]{:S(2)}, u32[]{:S(2)}) collective-permute-start(bf16[128,8192]{1,0:T(8,128)(2,1)} %fusion.31), channel_id=1, source_target_pairs={{16,0},{32,16},{48,32},{64,48},{80,64},{96,80},{112,96},{128,112},... | collective-permute-start | bytes 6291464 | tf_op jit(solution)/shard_map/while/body/eval_jaxpr/ppermute | solution.py:10
  227.1 2.8 copy-start.1
  232.9 47.1 %collective-permute-start = (bf16[128,8192]{1,0:T(8,128)(2,1)}, bf16[128,8192]{1,0:T(8,128)(2,1)}, u32[]{:S(2)}, u32[]{:S(2)}) collective-permute-start(bf16[128,8192]{1,0:T(8,128)(2,1)} %fusion.31), channel_id=1, source_target_pairs={{16,0},{32,16},{48,32},{64,48},{80,64},{96,80},{112,96},{128,112},... | collective-permute-start | bytes 6291464 | tf_op jit(solution)/shard_map/while/body/eval_jaxpr/ppermute | solution.py:10
  281.6 2.8 copy-start.1
  287.4 46.2 %collective-permute-start = (bf16[128,8192]{1,0:T(8,128)(2,1)}, bf16[128,8192]{1,0:T(8,128)(2,1)}, u32[]{:S(2)}, u32[]{:S(2)}) collective-permute-start(bf16[128,8192]{1,0:T(8,128)(2,1)} %fusion.31), channel_id=1, source_target_pairs={{16,0},{32,16},{48,32},{64,48},{80,64},{96,80},{112,96},{128,112},... | collective-permute-start | bytes 6291464 | tf_op jit(solution)/shard_map/while/body/eval_jaxpr/ppermute | solution.py:10
  335.1 2.8 copy-start.1
  340.9 45.3 %collective-permute-start = (bf16[128,8192]{1,0:T(8,128)(2,1)}, bf16[128,8192]{1,0:T(8,128)(2,1)}, u32[]{:S(2)}, u32[]{:S(2)}) collective-permute-start(bf16[128,8192]{1,0:T(8,128)(2,1)} %fusion.31), channel_id=1, source_target_pairs={{16,0},{32,16},{48,32},{64,48},{80,64},{96,80},{112,96},{128,112},... | collective-permute-start | bytes 6291464 | tf_op jit(solution)/shard_map/while/body/eval_jaxpr/ppermute | solution.py:10
  387.8 2.8 copy-start.1
  393.6 44.4 %collective-permute-start = (bf16[128,8192]{1,0:T(8,128)(2,1)}, bf16[128,8192]{1,0:T(8,128)(2,1)}, u32[]{:S(2)}, u32[]{:S(2)}) collective-permute-start(bf16[128,8192]{1,0:T(8,128)(2,1)} %fusion.31), channel_id=1, source_target_pairs={{16,0},{32,16},{48,32},{64,48},{80,64},{96,80},{112,96},{128,112},... | collective-permute-start | bytes 6291464 | tf_op jit(solution)/shard_map/while/body/eval_jaxpr/ppermute | solution.py:10
  439.5 2.8 copy-start.1
  445.3 43.4 %collective-permute-start = (bf16[128,8192]{1,0:T(8,128)(2,1)}, bf16[128,8192]{1,0:T(8,128)(2,1)}, u32[]{:S(2)}, u32[]{:S(2)}) collective-permute-start(bf16[128,8192]{1,0:T(8,128)(2,1)} %fusion.31), channel_id=1, source_target_pairs={{16,0},{32,16},{48,32},{64,48},{80,64},{96,80},{112,96},{128,112},... | collective-permute-start | bytes 6291464 | tf_op jit(solution)/shard_map/while/body/eval_jaxpr/ppermute | solution.py:10
  490.4 2.8 copy-start.1
  496.2 42.5 %collective-permute-start = (bf16[128,8192]{1,0:T(8,128)(2,1)}, bf16[128,8192]{1,0:T(8,128)(2,1)}, u32[]{:S(2)}, u32[]{:S(2)}) collective-permute-start(bf16[128,8192]{1,0:T(8,128)(2,1)} %fusion.31), channel_id=1, source_target_pairs={{16,0},{32,16},{48,32},{64,48},{80,64},{96,80},{112,96},{128,112},... | collective-permute-start | bytes 6291464 | tf_op jit(solution)/shard_map/while/body/eval_jaxpr/ppermute | solution.py:10
  540.3 2.8 copy-start.1
  546.0 41.6 %collective-permute-start = (bf16[128,8192]{1,0:T(8,128)(2,1)}, bf16[128,8192]{1,0:T(8,128)(2,1)}, u32[]{:S(2)}, u32[]{:S(2)}) collective-permute-start(bf16[128,8192]{1,0:T(8,128)(2,1)} %fusion.31), channel_id=1, source_target_pairs={{16,0},{32,16},{48,32},{64,48},{80,64},{96,80},{112,96},{128,112},... | collective-permute-start | bytes 6291464 | tf_op jit(solution)/shard_map/while/body/eval_jaxpr/ppermute | solution.py:10
  589.2 2.8 copy-start.1
  595.0 40.7 %collective-permute-start = (bf16[128,8192]{1,0:T(8,128)(2,1)}, bf16[128,8192]{1,0:T(8,128)(2,1)}, u32[]{:S(2)}, u32[]{:S(2)}) collective-permute-start(bf16[128,8192]{1,0:T(8,128)(2,1)} %fusion.31), channel_id=1, source_target_pairs={{16,0},{32,16},{48,32},{64,48},{80,64},{96,80},{112,96},{128,112},... | collective-permute-start | bytes 6291464 | tf_op jit(solution)/shard_map/while/body/eval_jaxpr/ppermute | solution.py:10
  637.3 2.8 copy-start.1
  643.1 39.7 %collective-permute-start = (bf16[128,8192]{1,0:T(8,128)(2,1)}, bf16[128,8192]{1,0:T(8,128)(2,1)}, u32[]{:S(2)}, u32[]{:S(2)}) collective-permute-start(bf16[128,8192]{1,0:T(8,128)(2,1)} %fusion.31), channel_id=1, source_target_pairs={{16,0},{32,16},{48,32},{64,48},{80,64},{96,80},{112,96},{128,112},... | collective-permute-start | bytes 6291464 | tf_op jit(solution)/shard_map/while/body/eval_jaxpr/ppermute | solution.py:10
  684.4 2.8 copy-start.1
  690.2 38.8 %collective-permute-start = (bf16[128,8192]{1,0:T(8,128)(2,1)}, bf16[128,8192]{1,0:T(8,128)(2,1)}, u32[]{:S(2)}, u32[]{:S(2)}) collective-permute-start(bf16[128,8192]{1,0:T(8,128)(2,1)} %fusion.31), channel_id=1, source_target_pairs={{16,0},{32,16},{48,32},{64,48},{80,64},{96,80},{112,96},{128,112},... | collective-permute-start | bytes 6291464 | tf_op jit(solution)/shard_map/while/body/eval_jaxpr/ppermute | solution.py:10
  730.6 2.8 copy-start.1
  736.4 37.9 %collective-permute-start = (bf16[128,8192]{1,0:T(8,128)(2,1)}, bf16[128,8192]{1,0:T(8,128)(2,1)}, u32[]{:S(2)}, u32[]{:S(2)}) collective-permute-start(bf16[128,8192]{1,0:T(8,128)(2,1)} %fusion.31), channel_id=1, source_target_pairs={{16,0},{32,16},{48,32},{64,48},{80,64},{96,80},{112,96},{128,112},... | collective-permute-start | bytes 6291464 | tf_op jit(solution)/shard_map/while/body/eval_jaxpr/ppermute | solution.py:10
  779.0 1.3 copy-start.3
  781.3 107.9 %copy-start.2 = (bf16[128,8192]{1,0:T(8,128)(2,1)S(1)}, bf16[128,8192]{1,0:T(8,128)(2,1)}, u32[]{:S(2)}) copy-start(bf16[128,8192]{1,0:T(8,128)(2,1)} %get-tuple-element.209) | copy-start | bytes 6291460
where the time goes:
time: 906 us; the launch traced here: 894 us
  waiting for transfers between devices  594 us (66%)
  other arithmetic  145 us (16%)
  blocking collectives  97.5 us (11%)
  local copies, waits for them, and re-layouts  28 us (3%)
  starting transfers between devices  19.2 us (2%)
  matrix products  9.09 us (1%)
    ppermute x15, waiting for transfers between devices, passed_along(): lax.ppermute(value, axis, [(source, source + steps) for source in range(f...  594 us
    psum x1, blocking collectives, shards(): summed, squares = lax.psum((partial_value, squares), 'section')  61.9 us
    select_n x15, other arithmetic, advance(): held_grad = jnp.where(section_index == active_section, incoming, held_grad)  47 us
    reduce_sum x16, other arithmetic, chain_back(): jnp.mean(resid_f32 * resid_f32, axis=-1, keepdims=True) + 1e-05  45 us
    convert_element_type x15, other arithmetic, chain_back(): return result.astype(jnp.bfloat16)  44.6 us
    all_gather x1, blocking collectives, shards(): gathered = lax.all_gather(example_grads, 'dp', axis=0, tiled=True)  35.5 us
    while x45, local copies, waits for them, and re-layouts  23.9 us
    ppermute x15, starting transfers between devices, passed_along(): lax.ppermute(value, axis, [(source, source + steps) for source in range(f...  19.2 us
  transfers between devices with their start and end apart: 15, of which 15 were waited for; matrix products, arithmetic and copies ran while one was open for 5% of the time, Pallas kernels for 0%

commit v1 on v0

v1 whole, which is shorter than its diff:
```python
import jax
import jax.numpy as jnp
from jax import lax
from jax.experimental import pallas as pl
from jax.experimental.pallas import tpu as pltpu
from jax.sharding import PartitionSpec as P

EPS = 1e-05
LANES = 128
SUBLANES = 16


def chain_kernel(recv_ref, top_ref, out_ref, gain_ref, *, sections, width, lanes_per):
    blocks = top_ref.shape[0]
    gain_blocks = gain_ref.shape[0] // SUBLANES
    step = 4
    chunks = blocks // step
    out_ref[sections - 1] = top_ref[...]

    def one(turn, _):
        s = sections - 1 - turn
        hi = recv_ref[s, pl.ds(blocks, gain_blocks)].astype(jnp.float32)
        lo = recv_ref[s, pl.ds(blocks + gain_blocks, gain_blocks)].astype(jnp.float32)
        gain_ref[...] = (hi + lo).reshape(gain_blocks * SUBLANES, LANES)

        def gain_of(k):
            return jnp.stack(
                [
                    jnp.concatenate(
                        [
                            jnp.broadcast_to(gain_ref[pl.ds(2 * i, 1), :], (8, LANES)),
                            jnp.broadcast_to(gain_ref[pl.ds(2 * i + 1, 1), :], (8, LANES)),
                        ],
                        axis=0,
                    )
                    for i in range(k * step, (k + 1) * step)
                ]
            )

        square = jnp.zeros((step, SUBLANES, LANES), jnp.float32)
        inner = jnp.zeros((step, SUBLANES, LANES), jnp.float32)
        for k in range(chunks):
            x = recv_ref[s, pl.ds(k * step, step)].astype(jnp.float32)
            g = out_ref[s, pl.ds(k * step, step)].astype(jnp.float32)
            square = square + x * x
            inner = inner + g * gain_of(k) * x

        def total(v):
            v = jnp.sum(v, axis=0)
            v = v[:8] + v[8:]
            v = jnp.sum(v, axis=-1, keepdims=True)
            return jnp.concatenate([v, v], axis=0)[None]

        inv = lax.rsqrt(total(square) / width + EPS)
        pull = inv * inv * inv * (total(inner) / width)
        for k in range(chunks):
            x = recv_ref[s, pl.ds(k * step, step)].astype(jnp.float32)
            g = out_ref[s, pl.ds(k * step, step)].astype(jnp.float32)
            new = g + inv * (g * gain_of(k)) - x * pull
            out_ref[s - 1, pl.ds(k * step, step)] = new.astype(jnp.bfloat16)
        return 0

    lax.fori_loop(0, sections - 1, one, 0)


def chain_all(recv, top):
    sections = recv.shape[0]
    blocks = top.shape[0]
    gain_blocks = (recv.shape[1] - blocks) // 2
    width = blocks * 2 * LANES

    def body(recv_ref, top_ref, out_ref, gain_ref):
        chain_kernel(recv_ref, top_ref, out_ref, gain_ref, sections=sections, width=width, lanes_per=LANES)

    return pl.pallas_call(
        body,
        out_shape=jax.ShapeDtypeStruct((sections, blocks, SUBLANES, LANES), jnp.bfloat16),
        in_specs=[pl.BlockSpec(memory_space=pltpu.VMEM)] * 2,
        out_specs=pl.BlockSpec(memory_space=pltpu.VMEM),
        scratch_shapes=[pltpu.VMEM((gain_blocks * SUBLANES, LANES), jnp.float32)],
        compiler_params=pltpu.CompilerParams(vmem_limit_bytes=24 * 1024 * 1024),
        name="chain_all",
    )(recv, top)


def to_tiles(rows):
    count, width = rows.shape
    tiles = rows.reshape(count // 8, 8, width // LANES, LANES).transpose(0, 2, 1, 3)
    return tiles.reshape(count // 8, width // (2 * LANES), SUBLANES, LANES)


def from_tiles(tiles):
    groups, blocks = tiles.shape[:2]
    rows = tiles.reshape(groups, blocks * 2, 8, LANES).transpose(0, 2, 1, 3)
    return rows.reshape(groups * 8, blocks * 2 * LANES)


def chain_back(grad_rows, resid_rows, norm_gain):
    grad_f32 = grad_rows.astype(jnp.float32)
    resid_f32 = resid_rows.astype(jnp.float32)
    inv_rms = lax.rsqrt(jnp.mean(resid_f32 * resid_f32, axis=-1, keepdims=True) + EPS)
    weighted = grad_f32 * norm_gain
    inner_mean = jnp.mean(weighted * resid_f32, axis=-1, keepdims=True)
    result = grad_f32 + inv_rms * weighted - resid_f32 * (inv_rms * inv_rms * inv_rms) * inner_mean
    return result.astype(jnp.bfloat16)


def shards(hidden_acts, resid_stream, norm_scale, out_grad, lengths, proj_in, proj_out, queries):
    tok_rows, features = out_grad.shape
    examples = lengths.shape[0]
    seq_len = tok_rows // examples
    rank_size = proj_in.shape[1]
    sections = lax.axis_size("section")
    ranks = lax.axis_size("dp")
    me = lax.axis_index("section")
    resid_rows = resid_stream[0]
    norm_gain = norm_scale[0]

    own = tok_rows // sections
    gain_hi = lax.reduce_precision(norm_gain, 8, 7)
    gain_halves = jnp.concatenate([gain_hi, norm_gain - gain_hi]).astype(jnp.bfloat16)
    gain_tiles = gain_halves.reshape(-1, SUBLANES, LANES)
    send = jnp.concatenate(
        [to_tiles(resid_rows), jnp.broadcast_to(gain_tiles[None], (sections,) + gain_tiles.shape)], axis=1
    )
    recv = lax.all_to_all(send, "section", 0, 0)

    own_rows = lax.dynamic_slice_in_dim(out_grad, me * own, own, axis=0)
    own_slots = me * own + jnp.arange(own, dtype=jnp.int32)
    own_live = own_slots % seq_len < jnp.take(lengths, own_slots // seq_len)
    own_top = jnp.where(own_live[:, None], own_rows, jnp.zeros_like(own_rows))
    grads = chain_all(recv, to_tiles(own_top)[0])
    held_grad = from_tiles(lax.all_to_all(grads, "section", 0, 0))

    side_in = jnp.einsum(
        "tf,rf->tr", hidden_acts[0], proj_in[0], preferred_element_type=jnp.float32
    ).astype(jnp.bfloat16)
    side_out = jnp.einsum(
        "td,rd->tr", held_grad, proj_out[0], preferred_element_type=jnp.float32
    ).astype(jnp.bfloat16)
    in_grad = chain_back(held_grad, resid_rows, norm_gain)
    outer = jnp.einsum(
        "eto,eti->eoi",
        side_out.reshape(examples, seq_len, rank_size),
        side_in.reshape(examples, seq_len, rank_size),
        preferred_element_type=jnp.float32,
    )
    example_grads = outer.reshape(examples, rank_size * rank_size).astype(jnp.bfloat16)
    spread = jnp.broadcast_to(example_grads[None], (ranks,) + example_grads.shape)
    gathered = lax.all_to_all(spread, "dp", 0, 0).reshape(ranks * examples, rank_size * rank_size)
    partial_value = jnp.einsum(
        "ek,qk->eq", gathered, queries[0], preferred_element_type=jnp.float32
    )
    grads_f32 = gathered.astype(jnp.float32)
    squares = jnp.sum(grads_f32 * grads_f32, axis=1, keepdims=True)
    both = jnp.concatenate([partial_value, squares], axis=1)
    parts = lax.all_to_all(jnp.broadcast_to(both[None], (sections,) + both.shape), "section", 0, 0)
    summed = jnp.sum(parts, axis=0)
    scores = summed[:, :-1] / jnp.sqrt(summed[:, -1:] / (sections * rank_size * rank_size) + 1e-06)
    return (scores, in_grad[None])


def solution(mesh):
    in_specs = (
        P("section", "dp", None),
        P("section", "dp", None),
        P("section", None),
        P("dp", None),
        P("dp"),
        P("section", None, None),
        P("section", None, None),
        P("section", "dp", None),
    )
    out_specs = (P(None, "dp"), P("section", "dp", None))
    return jax.shard_map(shards, mesh=mesh, in_specs=in_specs, out_specs=out_specs, check_vma=False)
```

time: 906 us -> 137 us (0.15); the launches traced: 894 us -> 136 us
  waiting for transfers between devices: 594 us -> 69.2 us
  other arithmetic: 145 us -> 14.8 us
  blocking collectives: 97.5 us -> 0 us
  local copies, waits for them, and re-layouts: 28 us -> 4.75 us
    ppermute x15 -> x0, waiting for transfers between devices: 594 us -> none  [passed_along(): lax.ppermute(value, axis, [(source, source + steps) for source in range(f...]
    all_to_all x0 -> x4, waiting for transfers between devices: none -> 69.2 us  [the longest x1 37.2 us: shards(): recv = lax.all_to_all(send, 'section', 0, 0)]
    psum x1 -> x0, blocking collectives: 61.9 us -> none  [shards(): summed, squares = lax.psum((partial_value, squares), 'section')]
    select_n x16 -> x2, other arithmetic: 48.8 us -> 1.01 us  [the longest x1 1 us: shards(): own_top = jnp.where(own_live[:, None], own_rows, jnp.zeros_like(own_rows))]
    reduce_sum x17 -> x4, other arithmetic: 45.2 us -> 3.24 us  [the longest x1 2.37 us: chain_back(): inner_mean = jnp.mean(weighted * resid_f32, axis=-1, keepdims=True)]
    convert_element_type x15 -> x1, other arithmetic: 44.6 us -> 4.53 us  [chain_back(): return result.astype(jnp.bfloat16)]
    all_gather x1 -> x0, blocking collectives: 35.5 us -> none  [shards(): gathered = lax.all_gather(example_grads, 'dp', axis=0, tiled=True)]
    all_to_all x0 -> x4, starting transfers between devices: none -> 28.1 us  [the longest x1 12.4 us: shards(): lax.all_to_all(spread, 'dp', 0, 0)]
  transfers between devices with their start and end apart: 15 -> 4, of which waited for: 15 -> 4; matrix products, arithmetic and copies ran while one was open for 5% -> 12% of each run, Pallas kernels for 0% -> 0%
where the time goes in v1:
time: 137 us; the launch traced here: 136 us
  waiting for transfers between devices  69.2 us (51%)
  starting transfers between devices  28.1 us (21%)
  other arithmetic  14.8 us (11%)
  matrix products  10.7 us (8%)
  Pallas kernels  7.57 us (6%)
  local copies, waits for them, and re-layouts  4.75 us (3%)
    all_to_all x1, waiting for transfers between devices, shards(): recv = lax.all_to_all(send, 'section', 0, 0)  37.2 us
    all_to_all x1, waiting for transfers between devices, shards(): held_grad = from_tiles(lax.all_to_all(grads, 'section', 0, 0))  20.1 us
    all_to_all x1, starting transfers between devices, shards(): lax.all_to_all(spread, 'dp', 0, 0)  12.4 us
    all_to_all x1, waiting for transfers between devices, shards(): lax.all_to_all(spread, 'dp', 0, 0)  9.24 us
    all_to_all x1, starting transfers between devices, shards(): recv = lax.all_to_all(send, 'section', 0, 0)  7.76 us
    pallas_call x1, Pallas kernels, chain_all(): pl.pallas_call(body, out_shape=jax.ShapeDtypeStruct((sections, blocks, SU...  7.57 us
    dot_general x1, matrix products, shards(): jnp.einsum('tf,rf->tr', hidden_acts[0], proj_in[0], preferred_element_typ...  6.93 us
    convert_element_type x1, other arithmetic, chain_back(): return result.astype(jnp.bfloat16)  4.53 us
  transfers between devices with their start and end apart: 4, of which 4 were waited for; matrix products, arithmetic and copies ran while one was open for 12% of the time, Pallas kernels for 0%

profile of v1, /device:TPU:1, one launch (start us, length us, event | category | flops | bytes accessed | tf_op | source)
XLA Modules:
  0.0 136.0 jit_solution(14830341814760532805)
XLA Ops:
  0.6 0.0 copy-start
  0.6 0.9 reduce-precision_convert_fusion
  1.5 0.1 broadcast_in_dim.20
  1.6 3.4 %pad_maximum_fusion = bf16[16,40,16,128]{3,2,1,0:T(8,128)(2,1)} fusion(bf16[16,8,16,128]{3,2,1,0:T(8,128)(2,1)S(1)} %broadcast_in_dim.20, bf16[16,32,16,128]{3,2,1,0:T(8,128)(2,1)} %bitcast.56), kind=kLoop, calls=%fused_computation.17 | loop fusion | flops 1310720 | bytes 5242880 | tf_op jit(solution)/shard_map/concatenate | solution.py:123
  5.0 0.0 copy-start.1
  5.0 7.8 %all-to-all-start = ((bf16[16,40,16,128]{3,2,1,0:T(8,128)(2,1)}), bf16[16,40,16,128]{3,2,1,0:T(8,128)(2,1)}, u32[]{:S(2)}, u32[]{:S(2)}) async-start(bf16[16,40,16,128]{3,2,1,0:T(8,128)(2,1)} %pad_maximum_fusion), calls=%async_computation | async-start | bytes 5242880 | tf_op jit(solution)/shard_map/all_to_all | solution.py:126
  12.8 0.0 copy-done.1
  12.8 0.6 gather_fusion
  13.5 1.0 dynamic-slice_select_fusion
  14.5 37.2 %all-to-all-done.recv_ref = bf16[16,40,16,128]{3,2,1,0:T(8,128)(2,1)} async-done(((bf16[16,40,16,128]{3,2,1,0:T(8,128)(2,1)}), bf16[16,40,16,128]{3,2,1,0:T(8,128)(2,1)}, u32[]{:S(2)}, u32[]{:S(2)}) %all-to-all-start) | async-done | bytes 2621472 | tf_op jit(solution)/shard_map/all_to_all | solution.py:126
  51.7 7.6 %chain_all.1 = bf16[16,32,16,128]{3,2,1,0:T(8,128)(2,1)} custom-call(bf16[16,40,16,128]{3,2,1,0:T(8,128)(2,1)} %all-to-all-done.recv_ref, bf16[32,16,128]{2,1,0:T(8,128)(2,1)S(1)} %bitcast.55), custom_call_target="tpu_custom_call" | custom-call | tf_op jit(solution)/shard_map/chain_all/pallas_call | solution.py:75
  59.3 4.4 %all-to-all-start.1 = ((bf16[16,32,16,128]{3,2,1,0:T(8,128)(2,1)}), bf16[16,32,16,128]{3,2,1,0:T(8,128)(2,1)}, u32[]{:S(2)}, u32[]{:S(2)}) async-start(bf16[16,32,16,128]{3,2,1,0:T(8,128)(2,1)} %chain_all.1), calls=%async_computation.1 | async-start | bytes 4194304 | tf_op jit(solution)/shard_map/all_to_all | solution.py:133
  63.7 0.0 copy-start.2
  63.7 6.9 %fusion.12 = bf16[128,64]{0,1:T(8,128)(2,1)S(1)} fusion(bf16[1,64,28672]{2,1,0:T(8,128)(2,1)} %param.13, bf16[1,128,28672]{2,1,0:T(8,128)(2,1)} %param.8), kind=kOutput, calls=%fused_computation.19 | convolution fusion | flops 469770240 | bytes 11026432 | tf_op jit(solution)/shard_map/tf,rf->tr/dot_general | solution.py:135
  70.7 0.0 copy-start.3
  70.7 0.1 copy.35
  70.8 0.0 copy-done.2
  70.8 0.5 fusion.4
  71.3 20.1 %all-to-all-done.1 = bf16[16,32,16,128]{3,2,1,0:T(8,128)(2,1)} async-done(((bf16[16,32,16,128]{3,2,1,0:T(8,128)(2,1)}), bf16[16,32,16,128]{3,2,1,0:T(8,128)(2,1)}, u32[]{:S(2)}, u32[]{:S(2)}) %all-to-all-start.1) | async-done | bytes 2097184 | tf_op jit(solution)/shard_map/all_to_all | solution.py:133
  91.4 0.0 copy-done
  91.4 2.4 %convolution_convert_fusion.1 = bf16[128,64]{0,1:T(8,128)(2,1)S(1)} fusion(bf16[128,8192]{1,0:T(8,128)(2,1)} %bitcast.10, bf16[1,64,8192]{2,1,0:T(8,128)(2,1)S(1)} %copy-done), kind=kOutput, calls=%fused_computation.20 | convolution fusion | flops 134225920 | bytes 3162112 | tf_op jit(solution)/shard_map/td,rd->tr/dot_general | solution.py:138
  93.9 0.1 reshape.248
  94.0 0.1 convolution_convert_fusion
  94.1 0.1 convert_element_type.56
  94.2 0.9 broadcast_in_dim.23
  95.1 12.4 %all-to-all-start.2 = ((bf16[16,2,4096]{2,1,0:T(2,128)(2,1)}), bf16[16,2,4096]{2,1,0:T(2,128)(2,1)S(1)}, u32[]{:S(2)}, u32[]{:S(2)}) async-start(bf16[16,2,4096]{2,1,0:T(2,128)(2,1)} %broadcast_in_dim.23), calls=%async_computation.2 | async-start | bytes 524288 | tf_op jit(solution)/shard_map/all_to_all | solution.py:150
  107.5 0.0 copy-done.3
  107.5 2.4 %fusion.10 = f32[16,8]{1,0:T(8,128)S(1)} fusion(bf16[16,8,64,128]{3,1,2,0:T(8,128)(2,1)} %bitcast.9, bf16[1,128,8192]{2,1,0:T(8,128)(2,1)S(1)} %copy-done.2, f32[64,128]{1,0:T(8,128)S(1)} %bitcast.58), kind=kLoop, calls=%fused_computation.15 | loop fusion | flops 5242752 | bytes 4227584 | tf_op jit(solution)/shard_map/reduce_sum | solution.py:103
  109.9 0.1 div.59
  110.0 9.2 %all-to-all-done.2 = bf16[16,2,4096]{2,1,0:T(2,128)(2,1)S(1)} async-done(((bf16[16,2,4096]{2,1,0:T(2,128)(2,1)}), bf16[16,2,4096]{2,1,0:T(2,128)(2,1)S(1)}, u32[]{:S(2)}, u32[]{:S(2)}) %all-to-all-start.2) | async-done | bytes 262176 | tf_op jit(solution)/shard_map/all_to_all | solution.py:150
  119.2 0.4 multiply_reduce_fusion
  119.6 0.1 copy.33
  119.7 0.1 broadcast_in_dim.43
  119.7 0.8 reshape.250
  120.5 1.2 fusion.18
  121.8 0.1 pad_maximum_fusion.2
  121.9 0.9 reshape.261
  122.8 3.5 %all-to-all-start.3 = ((f32[16,1,1056]{2,1,0:T(1,128)}), f32[16,1,1056]{2,1,0:T(1,128)S(1)}, u32[]{:S(2)}, u32[]{:S(2)}) async-start(f32[16,1,1056]{2,1,0:T(1,128)} %reshape.261), calls=%async_computation.3 | async-start | bytes 147456 | tf_op jit(solution)/shard_map/all_to_all | solution.py:157
  126.3 4.5 %fusion.7 = bf16[1,128,8192]{2,1,0:T(8,128)(2,1)} fusion(bf16[1,128,8192]{2,1,0:T(8,128)(2,1)S(1)} %copy-done.2, bf16[16,8,64,128]{3,1,2,0:T(8,128)(2,1)} %bitcast.9, f32[128]{0:T(128)S(1)} %div.59, f32[128]{0:T(128)S(1)} %get-tuple-element.5, f32[8192]{0:T(1024)S(1)} %bitcast.59, f32[128]{0:T(128)S(1)} %get-tuple-element.4), kind=kLoop, calls=%fused_computation.12 | loop fusion | flops 9437184 | bytes 6325760 | tf_op jit(solution)/shard_map/convert_element_type | solution.py:105
  130.8 2.6 %all-to-all-done.3 = f32[16,1,1056]{2,1,0:T(1,128)S(1)} async-done(((f32[16,1,1056]{2,1,0:T(1,128)}), f32[16,1,1056]{2,1,0:T(1,128)S(1)}, u32[]{:S(2)}, u32[]{:S(2)}) %all-to-all-start.3) | async-done | bytes 67616 | tf_op jit(solution)/shard_map/all_to_all | solution.py:157
  133.4 0.5 broadcast.264
  134.0 0.8 reduce.5
  134.8 0.3 reshape.262
  135.1 0.2 fusion.24
  135.3 0.7 slice_divide_fusion
  (8 shorter events, 0.1 us)
Async XLA Ops:
  0.6 90.8 %copy-start = (bf16[1,64,8192]{2,1,0:T(8,128)(2,1)S(1)}, bf16[1,64,8192]{2,1,0:T(8,128)(2,1)}, u32[]{:S(2)}) copy-start(bf16[1,64,8192]{2,1,0:T(8,128)(2,1)} %param.14) | copy-start | bytes 3145732
  5.0 7.8 %copy-start.1 = (s32[2]{0:T(128)S(1)}, s32[2]{0:T(128)}, u32[]{:S(2)}) copy-start(s32[2]{0:T(128)} %param.12) | copy-start | bytes 28
  5.0 46.7 %all-to-all-start = ((bf16[16,40,16,128]{3,2,1,0:T(8,128)(2,1)}), bf16[16,40,16,128]{3,2,1,0:T(8,128)(2,1)}, u32[]{:S(2)}, u32[]{:S(2)}) async-start(bf16[16,40,16,128]{3,2,1,0:T(8,128)(2,1)} %pad_maximum_fusion), calls=%async_computation | async-start | bytes 5242880 | tf_op jit(solution)/shard_map/all_to_all | solution.py:126
  59.3 32.2 %all-to-all-start.1 = ((bf16[16,32,16,128]{3,2,1,0:T(8,128)(2,1)}), bf16[16,32,16,128]{3,2,1,0:T(8,128)(2,1)}, u32[]{:S(2)}, u32[]{:S(2)}) async-start(bf16[16,32,16,128]{3,2,1,0:T(8,128)(2,1)} %chain_all.1), calls=%async_computation.1 | async-start | bytes 4194304 | tf_op jit(solution)/shard_map/all_to_all | solution.py:133
  63.7 7.1 %copy-start.2 = (bf16[1,128,8192]{2,1,0:T(8,128)(2,1)S(1)}, bf16[1,128,8192]{2,1,0:T(8,128)(2,1)}, u32[]{:S(2)}) copy-start(bf16[1,128,8192]{2,1,0:T(8,128)(2,1)} %param.9) | copy-start | bytes 6291460
  70.7 36.9 %copy-start.3 = (f32[1,8192]{1,0:T(1,128)S(1)}, f32[1,8192]{1,0:T(1,128)}, u32[]{:S(2)}) copy-start(f32[1,8192]{1,0:T(1,128)} %param.10) | copy-start | bytes 98308
  95.1 24.1 %all-to-all-start.2 = ((bf16[16,2,4096]{2,1,0:T(2,128)(2,1)}), bf16[16,2,4096]{2,1,0:T(2,128)(2,1)S(1)}, u32[]{:S(2)}, u32[]{:S(2)}) async-start(bf16[16,2,4096]{2,1,0:T(2,128)(2,1)} %broadcast_in_dim.23), calls=%async_computation.2 | async-start | bytes 524288 | tf_op jit(solution)/shard_map/all_to_all | solution.py:150
  122.8 10.7 %all-to-all-start.3 = ((f32[16,1,1056]{2,1,0:T(1,128)}), f32[16,1,1056]{2,1,0:T(1,128)S(1)}, u32[]{:S(2)}, u32[]{:S(2)}) async-start(f32[16,1,1056]{2,1,0:T(1,128)} %reshape.261), calls=%async_computation.3 | async-start | bytes 147456 | tf_op jit(solution)/shard_map/all_to_all | solution.py:157

commit v2 on v0

v2 whole, which is shorter than its diff:
```python
import functools
import math

import jax
import jax.numpy as jnp
from jax import lax
from jax.experimental import pallas as pl
from jax.experimental.pallas import tpu as pltpu
from jax.sharding import PartitionSpec as P

EPS = 1e-05
LANES = 128
SUBLANES = 16


def chain_kernel(place_ref, recv_ref, top_ref, *refs):
    *near_refs, out_ref, gain_ref, grad_ref, kept_ref, inv_ref, out_sem = refs
    sections, blocks = recv_ref.shape[:2]
    side = len(near_refs)
    width = blocks * 2 * LANES
    step = 4
    chunks = blocks // step
    row, column = place_ref[0] // side, place_ref[0] % side

    def leaving(group):
        span = pl.ds(group * side, side)
        return pltpu.make_async_copy(grad_ref.at[span], out_ref.at[span], out_sem.at[group])

    for down in range(side):
        for across in range(side):
            s = (row + side - down) % side * side + (column + side - across) % side
            gain_ref[s] = near_refs[down][across]
    grad_ref[sections - 1] = top_ref[...]

    def gain_of(s, k):
        return jnp.stack(
            [
                jnp.concatenate(
                    [
                        jnp.broadcast_to(gain_ref[s, pl.ds(2 * i, 1), :], (8, LANES)),
                        jnp.broadcast_to(gain_ref[s, pl.ds(2 * i + 1, 1), :], (8, LANES)),
                    ],
                    axis=0,
                )
                for i in range(k * step, (k + 1) * step)
            ]
        )

    def span(k):
        return pl.ds(k * step, step)

    def mean(v):
        v = jnp.sum(v, axis=0)
        v = v[:8] + v[8:]
        v = jnp.sum(v, axis=-1, keepdims=True) / width
        return jnp.broadcast_to(jnp.concatenate([v, v], axis=0), (SUBLANES, LANES))

    zero = jnp.zeros((step, SUBLANES, LANES), jnp.float32)
    for s in range(sections - 1, 0, -1):
        square = zero
        for k in range(chunks):
            x = recv_ref[s, span(k)].astype(jnp.float32)
            square = square + x * x
        inv_ref[s] = lax.rsqrt(mean(square) + EPS)

    def enter(s, k, g, inner):
        weighted = g * gain_of(s, k)
        kept_ref[span(k)] = g + inv_ref[s][None] * weighted
        return inner + weighted * recv_ref[s, span(k)].astype(jnp.float32)

    inner = zero
    for k in range(chunks):
        inner = enter(sections - 1, k, grad_ref[sections - 1, span(k)].astype(jnp.float32), inner)
    for s in range(sections - 1, 0, -1):
        inv = inv_ref[s]
        pull = (inv * inv * inv * mean(inner))[None]
        inner = zero
        for k in range(chunks):
            new = kept_ref[span(k)] - recv_ref[s, span(k)].astype(jnp.float32) * pull
            new = new.astype(jnp.bfloat16)
            grad_ref[s - 1, span(k)] = new
            if s > 1:
                inner = enter(s - 1, k, new.astype(jnp.float32), inner)
        if (s - 1) % side == 0:
            leaving((s - 1) // side).start()
    for group in range(side):
        leaving(group).wait()


def in_vmem(body, out_shape, name, scalars=0, scratch=()):
    def call(*args):
        specs = [pl.BlockSpec(memory_space=pltpu.SMEM)] * scalars
        specs += [pl.BlockSpec(memory_space=pltpu.VMEM)] * (len(args) - scalars)
        return pl.pallas_call(
            body,
            out_shape=out_shape,
            in_specs=specs,
            out_specs=pl.BlockSpec(memory_space=pltpu.VMEM),
            scratch_shapes=list(scratch),
            compiler_params=pltpu.CompilerParams(vmem_limit_bytes=24 * 1024 * 1024),
            name=name,
        )(*args)

    return call


def chain_all(place, recv, top, near):
    sections, blocks = recv.shape[:2]
    shape = (sections, blocks, SUBLANES, LANES)
    side = len(near)
    return pl.pallas_call(
        chain_kernel,
        out_shape=pltpu.HBM(shape, jnp.bfloat16),
        in_specs=[pl.BlockSpec(memory_space=pltpu.SMEM)] + [pl.BlockSpec(memory_space=pltpu.VMEM)] * (2 + side),
        out_specs=pl.BlockSpec(memory_space=pltpu.HBM),
        scratch_shapes=[
            pltpu.VMEM((sections, 2 * blocks, LANES), jnp.float32),
            pltpu.VMEM(shape, jnp.bfloat16),
            pltpu.VMEM(shape[1:], jnp.float32),
            pltpu.VMEM((sections, SUBLANES, LANES), jnp.float32),
            pltpu.SemaphoreType.DMA((side,)),
        ],
        compiler_params=pltpu.CompilerParams(vmem_limit_bytes=16 * 1024 * 1024),
        name="chain_all",
    )(place, recv, top, *near)


def front_kernel(held_ref, weight_ref, side_in_ref, out_ref):
    side_out = lax.dot_general(
        held_ref[...], weight_ref[...], (((1,), (1,)), ((), ())), preferred_element_type=jnp.float32
    ).astype(jnp.bfloat16)
    examples = out_ref.shape[0]
    rows = side_out.shape[0] // examples
    for e in range(examples):
        out_ref[e] = lax.dot_general(
            side_out[e * rows : (e + 1) * rows],
            side_in_ref[pl.ds(e * rows, rows), :],
            (((0,), (0,)), ((), ())),
            preferred_element_type=jnp.float32,
        ).astype(jnp.bfloat16)


def raw_kernel(grads_ref, queries_ref, out_ref):
    grads = grads_ref[...]
    share = queries_ref.shape[0]
    raw = lax.dot_general(
        grads, queries_ref[...], (((1,), (1,)), ((), ())), preferred_element_type=jnp.float32
    )
    wide = grads.astype(jnp.float32)
    squares = jnp.broadcast_to(jnp.sum(wide * wide, axis=1, keepdims=True), raw.shape)

    def folded(v):
        return jnp.concatenate([v[8 * j : 8 * j + 8] for j in range(v.shape[0] // 8)], axis=1)

    block = jnp.concatenate([folded(raw), folded(squares)], axis=0)
    for s in range(out_ref.shape[0]):
        out_ref[s] = block


def scores_kernel(parts_ref, out_ref, *, count):
    total = parts_ref[0]
    for s in range(1, parts_ref.shape[0]):
        total = total + parts_ref[s]
    scores = total[:8] / jnp.sqrt(total[8:] / count + 1e-06)
    share = out_ref.shape[1]
    for j in range(out_ref.shape[0] // 8):
        out_ref[pl.ds(8 * j, 8), :] = scores[:, j * share : (j + 1) * share]


def to_tiles(rows):
    count, width = rows.shape
    tiles = rows.reshape(count // 8, 8, width // LANES, LANES).transpose(0, 2, 1, 3)
    return tiles.reshape(count // 8, width // (2 * LANES), SUBLANES, LANES)


def from_tiles(tiles):
    groups, blocks = tiles.shape[:2]
    rows = tiles.reshape(groups, blocks * 2, 8, LANES).transpose(0, 2, 1, 3)
    return rows.reshape(groups * 8, blocks * 2 * LANES)


def chain_back(grad_rows, resid_rows, norm_gain):
    grad_f32 = grad_rows.astype(jnp.float32)
    resid_f32 = resid_rows.astype(jnp.float32)
    inv_rms = lax.rsqrt(jnp.mean(resid_f32 * resid_f32, axis=-1, keepdims=True) + EPS)
    weighted = grad_f32 * norm_gain
    inner_mean = jnp.mean(weighted * resid_f32, axis=-1, keepdims=True)
    result = grad_f32 + inv_rms * weighted - resid_f32 * (inv_rms * inv_rms * inv_rms) * inner_mean
    return result.astype(jnp.bfloat16)


def shards(hidden_acts, resid_stream, norm_scale, out_grad, lengths, proj_in, proj_out, queries):
    tok_rows, features = out_grad.shape
    examples = lengths.shape[0]
    seq_len = tok_rows // examples
    rank_size = proj_in.shape[1]
    sections = lax.axis_size("section")
    ranks = lax.axis_size("dp")
    share = queries.shape[1]
    me = lax.axis_index("section")
    resid_rows = resid_stream[0]
    norm_gain = norm_scale[0]

    side = math.isqrt(sections)
    grid = [(row, column) for row in range(side) for column in range(side)]

    def moved(value, down, across):
        pairs = [
            (row * side + column, (row + down) % side * side + (column + across) % side) for row, column in grid
        ]
        return lax.ppermute(value, "section", pairs)

    gain_tiles = norm_gain.reshape(-1, LANES)
    across = [moved(gain_tiles, 0, k) for k in range(1, side)]
    resid_first, across[0] = lax.optimization_barrier((resid_rows, across[0]))
    near = [jnp.stack([gain_tiles] + across)]
    near += [moved(near[0], k, 0) for k in range(1, side)]

    own = tok_rows // sections
    recv = lax.all_to_all(to_tiles(resid_first), "section", 0, 0)
    own_rows = lax.dynamic_slice_in_dim(out_grad, me * own, own, axis=0)
    own_slots = me * own + jnp.arange(own, dtype=jnp.int32)
    own_live = own_slots % seq_len < jnp.take(lengths, own_slots // seq_len)
    own_top = jnp.where(own_live[:, None], own_rows, jnp.zeros_like(own_rows))
    grads = chain_all(me.astype(jnp.int32).reshape(1), recv, to_tiles(own_top)[0], near)
    held_grad = from_tiles(lax.all_to_all(grads, "section", 0, 0))

    side_in = jnp.einsum(
        "tf,rf->tr", hidden_acts[0], proj_in[0], preferred_element_type=jnp.float32
    ).astype(jnp.bfloat16)
    in_grad = chain_back(held_grad, resid_rows, norm_gain)
    outer = in_vmem(front_kernel, jax.ShapeDtypeStruct((examples, rank_size, rank_size), jnp.bfloat16), "front")(
        held_grad, proj_out[0], side_in
    )
    example_grads = outer.reshape(examples, rank_size * rank_size)
    spread = jnp.broadcast_to(example_grads[None], (ranks,) + example_grads.shape)
    gathered = lax.all_to_all(spread, "dp", 0, 0).reshape(ranks * examples, rank_size * rank_size)
    folded = in_vmem(raw_kernel, jax.ShapeDtypeStruct((sections, 16, LANES), jnp.float32), "raw")(
        gathered, queries[0]
    )
    parts = lax.all_to_all(folded, "section", 0, 0)
    scores = in_vmem(
        functools.partial(scores_kernel, count=sections * rank_size * rank_size),
        jax.ShapeDtypeStruct((ranks * examples, share), jnp.float32),
        "scores",
    )(parts)
    return (scores, in_grad[None])


def solution(mesh):
    in_specs = (
        P("section", "dp", None),
        P("section", "dp", None),
        P("section", None),
        P("dp", None),
        P("dp"),
        P("section", None, None),
        P("section", None, None),
        P("section", "dp", None),
    )
    out_specs = (P(None, "dp"), P("section", "dp", None))
    return jax.shard_map(shards, mesh=mesh, in_specs=in_specs, out_specs=out_specs, check_vma=False)
```

time: 906 us -> 120 us (0.13); the launches traced: 894 us -> 119 us
  waiting for transfers between devices: 594 us -> 54.6 us
  other arithmetic: 145 us -> 10.2 us
  blocking collectives: 97.5 us -> 0 us
  local copies, waits for them, and re-layouts: 28 us -> 1.98 us
  starting transfers between devices: 19.2 us -> 37.8 us
    ppermute x15 -> x6, waiting for transfers between devices: 594 us -> 22.5 us  [moved(): return lax.ppermute(value, 'section', pairs)]
    psum x1 -> x0, blocking collectives: 61.9 us -> none  [shards(): summed, squares = lax.psum((partial_value, squares), 'section')]
    select_n x16 -> x2, other arithmetic: 48.8 us -> 1 us  [the longest x1 0.99 us: shards(): own_top = jnp.where(own_live[:, None], own_rows, jnp.zeros_like(own_rows))]
    reduce_sum x17 -> x2, other arithmetic: 45.2 us -> 4.51 us  [the longest x1 2.43 us: chain_back(): inner_mean = jnp.mean(weighted * resid_f32, axis=-1, keepdims=True)]
    convert_element_type x15 -> x1, other arithmetic: 44.6 us -> 4.63 us  [chain_back(): return result.astype(jnp.bfloat16)]
    all_gather x1 -> x0, blocking collectives: 35.5 us -> none  [shards(): gathered = lax.all_gather(example_grads, 'dp', axis=0, tiled=True)]
    all_to_all x0 -> x4, waiting for transfers between devices: none -> 32.1 us  [the longest x1 19.8 us: shards(): held_grad = from_tiles(lax.all_to_all(grads, 'section', 0, 0))]
    all_to_all x0 -> x4, starting transfers between devices: none -> 27 us  [the longest x1 11.4 us: shards(): lax.all_to_all(spread, 'dp', 0, 0)]
  transfers between devices with their start and end apart: 15 -> 10, of which waited for: 15 -> 6; matrix products, arithmetic and copies ran while one was open for 5% -> 15% of each run, Pallas kernels for 0% -> 0%
where the time goes in v2:
time: 120 us; the launch traced here: 119 us
  waiting for transfers between devices  54.6 us (46%)
  starting transfers between devices  37.8 us (31%)
  other arithmetic  10.2 us (8%)
  Pallas kernels  7.04 us (6%)
  matrix products  6.87 us (6%)
  local copies, waits for them, and re-layouts  1.98 us (2%)
    ppermute x6, waiting for transfers between devices, moved(): return lax.ppermute(value, 'section', pairs)  22.5 us
    all_to_all x1, waiting for transfers between devices, shards(): held_grad = from_tiles(lax.all_to_all(grads, 'section', 0, 0))  19.8 us
    all_to_all x1, starting transfers between devices, shards(): lax.all_to_all(spread, 'dp', 0, 0)  11.4 us
    ppermute x6, starting transfers between devices, moved(): return lax.ppermute(value, 'section', pairs)  10.7 us
    all_to_all x1, waiting for transfers between devices, shards(): lax.all_to_all(spread, 'dp', 0, 0)  9.19 us
    all_to_all x1, starting transfers between devices, shards(): held_grad = from_tiles(lax.all_to_all(grads, 'section', 0, 0))  7.79 us
    dot_general x1, matrix products, shards(): jnp.einsum('tf,rf->tr', hidden_acts[0], proj_in[0], preferred_element_typ...  6.87 us
    convert_element_type x1, other arithmetic, chain_back(): return result.astype(jnp.bfloat16)  4.63 us
  transfers between devices with their start and end apart: 10, of which 6 were waited for; matrix products, arithmetic and copies ran while one was open for 15% of the time, Pallas kernels for 0%

profile of v2, /device:TPU:1, one launch (start us, length us, event | category | flops | bytes accessed | tf_op | source)
XLA Modules:
  0.0 119.2 jit_solution(7772910047271358316)
XLA Ops:
  0.6 0.0 copy-start
  0.6 0.0 copy-start.3
  0.7 2.1 %collective-permute-start = (f32[64,128]{1,0:T(8,128)}, f32[64,128]{1,0:T(8,128)S(1)}, u32[]{:S(2)}, u32[]{:S(2)}) collective-permute-start(f32[64,128]{1,0:T(8,128)} %bitcast.63), channel_id=1, source_target_pairs={{0,16},{16,32},{32,48},{48,0},{64,80},{80,96},{96,112},{112,64},{1... | collective-permute-start | bytes 98312 | tf_op jit(solution)/shard_map/ppermute | solution.py:211
  2.8 2.5 %collective-permute-start.1 = (f32[64,128]{1,0:T(8,128)}, f32[64,128]{1,0:T(8,128)S(1)}, u32[]{:S(2)}, u32[]{:S(2)}) collective-permute-start(f32[64,128]{1,0:T(8,128)} %bitcast.64), channel_id=1, source_target_pairs={{0,32},{16,48},{32,0},{48,16},{64,96},{80,112},{96,64},{112,80},{1... | collective-permute-start | bytes 98312 | tf_op jit(solution)/shard_map/ppermute | solution.py:211
  5.2 1.2 collective-permute-start.2
  6.4 0.0 copy-done
  6.4 0.6 gather_fusion
  7.1 0.0 collective-permute-done
  7.1 4.3 %all-to-all-start = ((bf16[16,32,16,128]{3,2,1,0:T(8,128)(2,1)}), bf16[16,32,16,128]{3,2,1,0:T(8,128)(2,1)S(1)}, u32[]{:S(2)}, u32[]{:S(2)}) async-start(bf16[16,32,16,128]{3,2,1,0:T(8,128)(2,1)} %bitcast.62), calls=%async_computation | async-start | bytes 4194304 | tf_op jit(solution)/shard_map/all_to_all | solution.py:220
  11.4 0.0 collective-permute-done.1
  11.4 0.0 collective-permute-done.2
  11.4 0.0 copy-done.3
  11.5 1.4 %collective-permute-start.3 = (f32[4,64,128]{2,1,0:T(8,128)S(1)}, f32[4,64,128]{2,1,0:T(8,128)S(1)}, u32[]{:S(2)}, u32[]{:S(2)}) collective-permute-start(f32[4,64,128]{2,1,0:T(8,128)S(1)} %pad_maximum_fusion.refs_0_), channel_id=1, source_target_pairs={{0,64},{16,80},{32,96},{48,112},{64,128},{80,144},{96,160},{112,17... | collective-permute-start | bytes 393224 | tf_op jit(solution)/shard_map/ppermute | solution.py:211
  12.9 2.4 %collective-permute-start.4 = (f32[4,64,128]{2,1,0:T(8,128)S(1)}, f32[4,64,128]{2,1,0:T(8,128)S(1)}, u32[]{:S(2)}, u32[]{:S(2)}) collective-permute-start(f32[4,64,128]{2,1,0:T(8,128)S(1)} %pad_maximum_fusion.refs_0_), channel_id=1, source_target_pairs={{0,128},{16,144},{32,160},{48,176},{64,192},{80,208},{96,224},{112... | collective-permute-start | bytes 393224 | tf_op jit(solution)/shard_map/ppermute | solution.py:211
  15.3 1.2 collective-permute-start.5
  16.5 1.0 dynamic-slice_select_fusion
  17.5 17.1 %collective-permute-done.3.refs_1_ = f32[4,64,128]{2,1,0:T(8,128)S(1)} collective-permute-done((f32[4,64,128]{2,1,0:T(8,128)S(1)}, f32[4,64,128]{2,1,0:T(8,128)S(1)}, u32[]{:S(2)}, u32[]{:S(2)}) %collective-permute-start.3) | collective-permute-done | bytes 131104 | tf_op jit(solution)/shard_map/ppermute | solution.py:211
  34.6 5.2 %collective-permute-done.4.refs_2_ = f32[4,64,128]{2,1,0:T(8,128)S(1)} collective-permute-done((f32[4,64,128]{2,1,0:T(8,128)S(1)}, f32[4,64,128]{2,1,0:T(8,128)S(1)}, u32[]{:S(2)}, u32[]{:S(2)}) %collective-permute-start.4) | collective-permute-done | bytes 131104 | tf_op jit(solution)/shard_map/ppermute | solution.py:211
  39.9 0.1 collective-permute-done.5.refs_3_
  40.0 0.0 all-to-all-done.recv_ref
  40.0 4.5 %chain_all.1 = bf16[16,32,16,128]{3,2,1,0:T(8,128)(2,1)} custom-call(s32[1]{0:T(128)} %bitcast.place_ref, bf16[16,32,16,128]{3,2,1,0:T(8,128)(2,1)S(1)} %all-to-all-done.recv_ref, bf16[32,16,128]{2,1,0:T(8,128)(2,1)S(1)} %bitcast.60, f32[4,64,128]{2,1,0:T(8,128)S(1)} %pad_maximum_fusion.refs_0_, f32[4,64,128]{2,1,0:T(8,128)S(1)} %collective-permute-done.3.refs_1_, ...), custom_call_target="tpu_custom_call" | custom-call | tf_op jit(solution)/shard_map/chain_all/pallas_call | solution.py:111
  44.5 7.8 %all-to-all-start.1 = ((bf16[16,32,16,128]{3,2,1,0:T(8,128)(2,1)}), bf16[16,32,16,128]{3,2,1,0:T(8,128)(2,1)S(1)}, u32[]{:S(2)}, u32[]{:S(2)}) async-start(bf16[16,32,16,128]{3,2,1,0:T(8,128)(2,1)} %chain_all.1), calls=%async_computation.1 | async-start | bytes 4194304 | tf_op jit(solution)/shard_map/all_to_all | solution.py:226
  52.3 0.0 copy-start.1
  52.3 6.9 %fusion.11 = bf16[128,64]{0,1:T(8,128)(2,1)S(1)} fusion(bf16[1,64,28672]{2,1,0:T(8,128)(2,1)} %param.13, bf16[1,128,28672]{2,1,0:T(8,128)(2,1)} %param.8), kind=kOutput, calls=%fused_computation.17 | convolution fusion | flops 469770240 | bytes 11026432 | tf_op jit(solution)/shard_map/tf,rf->tr/dot_general | solution.py:228
  59.1 0.1 copy.12.side_in_ref
  59.3 2.1 %multiply_reduce_fusion = f32[128]{0:T(128)S(1)} fusion(bf16[1,128,8192]{2,1,0:T(8,128)(2,1)} %param.9), kind=kLoop, calls=%fused_computation.15 | loop fusion | flops 3145600 | bytes 2097664 | tf_op jit(solution)/shard_map/reduce_sum | solution.py:185
  61.4 19.8 %all-to-all-done.1 = bf16[16,32,16,128]{3,2,1,0:T(8,128)(2,1)S(1)} async-done(((bf16[16,32,16,128]{3,2,1,0:T(8,128)(2,1)}), bf16[16,32,16,128]{3,2,1,0:T(8,128)(2,1)S(1)}, u32[]{:S(2)}, u32[]{:S(2)}) %all-to-all-start.1) | async-done | bytes 2097184 | tf_op jit(solution)/shard_map/all_to_all | solution.py:226
  81.2 0.0 copy-done.1
  81.2 0.0 copy-start.2
  81.2 0.9 front.1
  82.1 0.1 broadcast_in_dim.26
  82.2 0.9 broadcast_in_dim.27
  83.1 11.4 %all-to-all-start.2 = ((bf16[16,2,4096]{2,1,0:T(2,128)(2,1)}), bf16[16,2,4096]{2,1,0:T(2,128)(2,1)S(1)}, u32[]{:S(2)}, u32[]{:S(2)}) async-start(bf16[16,2,4096]{2,1,0:T(2,128)(2,1)} %broadcast_in_dim.27), calls=%async_computation.2 | async-start | bytes 524288 | tf_op jit(solution)/shard_map/all_to_all | solution.py:237
  94.5 2.4 %fusion.8 = f32[16,8]{1,0:T(8,128)S(1)} fusion(bf16[1,128,8192]{2,1,0:T(8,128)(2,1)} %param.9, bf16[16,8,64,128]{3,1,2,0:T(8,128)(2,1)S(1)} %bitcast.57, f32[64,128]{1,0:T(8,128)S(1)} %bitcast.67), kind=kLoop, calls=%fused_computation.13 | loop fusion | flops 5242752 | bytes 4227584 | tf_op jit(solution)/shard_map/reduce_sum | solution.py:187
  96.9 0.1 div.38
  97.0 9.2 %all-to-all-done.2 = bf16[16,2,4096]{2,1,0:T(2,128)(2,1)S(1)} async-done(((bf16[16,2,4096]{2,1,0:T(2,128)(2,1)}), bf16[16,2,4096]{2,1,0:T(2,128)(2,1)S(1)}, u32[]{:S(2)}, u32[]{:S(2)}) %all-to-all-start.2) | async-done | bytes 262176 | tf_op jit(solution)/shard_map/all_to_all | solution.py:237
  106.2 0.1 reshape.228.grads_ref
  106.3 0.0 copy-done.2
  106.3 0.9 raw.1
  107.2 3.5 %all-to-all-start.3 = ((f32[16,16,128]{2,1,0:T(8,128)}), f32[16,16,128]{2,1,0:T(8,128)S(1)}, u32[]{:S(2)}, u32[]{:S(2)}) async-start(f32[16,16,128]{2,1,0:T(8,128)} %raw.1), calls=%async_computation.3 | async-start | bytes 262144 | tf_op jit(solution)/shard_map/all_to_all | solution.py:241
  110.7 4.6 %fusion.6 = bf16[1,128,8192]{2,1,0:T(8,128)(2,1)} fusion(bf16[1,128,8192]{2,1,0:T(8,128)(2,1)} %param.9, bf16[16,8,64,128]{3,1,2,0:T(8,128)(2,1)S(1)} %bitcast.58, f32[128]{0:T(128)S(1)} %div.38, f32[128]{0:T(128)S(1)} %get-tuple-element.7, f32[8192]{0:T(1024)S(1)} %bitcast.68, f32[128]{0:T(128)S(1)} %get-tuple-element.6), kind=kLoop, calls=%fused_computation.11 | loop fusion | flops 9437184 | bytes 6325760 | tf_op jit(solution)/shard_map/convert_element_type | solution.py:189
  115.4 3.1 %all-to-all-done.3.parts_ref = f32[16,16,128]{2,1,0:T(8,128)S(1)} async-done(((f32[16,16,128]{2,1,0:T(8,128)}), f32[16,16,128]{2,1,0:T(8,128)S(1)}, u32[]{:S(2)}, u32[]{:S(2)}) %all-to-all-start.3) | async-done | bytes 131104 | tf_op jit(solution)/shard_map/all_to_all | solution.py:241
  118.5 0.7 scores.1
  (6 shorter events, 0.1 us)
Async XLA Ops:
  0.6 5.8 %copy-start = (s32[2]{0:T(128)S(1)}, s32[2]{0:T(128)}, u32[]{:S(2)}) copy-start(s32[2]{0:T(128)} %param.12) | copy-start | bytes 28
  0.6 10.8 %copy-start.3 = (f32[1,8192]{1,0:T(1,128)S(1)}, f32[1,8192]{1,0:T(1,128)}, u32[]{:S(2)}) copy-start(f32[1,8192]{1,0:T(1,128)} %param.10) | copy-start | bytes 98308
  0.7 6.4 %collective-permute-start = (f32[64,128]{1,0:T(8,128)}, f32[64,128]{1,0:T(8,128)S(1)}, u32[]{:S(2)}, u32[]{:S(2)}) collective-permute-start(f32[64,128]{1,0:T(8,128)} %bitcast.63), channel_id=1, source_target_pairs={{0,16},{16,32},{32,48},{48,0},{64,80},{80,96},{96,112},{112,64},{1... | collective-permute-start | bytes 98312 | tf_op jit(solution)/shard_map/ppermute | solution.py:211
  2.8 8.7 %collective-permute-start.1 = (f32[64,128]{1,0:T(8,128)}, f32[64,128]{1,0:T(8,128)S(1)}, u32[]{:S(2)}, u32[]{:S(2)}) collective-permute-start(f32[64,128]{1,0:T(8,128)} %bitcast.64), channel_id=1, source_target_pairs={{0,32},{16,48},{32,0},{48,16},{64,96},{80,112},{96,64},{112,80},{1... | collective-permute-start | bytes 98312 | tf_op jit(solution)/shard_map/ppermute | solution.py:211
  5.2 6.2 %collective-permute-start.2 = (f32[64,128]{1,0:T(8,128)}, f32[64,128]{1,0:T(8,128)S(1)}, u32[]{:S(2)}, u32[]{:S(2)}) collective-permute-start(f32[64,128]{1,0:T(8,128)} %bitcast.65), channel_id=1, source_target_pairs={{0,48},{16,0},{32,16},{48,32},{64,112},{80,64},{96,80},{112,96},{1... | collective-permute-start | bytes 98312 | tf_op jit(solution)/shard_map/ppermute | solution.py:211
  7.1 32.9 %all-to-all-start = ((bf16[16,32,16,128]{3,2,1,0:T(8,128)(2,1)}), bf16[16,32,16,128]{3,2,1,0:T(8,128)(2,1)S(1)}, u32[]{:S(2)}, u32[]{:S(2)}) async-start(bf16[16,32,16,128]{3,2,1,0:T(8,128)(2,1)} %bitcast.62), calls=%async_computation | async-start | bytes 4194304 | tf_op jit(solution)/shard_map/all_to_all | solution.py:220
  11.5 23.2 %collective-permute-start.3 = (f32[4,64,128]{2,1,0:T(8,128)S(1)}, f32[4,64,128]{2,1,0:T(8,128)S(1)}, u32[]{:S(2)}, u32[]{:S(2)}) collective-permute-start(f32[4,64,128]{2,1,0:T(8,128)S(1)} %pad_maximum_fusion.refs_0_), channel_id=1, source_target_pairs={{0,64},{16,80},{32,96},{48,112},{64,128},{80,144},{96,160},{112,17... | collective-permute-start | bytes 393224 | tf_op jit(solution)/shard_map/ppermute | solution.py:211
  12.9 27.0 %collective-permute-start.4 = (f32[4,64,128]{2,1,0:T(8,128)S(1)}, f32[4,64,128]{2,1,0:T(8,128)S(1)}, u32[]{:S(2)}, u32[]{:S(2)}) collective-permute-start(f32[4,64,128]{2,1,0:T(8,128)S(1)} %pad_maximum_fusion.refs_0_), channel_id=1, source_target_pairs={{0,128},{16,144},{32,160},{48,176},{64,192},{80,208},{96,224},{112... | collective-permute-start | bytes 393224 | tf_op jit(solution)/shard_map/ppermute | solution.py:211
  15.3 24.6 %collective-permute-start.5 = (f32[4,64,128]{2,1,0:T(8,128)S(1)}, f32[4,64,128]{2,1,0:T(8,128)S(1)}, u32[]{:S(2)}, u32[]{:S(2)}) collective-permute-start(f32[4,64,128]{2,1,0:T(8,128)S(1)} %pad_maximum_fusion.refs_0_), channel_id=1, source_target_pairs={{0,192},{16,208},{32,224},{48,240},{64,0},{80,16},{96,32},{112,48}... | collective-permute-start | bytes 393224 | tf_op jit(solution)/shard_map/ppermute | solution.py:211
  44.5 36.7 %all-to-all-start.1 = ((bf16[16,32,16,128]{3,2,1,0:T(8,128)(2,1)}), bf16[16,32,16,128]{3,2,1,0:T(8,128)(2,1)S(1)}, u32[]{:S(2)}, u32[]{:S(2)}) async-start(bf16[16,32,16,128]{3,2,1,0:T(8,128)(2,1)} %chain_all.1), calls=%async_computation.1 | async-start | bytes 4194304 | tf_op jit(solution)/shard_map/all_to_all | solution.py:226
  52.3 28.9 %copy-start.1 = (bf16[1,64,8192]{2,1,0:T(8,128)(2,1)S(1)}, bf16[1,64,8192]{2,1,0:T(8,128)(2,1)}, u32[]{:S(2)}) copy-start(bf16[1,64,8192]{2,1,0:T(8,128)(2,1)} %param.14) | copy-start | bytes 3145732
  81.2 25.1 %copy-start.2 = (bf16[1,32,4096]{2,1,0:T(8,128)(2,1)S(1)}, bf16[1,32,4096]{2,1,0:T(8,128)(2,1)}, u32[]{:S(2)}) copy-start(bf16[1,32,4096]{2,1,0:T(8,128)(2,1)} %param.15) | copy-start | bytes 786436
  83.1 23.1 %all-to-all-start.2 = ((bf16[16,2,4096]{2,1,0:T(2,128)(2,1)}), bf16[16,2,4096]{2,1,0:T(2,128)(2,1)S(1)}, u32[]{:S(2)}, u32[]{:S(2)}) async-start(bf16[16,2,4096]{2,1,0:T(2,128)(2,1)} %broadcast_in_dim.27), calls=%async_computation.2 | async-start | bytes 524288 | tf_op jit(solution)/shard_map/all_to_all | solution.py:237
  107.2 11.3 %all-to-all-start.3 = ((f32[16,16,128]{2,1,0:T(8,128)}), f32[16,16,128]{2,1,0:T(8,128)S(1)}, u32[]{:S(2)}, u32[]{:S(2)}) async-start(f32[16,16,128]{2,1,0:T(8,128)} %raw.1), calls=%async_computation.3 | async-start | bytes 262144 | tf_op jit(solution)/shard_map/all_to_all | solution.py:241

commit v3 on v2

--- a/solution.py
+++ b/solution.py
@@ -97,7 +97,7 @@
             in_specs=specs,
             out_specs=pl.BlockSpec(memory_space=pltpu.VMEM),
             scratch_shapes=list(scratch),
-            compiler_params=pltpu.CompilerParams(vmem_limit_bytes=24 * 1024 * 1024),
+            compiler_params=pltpu.CompilerParams(vmem_limit_bytes=8 * 1024 * 1024),
             name=name,
         )(*args)
 
@@ -140,19 +140,48 @@
         ).astype(jnp.bfloat16)
 
 
-def raw_kernel(grads_ref, queries_ref, out_ref):
+def stage_kernel(queries_ref, out_ref, sem):
+    copy = pltpu.make_async_copy(queries_ref, out_ref, sem)
+    copy.start()
+    copy.wait()
+
+
+def staged(queries):
+    return pl.pallas_call(
+        stage_kernel,
+        out_shape=pltpu.VMEM(queries.shape, queries.dtype),
+        in_specs=[pl.BlockSpec(memory_space=pl.ANY)],
+        out_specs=pl.BlockSpec(memory_space=pltpu.VMEM),
+        scratch_shapes=[pltpu.SemaphoreType.DMA],
+        compiler_params=pltpu.CompilerParams(vmem_limit_bytes=8 * 1024 * 1024),
+        name="stage",
+    )(queries)
+
+
+def raw_kernel(place_ref, grads_ref, queries_ref, out_ref):
+    chips, _, lanes = out_ref.shape
+    share = queries_ref.shape[0] // chips
     grads = grads_ref[...]
-    share = queries_ref.shape[0]
     raw = lax.dot_general(
         grads, queries_ref[...], (((1,), (1,)), ((), ())), preferred_element_type=jnp.float32
     )
     wide = grads.astype(jnp.float32)
-    squares = jnp.broadcast_to(jnp.sum(wide * wide, axis=1, keepdims=True), raw.shape)
-
-    def folded(v):
-        return jnp.concatenate([v[8 * j : 8 * j + 8] for j in range(v.shape[0] // 8)], axis=1)
-
-    block = jnp.concatenate([folded(raw), folded(squares)], axis=0)
+    squares = jnp.sum(wide * wide, axis=1, keepdims=True)
+    fill = jnp.broadcast_to(squares, (grads.shape[0], lanes - share))
+    for slot in range(chips):
+        origin = (place_ref[0] + chips - slot) % chips
+        out_ref[origin] = jnp.concatenate([raw[:, slot * share : (slot + 1) * share], fill], axis=1)
+
+
+def fold_kernel(parts_ref, out_ref, *, share):
+    chips, per = parts_ref.shape[:2]
+    each = 8 // per
+    raws, squares = [], []
+    for j in range(chips // each):
+        rows = jnp.concatenate([parts_ref[j * each + k] for k in range(each)], axis=0)
+        raws.append(rows[:, :share])
+        squares.append(rows[:, share : 2 * share])
+    block = jnp.concatenate([jnp.concatenate(raws, axis=1), jnp.concatenate(squares, axis=1)], axis=0)
     for s in range(out_ref.shape[0]):
         out_ref[s] = block
 
@@ -214,30 +243,64 @@
     across = [moved(gain_tiles, 0, k) for k in range(1, side)]
     resid_first, across[0] = lax.optimization_barrier((resid_rows, across[0]))
     near = [jnp.stack([gain_tiles] + across)]
+    near[0], own_queries = lax.optimization_barrier((near[0], queries[0]))
     near += [moved(near[0], k, 0) for k in range(1, side)]
+
+    side_in = jnp.einsum(
+        "tf,rf->tr", hidden_acts[0], proj_in[0], preferred_element_type=jnp.float32
+    ).astype(jnp.bfloat16)
+
+    chips = ranks // 2
+
+    def around(value, steps):
+        return lax.ppermute(value, "dp", [(i, (i + 2 * steps) % ranks) for i in range(ranks)])
+
+    def longer(ring, steps, count):
+        for _ in range(count):
+            ring.append(around(ring[-1], steps))
+
+    up, down = [own_queries], [own_queries]
+    longer(up, 1, 1)
+    longer(down, -1, 1)
 
     own = tok_rows // sections
     recv = lax.all_to_all(to_tiles(resid_first), "section", 0, 0)
+    recv, side_in, up, down = lax.optimization_barrier((recv, side_in, up, down))
+    longer(up, 1, chips // 2 - 1)
+    longer(down, -1, chips - 2 - chips // 2)
+    all_queries = jnp.concatenate(up + down[:0:-1])
     own_rows = lax.dynamic_slice_in_dim(out_grad, me * own, own, axis=0)
     own_slots = me * own + jnp.arange(own, dtype=jnp.int32)
     own_live = own_slots % seq_len < jnp.take(lengths, own_slots // seq_len)
     own_top = jnp.where(own_live[:, None], own_rows, jnp.zeros_like(own_rows))
     grads = chain_all(me.astype(jnp.int32).reshape(1), recv, to_tiles(own_top)[0], near)
-    held_grad = from_tiles(lax.all_to_all(grads, "section", 0, 0))
-
-    side_in = jnp.einsum(
-        "tf,rf->tr", hidden_acts[0], proj_in[0], preferred_element_type=jnp.float32
-    ).astype(jnp.bfloat16)
-    in_grad = chain_back(held_grad, resid_rows, norm_gain)
+    held, all_queries = lax.optimization_barrier((lax.all_to_all(grads, "section", 0, 0), all_queries))
+    held_grad = from_tiles(held)
+
     outer = in_vmem(front_kernel, jax.ShapeDtypeStruct((examples, rank_size, rank_size), jnp.bfloat16), "front")(
         held_grad, proj_out[0], side_in
     )
     example_grads = outer.reshape(examples, rank_size * rank_size)
-    spread = jnp.broadcast_to(example_grads[None], (ranks,) + example_grads.shape)
-    gathered = lax.all_to_all(spread, "dp", 0, 0).reshape(ranks * examples, rank_size * rank_size)
-    folded = in_vmem(raw_kernel, jax.ShapeDtypeStruct((sections, 16, LANES), jnp.float32), "raw")(
-        gathered, queries[0]
-    )
+    example_grads, all_queries = lax.optimization_barrier((example_grads, all_queries))
+    all_queries = staged(all_queries)
+    rank = lax.axis_index("dp")
+    other_grads = lax.ppermute(example_grads, "dp", [(i, i ^ 1) for i in range(ranks)])
+    first, second = (jnp.where(rank % 2 == k, example_grads, other_grads) for k in range(2))
+    raw = in_vmem(
+        raw_kernel,
+        jax.ShapeDtypeStruct((chips, 2 * examples, LANES), jnp.float32),
+        "raw",
+        scalars=1,
+    )((rank // 2).astype(jnp.int32).reshape(1), jnp.concatenate([first, second]), all_queries)
+    held_grad, raw = lax.optimization_barrier((held_grad, raw))
+    in_grad = chain_back(held_grad, resid_rows, norm_gain)
+    same_core = [list(range(core, ranks, 2)) for core in range(2)]
+    raw = lax.all_to_all(raw, "dp", 0, 0, axis_index_groups=same_core)
+    folded = in_vmem(
+        functools.partial(fold_kernel, share=queries.shape[1]),
+        jax.ShapeDtypeStruct((sections, 16, LANES), jnp.float32),
+        "fold",
+    )(raw)
     parts = lax.all_to_all(folded, "section", 0, 0)
     scores = in_vmem(
         functools.partial(scores_kernel, count=sections * rank_size * rank_size),

time: 120 us -> 116 us (0.967)
  waiting for transfers between devices: 54.6 us -> 35.1 us
  starting transfers between devices: 37.8 us -> 51.2 us
  local copies, waits for them, and re-layouts: 1.98 us -> 5.51 us
  other arithmetic: 10.2 us -> 8.46 us
  Pallas kernels: 7.04 us -> 8.32 us
    all_to_all x2, waiting for transfers between devices: 29 us -> 6.67 us  [the longest x1 3.92 us: shards(): raw = lax.all_to_all(raw, 'dp', 0, 0, axis_index_groups=same_core)]
    ppermute x6, waiting for transfers between devices: 22.5 us -> 1.82 us  [moved(): return lax.ppermute(value, 'section', pairs)]
    ppermute x0 -> x8, starting transfers between devices: none -> 17.2 us  [the longest x7 14.2 us: around(): lax.ppermute(value, 'dp', [(i, (i + 2 * steps) % ranks) for i in range(ra...]
    ppermute x0 -> x8, waiting for transfers between devices: none -> 15.2 us  [the longest x7 15.2 us: around(): lax.ppermute(value, 'dp', [(i, (i + 2 * steps) % ranks) for i in range(ra...]
    all_to_all x1, waiting for transfers between devices: 0.01 us -> 9.24 us  [shards(): recv = lax.all_to_all(to_tiles(resid_first), 'section', 0, 0)]
    unnamed x8 -> x25, local copies, waits for them, and re-layouts: 0.02 us -> 4.75 us
    broadcast_in_dim x0 -> x1, other arithmetic: none -> 4.64 us  [shards(): return (scores, in_grad[None])]
    convert_element_type x1 -> x0, other arithmetic: 4.63 us -> none  [chain_back(): return result.astype(jnp.bfloat16)]
  transfers between devices with their start and end apart: 10 -> 18, of which waited for: 6 -> 9; matrix products, arithmetic and copies ran while one was open for 15% -> 14% of each run, Pallas kernels for 0% -> 0%
where the time goes in v3:
time: 116 us
  starting transfers between devices  51.2 us (44%)
  waiting for transfers between devices  35.1 us (30%)
  other arithmetic  8.46 us (7%)
  Pallas kernels  8.32 us (7%)
  matrix products  6.16 us (5%)
  local copies, waits for them, and re-layouts  5.51 us (5%)
    ppermute x7, waiting for transfers between devices, around(): lax.ppermute(value, 'dp', [(i, (i + 2 * steps) % ranks) for i in range(ra...  15.2 us
    ppermute x7, starting transfers between devices, around(): lax.ppermute(value, 'dp', [(i, (i + 2 * steps) % ranks) for i in range(ra...  14.2 us
    ppermute x6, starting transfers between devices, moved(): return lax.ppermute(value, 'section', pairs)  10.1 us
    all_to_all x1, waiting for transfers between devices, shards(): recv = lax.all_to_all(to_tiles(resid_first), 'section', 0, 0)  9.24 us
    all_to_all x1, starting transfers between devices, shards(): raw = lax.all_to_all(raw, 'dp', 0, 0, axis_index_groups=same_core)  8.19 us
    all_to_all x1, starting transfers between devices, shards(): lax.all_to_all(grads, 'section', 0, 0)  6.64 us
    dot_general x1, matrix products, shards(): jnp.einsum('tf,rf->tr', hidden_acts[0], proj_in[0], preferred_element_typ...  6.16 us
    all_to_all x1, starting transfers between devices, shards(): recv = lax.all_to_all(to_tiles(resid_first), 'section', 0, 0)  5.59 us
  transfers between devices with their start and end apart: 18, of which 9 were waited for; matrix products, arithmetic and copies ran while one was open for 14% of the time, Pallas kernels for 0%

profile of v3, /device:TPU:1, one launch (start us, length us, event | category | flops | bytes accessed | tf_op | source)
XLA Modules:
  0.0 115.7 jit_solution(17698147303962518421)
XLA Ops:
  0.6 0.0 copy-start
  0.6 2.1 %collective-permute-start = (f32[64,128]{1,0:T(8,128)}, f32[64,128]{1,0:T(8,128)S(1)}, u32[]{:S(2)}, u32[]{:S(2)}) collective-permute-start(f32[64,128]{1,0:T(8,128)} %bitcast.49), channel_id=1, source_target_pairs={{0,16},{16,32},{32,48},{48,0},{64,80},{80,96},{96,112},{112,64},{1... | collective-permute-start | bytes 98312 | tf_op jit(solution)/shard_map/ppermute | solution.py:240
  2.8 1.4 %collective-permute-start.2 = (f32[64,128]{1,0:T(8,128)}, f32[64,128]{1,0:T(8,128)S(1)}, u32[]{:S(2)}, u32[]{:S(2)}) collective-permute-start(f32[64,128]{1,0:T(8,128)} %bitcast.50), channel_id=1, source_target_pairs={{0,48},{16,0},{32,16},{48,32},{64,112},{80,64},{96,80},{112,96},{1... | collective-permute-start | bytes 98312 | tf_op jit(solution)/shard_map/ppermute | solution.py:240
  4.1 1.6 %collective-permute-start.1 = (f32[64,128]{1,0:T(8,128)}, f32[64,128]{1,0:T(8,128)S(1)}, u32[]{:S(2)}, u32[]{:S(2)}) collective-permute-start(f32[64,128]{1,0:T(8,128)} %bitcast.51), channel_id=1, source_target_pairs={{0,32},{16,48},{32,0},{48,16},{64,96},{80,112},{96,64},{112,80},{1... | collective-permute-start | bytes 98312 | tf_op jit(solution)/shard_map/ppermute | solution.py:240
  5.8 0.6 gather_fusion
  6.5 0.0 copy-start.4
  6.5 0.0 copy-start.5
  6.5 5.6 %all-to-all-start = ((bf16[16,32,16,128]{3,2,1,0:T(8,128)(2,1)}), bf16[16,32,16,128]{3,2,1,0:T(8,128)(2,1)S(1)}, u32[]{:S(2)}, u32[]{:S(2)}) async-start(bf16[16,32,16,128]{3,2,1,0:T(8,128)(2,1)} %bitcast.48), calls=%async_computation | async-start | bytes 4194304 | tf_op jit(solution)/shard_map/all_to_all | solution.py:267
  12.1 1.0 dynamic-slice_select_fusion
  13.1 0.0 collective-permute-done.1
  13.2 1.7 %collective-permute-start.3 = (bf16[32,4096]{1,0:T(8,128)(2,1)S(1)}, bf16[32,4096]{1,0:T(8,128)(2,1)S(1)}, u32[]{:S(2)}, u32[]{:S(2)}) collective-permute-start(bf16[32,4096]{1,0:T(8,128)(2,1)S(1)} %bitcast.55), channel_id=1, source_target_pairs={{0,2},{1,3},{2,4},{3,5},{4,6},{5,7},{6,8},{7,9},{8,10},{9,11},{10,... | collective-permute-start | bytes 786440 | tf_op jit(solution)/shard_map/ppermute | solution.py:256
  14.9 4.0 %collective-permute-start.4 = (bf16[32,4096]{1,0:T(8,128)(2,1)S(1)}, bf16[32,4096]{1,0:T(8,128)(2,1)S(1)}, u32[]{:S(2)}, u32[]{:S(2)}) collective-permute-start(bf16[32,4096]{1,0:T(8,128)(2,1)S(1)} %bitcast.56), channel_id=1, source_target_pairs={{0,14},{1,15},{2,0},{3,1},{4,2},{5,3},{6,4},{7,5},{8,6},{9,7},{10,... | collective-permute-start | bytes 786440 | tf_op jit(solution)/shard_map/ppermute | solution.py:256
  18.9 1.4 %collective-permute-start.5 = (f32[4,64,128]{2,1,0:T(8,128)S(1)}, f32[4,64,128]{2,1,0:T(8,128)S(1)}, u32[]{:S(2)}, u32[]{:S(2)}) collective-permute-start(f32[4,64,128]{2,1,0:T(8,128)S(1)} %pad_maximum_fusion.refs_0_), channel_id=1, source_target_pairs={{0,64},{16,80},{32,96},{48,112},{64,128},{80,144},{96,160},{112,17... | collective-permute-start | bytes 393224 | tf_op jit(solution)/shard_map/ppermute | solution.py:240
  20.3 2.4 %collective-permute-start.6 = (f32[4,64,128]{2,1,0:T(8,128)S(1)}, f32[4,64,128]{2,1,0:T(8,128)S(1)}, u32[]{:S(2)}, u32[]{:S(2)}) collective-permute-start(f32[4,64,128]{2,1,0:T(8,128)S(1)} %pad_maximum_fusion.refs_0_), channel_id=1, source_target_pairs={{0,128},{16,144},{32,160},{48,176},{64,192},{80,208},{96,224},{112... | collective-permute-start | bytes 393224 | tf_op jit(solution)/shard_map/ppermute | solution.py:240
  22.7 1.2 %collective-permute-start.7 = (f32[4,64,128]{2,1,0:T(8,128)S(1)}, f32[4,64,128]{2,1,0:T(8,128)S(1)}, u32[]{:S(2)}, u32[]{:S(2)}) collective-permute-start(f32[4,64,128]{2,1,0:T(8,128)S(1)} %pad_maximum_fusion.refs_0_), channel_id=1, source_target_pairs={{0,192},{16,208},{32,224},{48,240},{64,0},{80,16},{96,32},{112,48}... | collective-permute-start | bytes 393224 | tf_op jit(solution)/shard_map/ppermute | solution.py:240
  23.8 6.2 %fusion.10.side_in_ref = bf16[128,64]{1,0:T(8,128)(2,1)S(1)} fusion(bf16[1,64,28672]{2,1,0:T(8,128)(2,1)} %param.13, bf16[1,128,28672]{2,1,0:T(8,128)(2,1)} %param.8), kind=kOutput, calls=%fused_computation.16 | convolution fusion | flops 469770240 | bytes 11026432 | tf_op jit(solution)/shard_map/tf,rf->tr/dot_general | solution.py:249
  30.0 0.7 copy-done.8
  30.7 0.0 collective-permute-done.4
  30.7 9.2 %all-to-all-done.recv_ref = bf16[16,32,16,128]{3,2,1,0:T(8,128)(2,1)S(1)} async-done(((bf16[16,32,16,128]{3,2,1,0:T(8,128)(2,1)}), bf16[16,32,16,128]{3,2,1,0:T(8,128)(2,1)S(1)}, u32[]{:S(2)}, u32[]{:S(2)}) %all-to-all-start) | async-done | bytes 2097184 | tf_op jit(solution)/shard_map/all_to_all | solution.py:267
  40.0 0.9 collective-permute-done.5.refs_1_
  40.9 0.9 collective-permute-done.6.refs_2_
  41.8 4.5 %chain_all.1 = bf16[16,32,16,128]{3,2,1,0:T(8,128)(2,1)} custom-call(s32[1]{0:T(128)} %bitcast.place_ref, bf16[16,32,16,128]{3,2,1,0:T(8,128)(2,1)S(1)} %all-to-all-done.recv_ref, bf16[32,16,128]{2,1,0:T(8,128)(2,1)S(1)} %bitcast.47, f32[4,64,128]{2,1,0:T(8,128)S(1)} %pad_maximum_fusion.refs_0_, f32[4,64,128]{2,1,0:T(8,128)S(1)} %collective-permute-done.5.refs_1_, ...), custom_call_target="tpu_custom_call" | custom-call | tf_op jit(solution)/shard_map/chain_all/pallas_call | solution.py:111
  46.3 6.6 %all-to-all-start.1 = ((bf16[16,32,16,128]{3,2,1,0:T(8,128)(2,1)}), bf16[16,32,16,128]{3,2,1,0:T(8,128)(2,1)S(1)}, u32[]{:S(2)}, u32[]{:S(2)}) async-start(bf16[16,32,16,128]{3,2,1,0:T(8,128)(2,1)} %chain_all.1), calls=%async_computation.1 | async-start | bytes 4194304 | tf_op jit(solution)/shard_map/all_to_all | solution.py:277
  53.0 0.0 copy-start.3
  53.0 1.7 %collective-permute-start.8 = (bf16[32,4096]{1,0:T(8,128)(2,1)}, bf16[32,4096]{1,0:T(8,128)(2,1)S(1)}, u32[]{:S(2)}, u32[]{:S(2)}) collective-permute-start(bf16[32,4096]{1,0:T(8,128)(2,1)} %copy-done.8), channel_id=1, source_target_pairs={{0,2},{1,3},{2,4},{3,5},{4,6},{5,7},{6,8},{7,9},{8,10},{9,11},{10,... | collective-permute-start | bytes 786440 | tf_op jit(solution)/shard_map/ppermute | solution.py:256
  54.7 4.0 %collective-permute-start.11 = (bf16[32,4096]{1,0:T(8,128)(2,1)}, bf16[32,4096]{1,0:T(8,128)(2,1)S(1)}, u32[]{:S(2)}, u32[]{:S(2)}) collective-permute-start(bf16[32,4096]{1,0:T(8,128)(2,1)} %copy-done.6), channel_id=1, source_target_pairs={{0,14},{1,15},{2,0},{3,1},{4,2},{5,3},{6,4},{7,5},{8,6},{9,7},{10,... | collective-permute-start | bytes 786440 | tf_op jit(solution)/shard_map/ppermute | solution.py:256
  58.8 1.0 constant_dynamic-update-slice_fusion.6
  59.7 4.3 %collective-permute-done.8 = bf16[32,4096]{1,0:T(8,128)(2,1)S(1)} collective-permute-done((bf16[32,4096]{1,0:T(8,128)(2,1)}, bf16[32,4096]{1,0:T(8,128)(2,1)S(1)}, u32[]{:S(2)}, u32[]{:S(2)}) %collective-permute-start.8) | collective-permute-done | bytes 262176 | tf_op jit(solution)/shard_map/ppermute | solution.py:256
  64.0 0.0 collective-permute-start.9
  64.0 2.7 %collective-permute-start.12 = (bf16[32,4096]{1,0:T(8,128)(2,1)S(1)}, bf16[32,4096]{1,0:T(8,128)(2,1)S(1)}, u32[]{:S(2)}, u32[]{:S(2)}) collective-permute-start(bf16[32,4096]{1,0:T(8,128)(2,1)S(1)} %collective-permute-done.11), channel_id=1, source_target_pairs={{0,14},{1,15},{2,0},{3,1},{4,2},{5,3},{6,4},{7,5},{8,6},{9,7},{10,... | collective-permute-start | bytes 786440 | tf_op jit(solution)/shard_map/ppermute | solution.py:256
  66.7 4.2 %collective-permute-done.9 = bf16[32,4096]{1,0:T(8,128)(2,1)S(1)} collective-permute-done((bf16[32,4096]{1,0:T(8,128)(2,1)S(1)}, bf16[32,4096]{1,0:T(8,128)(2,1)S(1)}, u32[]{:S(2)}, u32[]{:S(2)}) %collective-permute-start.9) | collective-permute-done | bytes 262176 | tf_op jit(solution)/shard_map/ppermute | solution.py:256
  70.9 6.7 %collective-permute-done.10 = bf16[32,4096]{1,0:T(8,128)(2,1)S(1)} collective-permute-done((bf16[32,4096]{1,0:T(8,128)(2,1)S(1)}, bf16[32,4096]{1,0:T(8,128)(2,1)S(1)}, u32[]{:S(2)}, u32[]{:S(2)}) %collective-permute-start.10) | collective-permute-done | bytes 262176 | tf_op jit(solution)/shard_map/ppermute | solution.py:256
  77.8 1.3 %copy-done.1 = bf16[256,4096]{1,0:T(8,128)(2,1)} copy-done((bf16[256,4096]{1,0:T(8,128)(2,1)}, bf16[256,4096]{1,0:T(8,128)(2,1)S(1)}, u32[]{:S(2)}) %copy-start.1) | copy-done | bytes 2097176
  79.1 2.8 %all-to-all-done.1 = bf16[16,32,16,128]{3,2,1,0:T(8,128)(2,1)S(1)} async-done(((bf16[16,32,16,128]{3,2,1,0:T(8,128)(2,1)}), bf16[16,32,16,128]{3,2,1,0:T(8,128)(2,1)S(1)}, u32[]{:S(2)}, u32[]{:S(2)}) %all-to-all-start.1) | async-done | bytes 2097184 | tf_op jit(solution)/shard_map/all_to_all | solution.py:277
  81.9 0.9 front.1
  82.7 0.1 reshape.139
  82.8 3.0 %collective-permute-start.13 = (bf16[2,4096]{1,0:T(2,128)(2,1)S(1)}, bf16[2,4096]{1,0:T(2,128)(2,1)S(1)}, u32[]{:S(2)}, u32[]{:S(2)}) collective-permute-start(bf16[2,4096]{1,0:T(2,128)(2,1)S(1)} %reshape.139), channel_id=1, source_target_pairs={{0,1},{1,0},{2,3},{3,2},{4,5},{5,4},{6,7},{7,6},{8,9},{9,8},{10,11... | collective-permute-start | bytes 49160 | tf_op jit(solution)/shard_map/ppermute | solution.py:287
  85.9 1.6 %copy-done.2 = bf16[256,4096]{1,0:T(8,128)(2,1)S(1)} copy-done((bf16[256,4096]{1,0:T(8,128)(2,1)S(1)}, bf16[256,4096]{1,0:T(8,128)(2,1)}, u32[]{:S(2)}) %copy-start.2) | copy-done | bytes 2097176
  87.4 0.1 stage.1.queries_ref
  87.7 1.3 %raw.1 = f32[8,4,128]{2,1,0:T(4,128)} custom-call(s32[1]{0:T(128)} %bitcast.20.place_ref, bf16[4,4096]{1,0:T(4,128)(2,1)S(1)} %pad_maximum_fusion.1.grads_ref, bf16[256,4096]{1,0:T(8,128)(2,1)S(1)} %stage.1.queries_ref), custom_call_target="tpu_custom_call" | custom-call | tf_op jit(solution)/shard_map/raw/pallas_call | solution.py:94
  89.0 8.2 %all-to-all-start.2 = ((f32[8,4,128]{2,1,0:T(4,128)}), f32[8,4,128]{2,1,0:T(4,128)S(1)}, u32[]{:S(2)}, u32[]{:S(2)}) async-start(f32[8,4,128]{2,1,0:T(4,128)} %raw.1), calls=%async_computation.2 | async-start | bytes 32768 | tf_op jit(solution)/shard_map/all_to_all | solution.py:298
  97.2 2.7 %fusion.5 = (f32[128]{0:T(128)S(1)}, f32[128]{0:T(128)S(1)}) fusion(bf16[1,128,8192]{2,1,0:T(8,128)(2,1)} %param.9, f32[8192]{0:T(1024)S(1)} %bitcast.53, bf16[128,8192]{1,0:T(8,128)(2,1)S(1)} %bitcast.44), kind=kLoop, calls=%fused_computation.11 | loop fusion | flops 7339776 | bytes 4228096 | tf_op jit(solution)/shard_map/reduce_sum | solution.py:214
  99.9 3.9 %all-to-all-done.2.parts_ref = f32[8,4,128]{2,1,0:T(4,128)S(1)} async-done(((f32[8,4,128]{2,1,0:T(4,128)}), f32[8,4,128]{2,1,0:T(4,128)S(1)}, u32[]{:S(2)}, u32[]{:S(2)}) %all-to-all-start.2) | async-done | bytes 16416 | tf_op jit(solution)/shard_map/all_to_all | solution.py:298
  103.9 0.7 fold.1
  104.6 3.5 %all-to-all-start.3 = ((f32[16,16,128]{2,1,0:T(8,128)}), f32[16,16,128]{2,1,0:T(8,128)S(1)}, u32[]{:S(2)}, u32[]{:S(2)}) async-start(f32[16,16,128]{2,1,0:T(8,128)} %fold.1), calls=%async_computation.3 | async-start | bytes 262144 | tf_op jit(solution)/shard_map/all_to_all | solution.py:304
  108.1 4.6 %fusion.9 = bf16[1,128,8192]{2,1,0:T(8,128)(2,1)} fusion(bf16[128,8192]{1,0:T(8,128)(2,1)S(1)} %bitcast.45, f32[128]{0:T(128)S(1)} %broadcast_multiply_fusion, f32[128]{0:T(128)S(1)} %get-tuple-element.37, f32[8192]{0:T(1024)S(1)} %bitcast.54, f32[128]{0:T(128)S(1)} %get-tuple-element.36, bf16[1,128,8192]{2,1,0:T(8,128)(2,1)} %param.9), kind=kLoop, calls=%fused_computation.15 | loop fusion | flops 9437184 | bytes 6325760 | tf_op jit(solution)/shard_map/broadcast_in_dim | solution.py:310
  112.8 2.2 %all-to-all-done.3.parts_ref = f32[16,16,128]{2,1,0:T(8,128)S(1)} async-done(((f32[16,16,128]{2,1,0:T(8,128)}), f32[16,16,128]{2,1,0:T(8,128)S(1)}, u32[]{:S(2)}, u32[]{:S(2)}) %all-to-all-start.3) | async-done | bytes 131104 | tf_op jit(solution)/shard_map/all_to_all | solution.py:304
  115.0 0.7 scores.1
  (34 shorter events, 0.3 us)
Async XLA Ops:
  0.6 5.2 %copy-start = (s32[2]{0:T(128)S(1)}, s32[2]{0:T(128)}, u32[]{:S(2)}) copy-start(s32[2]{0:T(128)} %param.12) | copy-start | bytes 28
  0.6 5.8 %collective-permute-start = (f32[64,128]{1,0:T(8,128)}, f32[64,128]{1,0:T(8,128)S(1)}, u32[]{:S(2)}, u32[]{:S(2)}) collective-permute-start(f32[64,128]{1,0:T(8,128)} %bitcast.49), channel_id=1, source_target_pairs={{0,16},{16,32},{32,48},{48,0},{64,80},{80,96},{96,112},{112,64},{1... | collective-permute-start | bytes 98312 | tf_op jit(solution)/shard_map/ppermute | solution.py:240
  2.8 10.3 %collective-permute-start.2 = (f32[64,128]{1,0:T(8,128)}, f32[64,128]{1,0:T(8,128)S(1)}, u32[]{:S(2)}, u32[]{:S(2)}) collective-permute-start(f32[64,128]{1,0:T(8,128)} %bitcast.50), channel_id=1, source_target_pairs={{0,48},{16,0},{32,16},{48,32},{64,112},{80,64},{96,80},{112,96},{1... | collective-permute-start | bytes 98312 | tf_op jit(solution)/shard_map/ppermute | solution.py:240
  4.1 9.0 %collective-permute-start.1 = (f32[64,128]{1,0:T(8,128)}, f32[64,128]{1,0:T(8,128)S(1)}, u32[]{:S(2)}, u32[]{:S(2)}) collective-permute-start(f32[64,128]{1,0:T(8,128)} %bitcast.51), channel_id=1, source_target_pairs={{0,32},{16,48},{32,0},{48,16},{64,96},{80,112},{96,64},{112,80},{1... | collective-permute-start | bytes 98312 | tf_op jit(solution)/shard_map/ppermute | solution.py:240
  6.5 6.6 %copy-start.4 = (f32[1,8192]{1,0:T(1,128)S(1)}, f32[1,8192]{1,0:T(1,128)}, u32[]{:S(2)}) copy-start(f32[1,8192]{1,0:T(1,128)} %param.10) | copy-start | bytes 98308
  6.5 6.7 %copy-start.5 = (bf16[1,32,4096]{2,1,0:T(8,128)(2,1)S(1)}, bf16[1,32,4096]{2,1,0:T(8,128)(2,1)}, u32[]{:S(2)}) copy-start(bf16[1,32,4096]{2,1,0:T(8,128)(2,1)} %param.15) | copy-start | bytes 786436
  6.5 33.5 %all-to-all-start = ((bf16[16,32,16,128]{3,2,1,0:T(8,128)(2,1)}), bf16[16,32,16,128]{3,2,1,0:T(8,128)(2,1)S(1)}, u32[]{:S(2)}, u32[]{:S(2)}) async-start(bf16[16,32,16,128]{3,2,1,0:T(8,128)(2,1)} %bitcast.48), calls=%async_computation | async-start | bytes 4194304 | tf_op jit(solution)/shard_map/all_to_all | solution.py:267
  13.2 16.9 %collective-permute-start.3 = (bf16[32,4096]{1,0:T(8,128)(2,1)S(1)}, bf16[32,4096]{1,0:T(8,128)(2,1)S(1)}, u32[]{:S(2)}, u32[]{:S(2)}) collective-permute-start(bf16[32,4096]{1,0:T(8,128)(2,1)S(1)} %bitcast.55), channel_id=1, source_target_pairs={{0,2},{1,3},{2,4},{3,5},{4,6},{5,7},{6,8},{7,9},{8,10},{9,11},{10,... | collective-permute-start | bytes 786440 | tf_op jit(solution)/shard_map/ppermute | solution.py:256
  14.9 15.9 %collective-permute-start.4 = (bf16[32,4096]{1,0:T(8,128)(2,1)S(1)}, bf16[32,4096]{1,0:T(8,128)(2,1)S(1)}, u32[]{:S(2)}, u32[]{:S(2)}) collective-permute-start(bf16[32,4096]{1,0:T(8,128)(2,1)S(1)} %bitcast.56), channel_id=1, source_target_pairs={{0,14},{1,15},{2,0},{3,1},{4,2},{5,3},{6,4},{7,5},{8,6},{9,7},{10,... | collective-permute-start | bytes 786440 | tf_op jit(solution)/shard_map/ppermute | solution.py:256
  18.9 22.0 %collective-permute-start.5 = (f32[4,64,128]{2,1,0:T(8,128)S(1)}, f32[4,64,128]{2,1,0:T(8,128)S(1)}, u32[]{:S(2)}, u32[]{:S(2)}) collective-permute-start(f32[4,64,128]{2,1,0:T(8,128)S(1)} %pad_maximum_fusion.refs_0_), channel_id=1, source_target_pairs={{0,64},{16,80},{32,96},{48,112},{64,128},{80,144},{96,160},{112,17... | collective-permute-start | bytes 393224 | tf_op jit(solution)/shard_map/ppermute | solution.py:240
  20.3 21.5 %collective-permute-start.6 = (f32[4,64,128]{2,1,0:T(8,128)S(1)}, f32[4,64,128]{2,1,0:T(8,128)S(1)}, u32[]{:S(2)}, u32[]{:S(2)}) collective-permute-start(f32[4,64,128]{2,1,0:T(8,128)S(1)} %pad_maximum_fusion.refs_0_), channel_id=1, source_target_pairs={{0,128},{16,144},{32,160},{48,176},{64,192},{80,208},{96,224},{112... | collective-permute-start | bytes 393224 | tf_op jit(solution)/shard_map/ppermute | solution.py:240
  22.7 19.1 %collective-permute-start.7 = (f32[4,64,128]{2,1,0:T(8,128)S(1)}, f32[4,64,128]{2,1,0:T(8,128)S(1)}, u32[]{:S(2)}, u32[]{:S(2)}) collective-permute-start(f32[4,64,128]{2,1,0:T(8,128)S(1)} %pad_maximum_fusion.refs_0_), channel_id=1, source_target_pairs={{0,192},{16,208},{32,224},{48,240},{64,0},{80,16},{96,32},{112,48}... | collective-permute-start | bytes 393224 | tf_op jit(solution)/shard_map/ppermute | solution.py:240
  30.0 0.7 copy-start.8
  30.7 15.6 %copy-start.6 = (bf16[32,4096]{1,0:T(8,128)(2,1)}, bf16[32,4096]{1,0:T(8,128)(2,1)S(1)}, u32[]{:S(2)}) copy-start(bf16[32,4096]{1,0:T(8,128)(2,1)S(1)} %collective-permute-done.4) | copy-start | bytes 786436
  46.3 35.5 %all-to-all-start.1 = ((bf16[16,32,16,128]{3,2,1,0:T(8,128)(2,1)}), bf16[16,32,16,128]{3,2,1,0:T(8,128)(2,1)S(1)}, u32[]{:S(2)}, u32[]{:S(2)}) async-start(bf16[16,32,16,128]{3,2,1,0:T(8,128)(2,1)} %chain_all.1), calls=%async_computation.1 | async-start | bytes 4194304 | tf_op jit(solution)/shard_map/all_to_all | solution.py:277
  53.0 24.8 %copy-start.7 = (bf16[32,4096]{1,0:T(8,128)(2,1)S(1)}, bf16[32,4096]{1,0:T(8,128)(2,1)}, u32[]{:S(2)}) copy-start(bf16[32,4096]{1,0:T(8,128)(2,1)} %copy-done.6) | copy-start | bytes 786436
  53.0 28.9 %copy-start.3 = (bf16[1,64,8192]{2,1,0:T(8,128)(2,1)S(1)}, bf16[1,64,8192]{2,1,0:T(8,128)(2,1)}, u32[]{:S(2)}) copy-start(bf16[1,64,8192]{2,1,0:T(8,128)(2,1)} %param.14) | copy-start | bytes 3145732
  53.0 11.0 %collective-permute-start.8 = (bf16[32,4096]{1,0:T(8,128)(2,1)}, bf16[32,4096]{1,0:T(8,128)(2,1)S(1)}, u32[]{:S(2)}, u32[]{:S(2)}) collective-permute-start(bf16[32,4096]{1,0:T(8,128)(2,1)} %copy-done.8), channel_id=1, source_target_pairs={{0,2},{1,3},{2,4},{3,5},{4,6},{5,7},{6,8},{7,9},{8,10},{9,11},{10,... | collective-permute-start | bytes 786440 | tf_op jit(solution)/shard_map/ppermute | solution.py:256
  54.7 9.3 %collective-permute-start.11 = (bf16[32,4096]{1,0:T(8,128)(2,1)}, bf16[32,4096]{1,0:T(8,128)(2,1)S(1)}, u32[]{:S(2)}, u32[]{:S(2)}) collective-permute-start(bf16[32,4096]{1,0:T(8,128)(2,1)} %copy-done.6), channel_id=1, source_target_pairs={{0,14},{1,15},{2,0},{3,1},{4,2},{5,3},{6,4},{7,5},{8,6},{9,7},{10,... | collective-permute-start | bytes 786440 | tf_op jit(solution)/shard_map/ppermute | solution.py:256
  64.0 6.9 %collective-permute-start.9 = (bf16[32,4096]{1,0:T(8,128)(2,1)S(1)}, bf16[32,4096]{1,0:T(8,128)(2,1)S(1)}, u32[]{:S(2)}, u32[]{:S(2)}) collective-permute-start(bf16[32,4096]{1,0:T(8,128)(2,1)S(1)} %collective-permute-done.8), channel_id=1, source_target_pairs={{0,2},{1,3},{2,4},{3,5},{4,6},{5,7},{6,8},{7,9},{8,10},{9,11},{10,... | collective-permute-start | bytes 786440 | tf_op jit(solution)/shard_map/ppermute | solution.py:256
  64.0 13.6 %collective-permute-start.12 = (bf16[32,4096]{1,0:T(8,128)(2,1)S(1)}, bf16[32,4096]{1,0:T(8,128)(2,1)S(1)}, u32[]{:S(2)}, u32[]{:S(2)}) collective-permute-start(bf16[32,4096]{1,0:T(8,128)(2,1)S(1)} %collective-permute-done.11), channel_id=1, source_target_pairs={{0,14},{1,15},{2,0},{3,1},{4,2},{5,3},{6,4},{7,5},{8,6},{9,7},{10,... | collective-permute-start | bytes 786440 | tf_op jit(solution)/shard_map/ppermute | solution.py:256
  70.9 6.7 %collective-permute-start.10 = (bf16[32,4096]{1,0:T(8,128)(2,1)S(1)}, bf16[32,4096]{1,0:T(8,128)(2,1)S(1)}, u32[]{:S(2)}, u32[]{:S(2)}) collective-permute-start(bf16[32,4096]{1,0:T(8,128)(2,1)S(1)} %collective-permute-done.9), channel_id=1, source_target_pairs={{0,2},{1,3},{2,4},{3,5},{4,6},{5,7},{6,8},{7,9},{8,10},{9,11},{10,... | collective-permute-start | bytes 786440 | tf_op jit(solution)/shard_map/ppermute | solution.py:256
  77.8 1.3 %copy-start.1 = (bf16[256,4096]{1,0:T(8,128)(2,1)}, bf16[256,4096]{1,0:T(8,128)(2,1)S(1)}, u32[]{:S(2)}) copy-start(bf16[256,4096]{1,0:T(8,128)(2,1)S(1)} %constant_dynamic-update-slice_fusion.queries_ref) | copy-start | bytes 6291460
  82.8 4.8 %collective-permute-start.13 = (bf16[2,4096]{1,0:T(2,128)(2,1)S(1)}, bf16[2,4096]{1,0:T(2,128)(2,1)S(1)}, u32[]{:S(2)}, u32[]{:S(2)}) collective-permute-start(bf16[2,4096]{1,0:T(2,128)(2,1)S(1)} %reshape.139), channel_id=1, source_target_pairs={{0,1},{1,0},{2,3},{3,2},{4,5},{5,4},{6,7},{7,6},{8,9},{9,8},{10,11... | collective-permute-start | bytes 49160 | tf_op jit(solution)/shard_map/ppermute | solution.py:287
  85.9 1.6 %copy-start.2 = (bf16[256,4096]{1,0:T(8,128)(2,1)S(1)}, bf16[256,4096]{1,0:T(8,128)(2,1)}, u32[]{:S(2)}) copy-start(bf16[256,4096]{1,0:T(8,128)(2,1)} %copy-done.1) | copy-start | bytes 6291460
  89.0 14.8 %all-to-all-start.2 = ((f32[8,4,128]{2,1,0:T(4,128)}), f32[8,4,128]{2,1,0:T(4,128)S(1)}, u32[]{:S(2)}, u32[]{:S(2)}) async-start(f32[8,4,128]{2,1,0:T(4,128)} %raw.1), calls=%async_computation.2 | async-start | bytes 32768 | tf_op jit(solution)/shard_map/all_to_all | solution.py:298
  104.6 10.3 %all-to-all-start.3 = ((f32[16,16,128]{2,1,0:T(8,128)}), f32[16,16,128]{2,1,0:T(8,128)S(1)}, u32[]{:S(2)}, u32[]{:S(2)}) async-start(f32[16,16,128]{2,1,0:T(8,128)} %fold.1), calls=%async_computation.3 | async-start | bytes 262144 | tf_op jit(solution)/shard_map/all_to_all | solution.py:304

commit v4 on v3

--- a/solution.py
+++ b/solution.py
@@ -241,7 +241,7 @@
 
     gain_tiles = norm_gain.reshape(-1, LANES)
     across = [moved(gain_tiles, 0, k) for k in range(1, side)]
-    resid_first, across[0] = lax.optimization_barrier((resid_rows, across[0]))
+    resid_first = resid_rows
     near = [jnp.stack([gain_tiles] + across)]
     near[0], own_queries = lax.optimization_barrier((near[0], queries[0]))
     near += [moved(near[0], k, 0) for k in range(1, side)]

time: 116 us -> 116 us (level)
  no operation moved by 1% of the time
where the time goes in v4:
time: 116 us; the launch traced here: 115 us
  starting transfers between devices  50.9 us (44%)
  waiting for transfers between devices  34.6 us (30%)
  other arithmetic  8.46 us (7%)
  Pallas kernels  8.34 us (7%)
  matrix products  6.16 us (5%)
  local copies, waits for them, and re-layouts  5.51 us (5%)
    ppermute x7, waiting for transfers between devices, around(): lax.ppermute(value, 'dp', [(i, (i + 2 * steps) % ranks) for i in range(ra...  15.2 us
    ppermute x7, starting transfers between devices, around(): lax.ppermute(value, 'dp', [(i, (i + 2 * steps) % ranks) for i in range(ra...  14.2 us
    ppermute x6, starting transfers between devices, moved(): return lax.ppermute(value, 'section', pairs)  9.44 us
    all_to_all x1, waiting for transfers between devices, shards(): recv = lax.all_to_all(to_tiles(resid_first), 'section', 0, 0)  8.51 us
    all_to_all x1, starting transfers between devices, shards(): raw = lax.all_to_all(raw, 'dp', 0, 0, axis_index_groups=same_core)  8.18 us
    all_to_all x1, starting transfers between devices, shards(): lax.all_to_all(grads, 'section', 0, 0)  6.43 us
    all_to_all x1, starting transfers between devices, shards(): recv = lax.all_to_all(to_tiles(resid_first), 'section', 0, 0)  6.21 us
    dot_general x1, matrix products, shards(): jnp.einsum('tf,rf->tr', hidden_acts[0], proj_in[0], preferred_element_typ...  6.16 us
  transfers between devices with their start and end apart: 18, of which 9 were waited for; matrix products, arithmetic and copies ran while one was open for 14% of the time, Pallas kernels for 0%

profile of v4, /device:TPU:1, one launch (start us, length us, event | category | flops | bytes accessed | tf_op | source)
XLA Modules:
  0.0 114.9 jit_solution(14778691095524648737)
XLA Ops:
  0.6 0.0 copy-start
  0.6 3.4 %collective-permute-start.2 = (f32[64,128]{1,0:T(8,128)}, f32[64,128]{1,0:T(8,128)S(1)}, u32[]{:S(2)}, u32[]{:S(2)}) collective-permute-start(f32[64,128]{1,0:T(8,128)} %bitcast.50), channel_id=1, source_target_pairs={{0,48},{16,0},{32,16},{48,32},{64,112},{80,64},{96,80},{112,96},{1... | collective-permute-start | bytes 98312 | tf_op jit(solution)/shard_map/ppermute | solution.py:240
  4.0 0.5 collective-permute-start.1
  4.6 0.6 collective-permute-start
  5.2 6.2 %all-to-all-start = ((bf16[16,32,16,128]{3,2,1,0:T(8,128)(2,1)}), bf16[16,32,16,128]{3,2,1,0:T(8,128)(2,1)S(1)}, u32[]{:S(2)}, u32[]{:S(2)}) async-start(bf16[16,32,16,128]{3,2,1,0:T(8,128)(2,1)} %bitcast.49), calls=%async_computation | async-start | bytes 4194304 | tf_op jit(solution)/shard_map/all_to_all | solution.py:267
  11.4 0.6 gather_fusion
  12.1 1.0 dynamic-slice_select_fusion
  13.1 0.0 collective-permute-done
  13.2 1.7 %collective-permute-start.3 = (bf16[32,4096]{1,0:T(8,128)(2,1)S(1)}, bf16[32,4096]{1,0:T(8,128)(2,1)S(1)}, u32[]{:S(2)}, u32[]{:S(2)}) collective-permute-start(bf16[32,4096]{1,0:T(8,128)(2,1)S(1)} %bitcast.56), channel_id=1, source_target_pairs={{0,2},{1,3},{2,4},{3,5},{4,6},{5,7},{6,8},{7,9},{8,10},{9,11},{10,... | collective-permute-start | bytes 786440 | tf_op jit(solution)/shard_map/ppermute | solution.py:256
  14.9 4.0 %collective-permute-start.4 = (bf16[32,4096]{1,0:T(8,128)(2,1)S(1)}, bf16[32,4096]{1,0:T(8,128)(2,1)S(1)}, u32[]{:S(2)}, u32[]{:S(2)}) collective-permute-start(bf16[32,4096]{1,0:T(8,128)(2,1)S(1)} %bitcast.57), channel_id=1, source_target_pairs={{0,14},{1,15},{2,0},{3,1},{4,2},{5,3},{6,4},{7,5},{8,6},{9,7},{10,... | collective-permute-start | bytes 786440 | tf_op jit(solution)/shard_map/ppermute | solution.py:256
  18.9 1.4 %collective-permute-start.5 = (f32[4,64,128]{2,1,0:T(8,128)S(1)}, f32[4,64,128]{2,1,0:T(8,128)S(1)}, u32[]{:S(2)}, u32[]{:S(2)}) collective-permute-start(f32[4,64,128]{2,1,0:T(8,128)S(1)} %pad_maximum_fusion.refs_0_), channel_id=1, source_target_pairs={{0,64},{16,80},{32,96},{48,112},{64,128},{80,144},{96,160},{112,17... | collective-permute-start | bytes 393224 | tf_op jit(solution)/shard_map/ppermute | solution.py:240
  20.3 2.4 %collective-permute-start.6 = (f32[4,64,128]{2,1,0:T(8,128)S(1)}, f32[4,64,128]{2,1,0:T(8,128)S(1)}, u32[]{:S(2)}, u32[]{:S(2)}) collective-permute-start(f32[4,64,128]{2,1,0:T(8,128)S(1)} %pad_maximum_fusion.refs_0_), channel_id=1, source_target_pairs={{0,128},{16,144},{32,160},{48,176},{64,192},{80,208},{96,224},{112... | collective-permute-start | bytes 393224 | tf_op jit(solution)/shard_map/ppermute | solution.py:240
  22.7 1.2 %collective-permute-start.7 = (f32[4,64,128]{2,1,0:T(8,128)S(1)}, f32[4,64,128]{2,1,0:T(8,128)S(1)}, u32[]{:S(2)}, u32[]{:S(2)}) collective-permute-start(f32[4,64,128]{2,1,0:T(8,128)S(1)} %pad_maximum_fusion.refs_0_), channel_id=1, source_target_pairs={{0,192},{16,208},{32,224},{48,240},{64,0},{80,16},{96,32},{112,48}... | collective-permute-start | bytes 393224 | tf_op jit(solution)/shard_map/ppermute | solution.py:240
  23.9 6.2 %fusion.10.side_in_ref = bf16[128,64]{1,0:T(8,128)(2,1)S(1)} fusion(bf16[1,64,28672]{2,1,0:T(8,128)(2,1)} %param.13, bf16[1,128,28672]{2,1,0:T(8,128)(2,1)} %param.8), kind=kOutput, calls=%fused_computation.16 | convolution fusion | flops 469770240 | bytes 11026432 | tf_op jit(solution)/shard_map/tf,rf->tr/dot_general | solution.py:249
  30.0 0.0 collective-permute-done.3
  30.0 0.7 copy-done.8
  30.7 0.0 collective-permute-done.4
  30.8 8.5 %all-to-all-done.recv_ref = bf16[16,32,16,128]{3,2,1,0:T(8,128)(2,1)S(1)} async-done(((bf16[16,32,16,128]{3,2,1,0:T(8,128)(2,1)}), bf16[16,32,16,128]{3,2,1,0:T(8,128)(2,1)S(1)}, u32[]{:S(2)}, u32[]{:S(2)}) %all-to-all-start) | async-done | bytes 2097184 | tf_op jit(solution)/shard_map/all_to_all | solution.py:267
  39.3 1.2 %collective-permute-done.5.refs_1_ = f32[4,64,128]{2,1,0:T(8,128)S(1)} collective-permute-done((f32[4,64,128]{2,1,0:T(8,128)S(1)}, f32[4,64,128]{2,1,0:T(8,128)S(1)}, u32[]{:S(2)}, u32[]{:S(2)}) %collective-permute-start.5) | collective-permute-done | bytes 131104 | tf_op jit(solution)/shard_map/ppermute | solution.py:240
  40.4 0.8 collective-permute-done.6.refs_2_
  41.3 4.5 %chain_all.1 = bf16[16,32,16,128]{3,2,1,0:T(8,128)(2,1)} custom-call(s32[1]{0:T(128)} %bitcast.place_ref, bf16[16,32,16,128]{3,2,1,0:T(8,128)(2,1)S(1)} %all-to-all-done.recv_ref, bf16[32,16,128]{2,1,0:T(8,128)(2,1)S(1)} %bitcast.48, f32[4,64,128]{2,1,0:T(8,128)S(1)} %pad_maximum_fusion.refs_0_, f32[4,64,128]{2,1,0:T(8,128)S(1)} %collective-permute-done.5.refs_1_, ...), custom_call_target="tpu_custom_call" | custom-call | tf_op jit(solution)/shard_map/chain_all/pallas_call | solution.py:111
  45.8 6.4 %all-to-all-start.1 = ((bf16[16,32,16,128]{3,2,1,0:T(8,128)(2,1)}), bf16[16,32,16,128]{3,2,1,0:T(8,128)(2,1)S(1)}, u32[]{:S(2)}, u32[]{:S(2)}) async-start(bf16[16,32,16,128]{3,2,1,0:T(8,128)(2,1)} %chain_all.1), calls=%async_computation.1 | async-start | bytes 4194304 | tf_op jit(solution)/shard_map/all_to_all | solution.py:277
  52.3 0.0 copy-start.3
  52.3 1.7 %collective-permute-start.8 = (bf16[32,4096]{1,0:T(8,128)(2,1)}, bf16[32,4096]{1,0:T(8,128)(2,1)S(1)}, u32[]{:S(2)}, u32[]{:S(2)}) collective-permute-start(bf16[32,4096]{1,0:T(8,128)(2,1)} %copy-done.8), channel_id=1, source_target_pairs={{0,2},{1,3},{2,4},{3,5},{4,6},{5,7},{6,8},{7,9},{8,10},{9,11},{10,... | collective-permute-start | bytes 786440 | tf_op jit(solution)/shard_map/ppermute | solution.py:256
  54.0 4.0 %collective-permute-start.11 = (bf16[32,4096]{1,0:T(8,128)(2,1)}, bf16[32,4096]{1,0:T(8,128)(2,1)S(1)}, u32[]{:S(2)}, u32[]{:S(2)}) collective-permute-start(bf16[32,4096]{1,0:T(8,128)(2,1)} %copy-done.6), channel_id=1, source_target_pairs={{0,14},{1,15},{2,0},{3,1},{4,2},{5,3},{6,4},{7,5},{8,6},{9,7},{10,... | collective-permute-start | bytes 786440 | tf_op jit(solution)/shard_map/ppermute | solution.py:256
  58.0 1.0 constant_dynamic-update-slice_fusion.6
  59.0 4.3 %collective-permute-done.8 = bf16[32,4096]{1,0:T(8,128)(2,1)S(1)} collective-permute-done((bf16[32,4096]{1,0:T(8,128)(2,1)}, bf16[32,4096]{1,0:T(8,128)(2,1)S(1)}, u32[]{:S(2)}, u32[]{:S(2)}) %collective-permute-start.8) | collective-permute-done | bytes 262176 | tf_op jit(solution)/shard_map/ppermute | solution.py:256
  63.3 0.0 collective-permute-start.9
  63.3 0.0 collective-permute-done.11
  63.3 2.7 %collective-permute-start.12 = (bf16[32,4096]{1,0:T(8,128)(2,1)S(1)}, bf16[32,4096]{1,0:T(8,128)(2,1)S(1)}, u32[]{:S(2)}, u32[]{:S(2)}) collective-permute-start(bf16[32,4096]{1,0:T(8,128)(2,1)S(1)} %collective-permute-done.11), channel_id=1, source_target_pairs={{0,14},{1,15},{2,0},{3,1},{4,2},{5,3},{6,4},{7,5},{8,6},{9,7},{10,... | collective-permute-start | bytes 786440 | tf_op jit(solution)/shard_map/ppermute | solution.py:256
  66.0 4.2 %collective-permute-done.9 = bf16[32,4096]{1,0:T(8,128)(2,1)S(1)} collective-permute-done((bf16[32,4096]{1,0:T(8,128)(2,1)S(1)}, bf16[32,4096]{1,0:T(8,128)(2,1)S(1)}, u32[]{:S(2)}, u32[]{:S(2)}) %collective-permute-start.9) | collective-permute-done | bytes 262176 | tf_op jit(solution)/shard_map/ppermute | solution.py:256
  70.2 6.7 %collective-permute-done.10 = bf16[32,4096]{1,0:T(8,128)(2,1)S(1)} collective-permute-done((bf16[32,4096]{1,0:T(8,128)(2,1)S(1)}, bf16[32,4096]{1,0:T(8,128)(2,1)S(1)}, u32[]{:S(2)}, u32[]{:S(2)}) %collective-permute-start.10) | collective-permute-done | bytes 262176 | tf_op jit(solution)/shard_map/ppermute | solution.py:256
  77.0 1.3 %copy-done.1 = bf16[256,4096]{1,0:T(8,128)(2,1)} copy-done((bf16[256,4096]{1,0:T(8,128)(2,1)}, bf16[256,4096]{1,0:T(8,128)(2,1)S(1)}, u32[]{:S(2)}) %copy-start.1) | copy-done | bytes 2097176
  78.4 2.8 %all-to-all-done.1 = bf16[16,32,16,128]{3,2,1,0:T(8,128)(2,1)S(1)} async-done(((bf16[16,32,16,128]{3,2,1,0:T(8,128)(2,1)}), bf16[16,32,16,128]{3,2,1,0:T(8,128)(2,1)S(1)}, u32[]{:S(2)}, u32[]{:S(2)}) %all-to-all-start.1) | async-done | bytes 2097184 | tf_op jit(solution)/shard_map/all_to_all | solution.py:277
  81.1 0.9 front.1
  82.0 0.1 reshape.137
  82.1 3.0 %collective-permute-start.13 = (bf16[2,4096]{1,0:T(2,128)(2,1)S(1)}, bf16[2,4096]{1,0:T(2,128)(2,1)S(1)}, u32[]{:S(2)}, u32[]{:S(2)}) collective-permute-start(bf16[2,4096]{1,0:T(2,128)(2,1)S(1)} %reshape.137), channel_id=1, source_target_pairs={{0,1},{1,0},{2,3},{3,2},{4,5},{5,4},{6,7},{7,6},{8,9},{9,8},{10,11... | collective-permute-start | bytes 49160 | tf_op jit(solution)/shard_map/ppermute | solution.py:287
  85.1 1.6 %copy-done.2 = bf16[256,4096]{1,0:T(8,128)(2,1)S(1)} copy-done((bf16[256,4096]{1,0:T(8,128)(2,1)S(1)}, bf16[256,4096]{1,0:T(8,128)(2,1)}, u32[]{:S(2)}) %copy-start.2) | copy-done | bytes 2097176
  86.7 0.1 stage.1.queries_ref
  87.0 1.3 %raw.1 = f32[8,4,128]{2,1,0:T(4,128)} custom-call(s32[1]{0:T(128)} %bitcast.19.place_ref, bf16[4,4096]{1,0:T(4,128)(2,1)S(1)} %pad_maximum_fusion.1.grads_ref, bf16[256,4096]{1,0:T(8,128)(2,1)S(1)} %stage.1.queries_ref), custom_call_target="tpu_custom_call" | custom-call | tf_op jit(solution)/shard_map/raw/pallas_call | solution.py:94
  88.3 8.2 %all-to-all-start.2 = ((f32[8,4,128]{2,1,0:T(4,128)}), f32[8,4,128]{2,1,0:T(4,128)S(1)}, u32[]{:S(2)}, u32[]{:S(2)}) async-start(f32[8,4,128]{2,1,0:T(4,128)} %raw.1), calls=%async_computation.2 | async-start | bytes 32768 | tf_op jit(solution)/shard_map/all_to_all | solution.py:298
  96.5 2.7 %fusion.5 = (f32[128]{0:T(128)S(1)}, f32[128]{0:T(128)S(1)}) fusion(bf16[1,128,8192]{2,1,0:T(8,128)(2,1)} %param.9, f32[8192]{0:T(1024)S(1)} %bitcast.54, bf16[128,8192]{1,0:T(8,128)(2,1)S(1)} %bitcast.45), kind=kLoop, calls=%fused_computation.11 | loop fusion | flops 7339776 | bytes 4228096 | tf_op jit(solution)/shard_map/reduce_sum | solution.py:214
  99.2 3.9 %all-to-all-done.2.parts_ref = f32[8,4,128]{2,1,0:T(4,128)S(1)} async-done(((f32[8,4,128]{2,1,0:T(4,128)}), f32[8,4,128]{2,1,0:T(4,128)S(1)}, u32[]{:S(2)}, u32[]{:S(2)}) %all-to-all-start.2) | async-done | bytes 16416 | tf_op jit(solution)/shard_map/all_to_all | solution.py:298
  103.1 0.7 fold.1
  103.9 3.5 %all-to-all-start.3 = ((f32[16,16,128]{2,1,0:T(8,128)}), f32[16,16,128]{2,1,0:T(8,128)S(1)}, u32[]{:S(2)}, u32[]{:S(2)}) async-start(f32[16,16,128]{2,1,0:T(8,128)} %fold.1), calls=%async_computation.3 | async-start | bytes 262144 | tf_op jit(solution)/shard_map/all_to_all | solution.py:304
  107.4 4.6 %fusion.9 = bf16[1,128,8192]{2,1,0:T(8,128)(2,1)} fusion(bf16[128,8192]{1,0:T(8,128)(2,1)S(1)} %bitcast.46, bf16[1,128,8192]{2,1,0:T(8,128)(2,1)} %param.9, f32[128]{0:T(128)S(1)} %broadcast_multiply_fusion, f32[128]{0:T(128)S(1)} %get-tuple-element.33, f32[8192]{0:T(1024)S(1)} %bitcast.55, f32[128]{0:T(128)S(1)} %get-tuple-element.32), kind=kLoop, calls=%fused_computation.15 | loop fusion | flops 9437184 | bytes 6325760 | tf_op jit(solution)/shard_map/broadcast_in_dim | solution.py:310
  112.0 2.2 %all-to-all-done.3.parts_ref = f32[16,16,128]{2,1,0:T(8,128)S(1)} async-done(((f32[16,16,128]{2,1,0:T(8,128)}), f32[16,16,128]{2,1,0:T(8,128)S(1)}, u32[]{:S(2)}, u32[]{:S(2)}) %all-to-all-start.3) | async-done | bytes 131104 | tf_op jit(solution)/shard_map/all_to_all | solution.py:304
  114.2 0.7 scores.1
  (34 shorter events, 0.3 us)
Async XLA Ops:
  0.6 10.8 %copy-start = (s32[2]{0:T(128)S(1)}, s32[2]{0:T(128)}, u32[]{:S(2)}) copy-start(s32[2]{0:T(128)} %param.12) | copy-start | bytes 28
  0.6 12.5 %collective-permute-start.2 = (f32[64,128]{1,0:T(8,128)}, f32[64,128]{1,0:T(8,128)S(1)}, u32[]{:S(2)}, u32[]{:S(2)}) collective-permute-start(f32[64,128]{1,0:T(8,128)} %bitcast.50), channel_id=1, source_target_pairs={{0,48},{16,0},{32,16},{48,32},{64,112},{80,64},{96,80},{112,96},{1... | collective-permute-start | bytes 98312 | tf_op jit(solution)/shard_map/ppermute | solution.py:240
  4.0 9.1 %collective-permute-start.1 = (f32[64,128]{1,0:T(8,128)}, f32[64,128]{1,0:T(8,128)S(1)}, u32[]{:S(2)}, u32[]{:S(2)}) collective-permute-start(f32[64,128]{1,0:T(8,128)} %bitcast.51), channel_id=1, source_target_pairs={{0,32},{16,48},{32,0},{48,16},{64,96},{80,112},{96,64},{112,80},{1... | collective-permute-start | bytes 98312 | tf_op jit(solution)/shard_map/ppermute | solution.py:240
  4.6 8.6 %collective-permute-start = (f32[64,128]{1,0:T(8,128)}, f32[64,128]{1,0:T(8,128)S(1)}, u32[]{:S(2)}, u32[]{:S(2)}) collective-permute-start(f32[64,128]{1,0:T(8,128)} %bitcast.52), channel_id=1, source_target_pairs={{0,16},{16,32},{32,48},{48,0},{64,80},{80,96},{96,112},{112,64},{1... | collective-permute-start | bytes 98312 | tf_op jit(solution)/shard_map/ppermute | solution.py:240
  5.2 8.0 %copy-start.4 = (f32[1,8192]{1,0:T(1,128)S(1)}, f32[1,8192]{1,0:T(1,128)}, u32[]{:S(2)}) copy-start(f32[1,8192]{1,0:T(1,128)} %param.10) | copy-start | bytes 98308
  5.2 8.0 %copy-start.5 = (bf16[1,32,4096]{2,1,0:T(8,128)(2,1)S(1)}, bf16[1,32,4096]{2,1,0:T(8,128)(2,1)}, u32[]{:S(2)}) copy-start(bf16[1,32,4096]{2,1,0:T(8,128)(2,1)} %param.15) | copy-start | bytes 786436
  5.2 34.1 %all-to-all-start = ((bf16[16,32,16,128]{3,2,1,0:T(8,128)(2,1)}), bf16[16,32,16,128]{3,2,1,0:T(8,128)(2,1)S(1)}, u32[]{:S(2)}, u32[]{:S(2)}) async-start(bf16[16,32,16,128]{3,2,1,0:T(8,128)(2,1)} %bitcast.49), calls=%async_computation | async-start | bytes 4194304 | tf_op jit(solution)/shard_map/all_to_all | solution.py:267
  13.2 16.8 %collective-permute-start.3 = (bf16[32,4096]{1,0:T(8,128)(2,1)S(1)}, bf16[32,4096]{1,0:T(8,128)(2,1)S(1)}, u32[]{:S(2)}, u32[]{:S(2)}) collective-permute-start(bf16[32,4096]{1,0:T(8,128)(2,1)S(1)} %bitcast.56), channel_id=1, source_target_pairs={{0,2},{1,3},{2,4},{3,5},{4,6},{5,7},{6,8},{7,9},{8,10},{9,11},{10,... | collective-permute-start | bytes 786440 | tf_op jit(solution)/shard_map/ppermute | solution.py:256
  14.9 15.9 %collective-permute-start.4 = (bf16[32,4096]{1,0:T(8,128)(2,1)S(1)}, bf16[32,4096]{1,0:T(8,128)(2,1)S(1)}, u32[]{:S(2)}, u32[]{:S(2)}) collective-permute-start(bf16[32,4096]{1,0:T(8,128)(2,1)S(1)} %bitcast.57), channel_id=1, source_target_pairs={{0,14},{1,15},{2,0},{3,1},{4,2},{5,3},{6,4},{7,5},{8,6},{9,7},{10,... | collective-permute-start | bytes 786440 | tf_op jit(solution)/shard_map/ppermute | solution.py:256
  18.9 21.5 %collective-permute-start.5 = (f32[4,64,128]{2,1,0:T(8,128)S(1)}, f32[4,64,128]{2,1,0:T(8,128)S(1)}, u32[]{:S(2)}, u32[]{:S(2)}) collective-permute-start(f32[4,64,128]{2,1,0:T(8,128)S(1)} %pad_maximum_fusion.refs_0_), channel_id=1, source_target_pairs={{0,64},{16,80},{32,96},{48,112},{64,128},{80,144},{96,160},{112,17... | collective-permute-start | bytes 393224 | tf_op jit(solution)/shard_map/ppermute | solution.py:240
  20.3 21.0 %collective-permute-start.6 = (f32[4,64,128]{2,1,0:T(8,128)S(1)}, f32[4,64,128]{2,1,0:T(8,128)S(1)}, u32[]{:S(2)}, u32[]{:S(2)}) collective-permute-start(f32[4,64,128]{2,1,0:T(8,128)S(1)} %pad_maximum_fusion.refs_0_), channel_id=1, source_target_pairs={{0,128},{16,144},{32,160},{48,176},{64,192},{80,208},{96,224},{112... | collective-permute-start | bytes 393224 | tf_op jit(solution)/shard_map/ppermute | solution.py:240
  22.7 18.6 %collective-permute-start.7 = (f32[4,64,128]{2,1,0:T(8,128)S(1)}, f32[4,64,128]{2,1,0:T(8,128)S(1)}, u32[]{:S(2)}, u32[]{:S(2)}) collective-permute-start(f32[4,64,128]{2,1,0:T(8,128)S(1)} %pad_maximum_fusion.refs_0_), channel_id=1, source_target_pairs={{0,192},{16,208},{32,224},{48,240},{64,0},{80,16},{96,32},{112,48}... | collective-permute-start | bytes 393224 | tf_op jit(solution)/shard_map/ppermute | solution.py:240
  30.0 0.7 copy-start.8
  30.8 15.1 %copy-start.6 = (bf16[32,4096]{1,0:T(8,128)(2,1)}, bf16[32,4096]{1,0:T(8,128)(2,1)S(1)}, u32[]{:S(2)}) copy-start(bf16[32,4096]{1,0:T(8,128)(2,1)S(1)} %collective-permute-done.4) | copy-start | bytes 786436
  45.8 35.3 %all-to-all-start.1 = ((bf16[16,32,16,128]{3,2,1,0:T(8,128)(2,1)}), bf16[16,32,16,128]{3,2,1,0:T(8,128)(2,1)S(1)}, u32[]{:S(2)}, u32[]{:S(2)}) async-start(bf16[16,32,16,128]{3,2,1,0:T(8,128)(2,1)} %chain_all.1), calls=%async_computation.1 | async-start | bytes 4194304 | tf_op jit(solution)/shard_map/all_to_all | solution.py:277
  52.2 24.8 %copy-start.7 = (bf16[32,4096]{1,0:T(8,128)(2,1)S(1)}, bf16[32,4096]{1,0:T(8,128)(2,1)}, u32[]{:S(2)}) copy-start(bf16[32,4096]{1,0:T(8,128)(2,1)} %copy-done.6) | copy-start | bytes 786436
  52.3 28.9 %copy-start.3 = (bf16[1,64,8192]{2,1,0:T(8,128)(2,1)S(1)}, bf16[1,64,8192]{2,1,0:T(8,128)(2,1)}, u32[]{:S(2)}) copy-start(bf16[1,64,8192]{2,1,0:T(8,128)(2,1)} %param.14) | copy-start | bytes 3145732
  52.3 11.0 %collective-permute-start.8 = (bf16[32,4096]{1,0:T(8,128)(2,1)}, bf16[32,4096]{1,0:T(8,128)(2,1)S(1)}, u32[]{:S(2)}, u32[]{:S(2)}) collective-permute-start(bf16[32,4096]{1,0:T(8,128)(2,1)} %copy-done.8), channel_id=1, source_target_pairs={{0,2},{1,3},{2,4},{3,5},{4,6},{5,7},{6,8},{7,9},{8,10},{9,11},{10,... | collective-permute-start | bytes 786440 | tf_op jit(solution)/shard_map/ppermute | solution.py:256
  54.0 9.3 %collective-permute-start.11 = (bf16[32,4096]{1,0:T(8,128)(2,1)}, bf16[32,4096]{1,0:T(8,128)(2,1)S(1)}, u32[]{:S(2)}, u32[]{:S(2)}) collective-permute-start(bf16[32,4096]{1,0:T(8,128)(2,1)} %copy-done.6), channel_id=1, source_target_pairs={{0,14},{1,15},{2,0},{3,1},{4,2},{5,3},{6,4},{7,5},{8,6},{9,7},{10,... | collective-permute-start | bytes 786440 | tf_op jit(solution)/shard_map/ppermute | solution.py:256
  63.3 6.9 %collective-permute-start.9 = (bf16[32,4096]{1,0:T(8,128)(2,1)S(1)}, bf16[32,4096]{1,0:T(8,128)(2,1)S(1)}, u32[]{:S(2)}, u32[]{:S(2)}) collective-permute-start(bf16[32,4096]{1,0:T(8,128)(2,1)S(1)} %collective-permute-done.8), channel_id=1, source_target_pairs={{0,2},{1,3},{2,4},{3,5},{4,6},{5,7},{6,8},{7,9},{8,10},{9,11},{10,... | collective-permute-start | bytes 786440 | tf_op jit(solution)/shard_map/ppermute | solution.py:256
  63.3 13.6 %collective-permute-start.12 = (bf16[32,4096]{1,0:T(8,128)(2,1)S(1)}, bf16[32,4096]{1,0:T(8,128)(2,1)S(1)}, u32[]{:S(2)}, u32[]{:S(2)}) collective-permute-start(bf16[32,4096]{1,0:T(8,128)(2,1)S(1)} %collective-permute-done.11), channel_id=1, source_target_pairs={{0,14},{1,15},{2,0},{3,1},{4,2},{5,3},{6,4},{7,5},{8,6},{9,7},{10,... | collective-permute-start | bytes 786440 | tf_op jit(solution)/shard_map/ppermute | solution.py:256
  70.2 6.7 %collective-permute-start.10 = (bf16[32,4096]{1,0:T(8,128)(2,1)S(1)}, bf16[32,4096]{1,0:T(8,128)(2,1)S(1)}, u32[]{:S(2)}, u32[]{:S(2)}) collective-permute-start(bf16[32,4096]{1,0:T(8,128)(2,1)S(1)} %collective-permute-done.9), channel_id=1, source_target_pairs={{0,2},{1,3},{2,4},{3,5},{4,6},{5,7},{6,8},{7,9},{8,10},{9,11},{10,... | collective-permute-start | bytes 786440 | tf_op jit(solution)/shard_map/ppermute | solution.py:256
  77.0 1.3 %copy-start.1 = (bf16[256,4096]{1,0:T(8,128)(2,1)}, bf16[256,4096]{1,0:T(8,128)(2,1)S(1)}, u32[]{:S(2)}) copy-start(bf16[256,4096]{1,0:T(8,128)(2,1)S(1)} %constant_dynamic-update-slice_fusion.queries_ref) | copy-start | bytes 6291460
  82.1 4.8 %collective-permute-start.13 = (bf16[2,4096]{1,0:T(2,128)(2,1)S(1)}, bf16[2,4096]{1,0:T(2,128)(2,1)S(1)}, u32[]{:S(2)}, u32[]{:S(2)}) collective-permute-start(bf16[2,4096]{1,0:T(2,128)(2,1)S(1)} %reshape.137), channel_id=1, source_target_pairs={{0,1},{1,0},{2,3},{3,2},{4,5},{5,4},{6,7},{7,6},{8,9},{9,8},{10,11... | collective-permute-start | bytes 49160 | tf_op jit(solution)/shard_map/ppermute | solution.py:287
  85.1 1.6 %copy-start.2 = (bf16[256,4096]{1,0:T(8,128)(2,1)S(1)}, bf16[256,4096]{1,0:T(8,128)(2,1)}, u32[]{:S(2)}) copy-start(bf16[256,4096]{1,0:T(8,128)(2,1)} %copy-done.1) | copy-start | bytes 6291460
  88.3 14.8 %all-to-all-start.2 = ((f32[8,4,128]{2,1,0:T(4,128)}), f32[8,4,128]{2,1,0:T(4,128)S(1)}, u32[]{:S(2)}, u32[]{:S(2)}) async-start(f32[8,4,128]{2,1,0:T(4,128)} %raw.1), calls=%async_computation.2 | async-start | bytes 32768 | tf_op jit(solution)/shard_map/all_to_all | solution.py:298
  103.9 10.3 %all-to-all-start.3 = ((f32[16,16,128]{2,1,0:T(8,128)}), f32[16,16,128]{2,1,0:T(8,128)S(1)}, u32[]{:S(2)}, u32[]{:S(2)}) async-start(f32[16,16,128]{2,1,0:T(8,128)} %fold.1), calls=%async_computation.3 | async-start | bytes 262144 | tf_op jit(solution)/shard_map/all_to_all | solution.py:304

commit v5 on v4

--- a/solution.py
+++ b/solution.py
@@ -22,8 +22,10 @@
     chunks = blocks // step
     row, column = place_ref[0] // side, place_ref[0] % side
 
+    cuts = [0, 1, 2] + list(range(side, sections + 1, side))
+
     def leaving(group):
-        span = pl.ds(group * side, side)
+        span = pl.ds(cuts[group], cuts[group + 1] - cuts[group])
         return pltpu.make_async_copy(grad_ref.at[span], out_ref.at[span], out_sem.at[group])
 
     for down in range(side):
@@ -81,9 +83,9 @@
             grad_ref[s - 1, span(k)] = new
             if s > 1:
                 inner = enter(s - 1, k, new.astype(jnp.float32), inner)
-        if (s - 1) % side == 0:
-            leaving((s - 1) // side).start()
-    for group in range(side):
+        if s - 1 in cuts:
+            leaving(cuts.index(s - 1)).start()
+    for group in range(len(cuts) - 1):
         leaving(group).wait()
 
 
@@ -118,7 +120,7 @@
             pltpu.VMEM(shape, jnp.bfloat16),
             pltpu.VMEM(shape[1:], jnp.float32),
             pltpu.VMEM((sections, SUBLANES, LANES), jnp.float32),
-            pltpu.SemaphoreType.DMA((side,)),
+            pltpu.SemaphoreType.DMA((side + 2,)),
         ],
         compiler_params=pltpu.CompilerParams(vmem_limit_bytes=16 * 1024 * 1024),
         name="chain_all",

time: 116 us -> 115 us (level)
  no operation moved by 1% of the time
where the time goes in v5:
time: 115 us
  starting transfers between devices  51 us (44%)
  waiting for transfers between devices  34.6 us (30%)
  other arithmetic  8.46 us (7%)
  Pallas kernels  8.21 us (7%)
  matrix products  6.16 us (5%)
  local copies, waits for them, and re-layouts  5.51 us (5%)
    ppermute x7, waiting for transfers between devices, around(): lax.ppermute(value, 'dp', [(i, (i + 2 * steps) % ranks) for i in range(ra...  15.2 us
    ppermute x7, starting transfers between devices, around(): lax.ppermute(value, 'dp', [(i, (i + 2 * steps) % ranks) for i in range(ra...  14.2 us
    ppermute x6, starting transfers between devices, moved(): return lax.ppermute(value, 'section', pairs)  9.44 us
    all_to_all x1, waiting for transfers between devices, shards(): recv = lax.all_to_all(to_tiles(resid_first), 'section', 0, 0)  8.51 us
    all_to_all x1, starting transfers between devices, shards(): raw = lax.all_to_all(raw, 'dp', 0, 0, axis_index_groups=same_core)  8.18 us
    all_to_all x1, starting transfers between devices, shards(): lax.all_to_all(grads, 'section', 0, 0)  6.43 us
    all_to_all x1, starting transfers between devices, shards(): recv = lax.all_to_all(to_tiles(resid_first), 'section', 0, 0)  6.21 us
    dot_general x1, matrix products, shards(): jnp.einsum('tf,rf->tr', hidden_acts[0], proj_in[0], preferred_element_typ...  6.16 us
  transfers between devices with their start and end apart: 18, of which 9 were waited for; matrix products, arithmetic and copies ran while one was open for 14% of the time, Pallas kernels for 0%

profile of v5, /device:TPU:1, one launch (start us, length us, event | category | flops | bytes accessed | tf_op | source)
XLA Modules:
  0.0 114.8 jit_solution(11291361887977945298)
XLA Ops:
  0.6 0.0 copy-start
  0.6 3.4 %collective-permute-start.2 = (f32[64,128]{1,0:T(8,128)}, f32[64,128]{1,0:T(8,128)S(1)}, u32[]{:S(2)}, u32[]{:S(2)}) collective-permute-start(f32[64,128]{1,0:T(8,128)} %bitcast.50), channel_id=1, source_target_pairs={{0,48},{16,0},{32,16},{48,32},{64,112},{80,64},{96,80},{112,96},{1... | collective-permute-start | bytes 98312 | tf_op jit(solution)/shard_map/ppermute | solution.py:242
  4.0 0.5 collective-permute-start.1
  4.6 0.6 collective-permute-start
  5.2 6.2 %all-to-all-start = ((bf16[16,32,16,128]{3,2,1,0:T(8,128)(2,1)}), bf16[16,32,16,128]{3,2,1,0:T(8,128)(2,1)S(1)}, u32[]{:S(2)}, u32[]{:S(2)}) async-start(bf16[16,32,16,128]{3,2,1,0:T(8,128)(2,1)} %bitcast.49), calls=%async_computation | async-start | bytes 4194304 | tf_op jit(solution)/shard_map/all_to_all | solution.py:269
  11.4 0.6 gather_fusion
  12.1 1.0 dynamic-slice_select_fusion
  13.1 0.0 collective-permute-done
  13.2 1.7 %collective-permute-start.3 = (bf16[32,4096]{1,0:T(8,128)(2,1)S(1)}, bf16[32,4096]{1,0:T(8,128)(2,1)S(1)}, u32[]{:S(2)}, u32[]{:S(2)}) collective-permute-start(bf16[32,4096]{1,0:T(8,128)(2,1)S(1)} %bitcast.56), channel_id=1, source_target_pairs={{0,2},{1,3},{2,4},{3,5},{4,6},{5,7},{6,8},{7,9},{8,10},{9,11},{10,... | collective-permute-start | bytes 786440 | tf_op jit(solution)/shard_map/ppermute | solution.py:258
  14.9 4.0 %collective-permute-start.4 = (bf16[32,4096]{1,0:T(8,128)(2,1)S(1)}, bf16[32,4096]{1,0:T(8,128)(2,1)S(1)}, u32[]{:S(2)}, u32[]{:S(2)}) collective-permute-start(bf16[32,4096]{1,0:T(8,128)(2,1)S(1)} %bitcast.57), channel_id=1, source_target_pairs={{0,14},{1,15},{2,0},{3,1},{4,2},{5,3},{6,4},{7,5},{8,6},{9,7},{10,... | collective-permute-start | bytes 786440 | tf_op jit(solution)/shard_map/ppermute | solution.py:258
  18.9 1.4 %collective-permute-start.5 = (f32[4,64,128]{2,1,0:T(8,128)S(1)}, f32[4,64,128]{2,1,0:T(8,128)S(1)}, u32[]{:S(2)}, u32[]{:S(2)}) collective-permute-start(f32[4,64,128]{2,1,0:T(8,128)S(1)} %pad_maximum_fusion.refs_0_), channel_id=1, source_target_pairs={{0,64},{16,80},{32,96},{48,112},{64,128},{80,144},{96,160},{112,17... | collective-permute-start | bytes 393224 | tf_op jit(solution)/shard_map/ppermute | solution.py:242
  20.3 2.4 %collective-permute-start.6 = (f32[4,64,128]{2,1,0:T(8,128)S(1)}, f32[4,64,128]{2,1,0:T(8,128)S(1)}, u32[]{:S(2)}, u32[]{:S(2)}) collective-permute-start(f32[4,64,128]{2,1,0:T(8,128)S(1)} %pad_maximum_fusion.refs_0_), channel_id=1, source_target_pairs={{0,128},{16,144},{32,160},{48,176},{64,192},{80,208},{96,224},{112... | collective-permute-start | bytes 393224 | tf_op jit(solution)/shard_map/ppermute | solution.py:242
  22.7 1.2 %collective-permute-start.7 = (f32[4,64,128]{2,1,0:T(8,128)S(1)}, f32[4,64,128]{2,1,0:T(8,128)S(1)}, u32[]{:S(2)}, u32[]{:S(2)}) collective-permute-start(f32[4,64,128]{2,1,0:T(8,128)S(1)} %pad_maximum_fusion.refs_0_), channel_id=1, source_target_pairs={{0,192},{16,208},{32,224},{48,240},{64,0},{80,16},{96,32},{112,48}... | collective-permute-start | bytes 393224 | tf_op jit(solution)/shard_map/ppermute | solution.py:242
  23.9 6.2 %fusion.10.side_in_ref = bf16[128,64]{1,0:T(8,128)(2,1)S(1)} fusion(bf16[1,64,28672]{2,1,0:T(8,128)(2,1)} %param.13, bf16[1,128,28672]{2,1,0:T(8,128)(2,1)} %param.8), kind=kOutput, calls=%fused_computation.16 | convolution fusion | flops 469770240 | bytes 11026432 | tf_op jit(solution)/shard_map/tf,rf->tr/dot_general | solution.py:251
  30.0 0.0 collective-permute-done.3
  30.0 0.7 copy-done.8
  30.7 0.0 collective-permute-done.4
  30.8 8.5 %all-to-all-done.recv_ref = bf16[16,32,16,128]{3,2,1,0:T(8,128)(2,1)S(1)} async-done(((bf16[16,32,16,128]{3,2,1,0:T(8,128)(2,1)}), bf16[16,32,16,128]{3,2,1,0:T(8,128)(2,1)S(1)}, u32[]{:S(2)}, u32[]{:S(2)}) %all-to-all-start) | async-done | bytes 2097184 | tf_op jit(solution)/shard_map/all_to_all | solution.py:269
  39.3 1.2 %collective-permute-done.5.refs_1_ = f32[4,64,128]{2,1,0:T(8,128)S(1)} collective-permute-done((f32[4,64,128]{2,1,0:T(8,128)S(1)}, f32[4,64,128]{2,1,0:T(8,128)S(1)}, u32[]{:S(2)}, u32[]{:S(2)}) %collective-permute-start.5) | collective-permute-done | bytes 131104 | tf_op jit(solution)/shard_map/ppermute | solution.py:242
  40.4 0.8 collective-permute-done.6.refs_2_
  41.3 4.4 %chain_all.1 = bf16[16,32,16,128]{3,2,1,0:T(8,128)(2,1)} custom-call(s32[1]{0:T(128)} %bitcast.place_ref, bf16[16,32,16,128]{3,2,1,0:T(8,128)(2,1)S(1)} %all-to-all-done.recv_ref, bf16[32,16,128]{2,1,0:T(8,128)(2,1)S(1)} %bitcast.48, f32[4,64,128]{2,1,0:T(8,128)S(1)} %pad_maximum_fusion.refs_0_, f32[4,64,128]{2,1,0:T(8,128)S(1)} %collective-permute-done.5.refs_1_, ...), custom_call_target="tpu_custom_call" | custom-call | tf_op jit(solution)/shard_map/chain_all/pallas_call | solution.py:113
  45.7 6.4 %all-to-all-start.1 = ((bf16[16,32,16,128]{3,2,1,0:T(8,128)(2,1)}), bf16[16,32,16,128]{3,2,1,0:T(8,128)(2,1)S(1)}, u32[]{:S(2)}, u32[]{:S(2)}) async-start(bf16[16,32,16,128]{3,2,1,0:T(8,128)(2,1)} %chain_all.1), calls=%async_computation.1 | async-start | bytes 4194304 | tf_op jit(solution)/shard_map/all_to_all | solution.py:279
  52.1 0.0 copy-start.3
  52.2 1.7 %collective-permute-start.8 = (bf16[32,4096]{1,0:T(8,128)(2,1)}, bf16[32,4096]{1,0:T(8,128)(2,1)S(1)}, u32[]{:S(2)}, u32[]{:S(2)}) collective-permute-start(bf16[32,4096]{1,0:T(8,128)(2,1)} %copy-done.8), channel_id=1, source_target_pairs={{0,2},{1,3},{2,4},{3,5},{4,6},{5,7},{6,8},{7,9},{8,10},{9,11},{10,... | collective-permute-start | bytes 786440 | tf_op jit(solution)/shard_map/ppermute | solution.py:258
  53.9 4.0 %collective-permute-start.11 = (bf16[32,4096]{1,0:T(8,128)(2,1)}, bf16[32,4096]{1,0:T(8,128)(2,1)S(1)}, u32[]{:S(2)}, u32[]{:S(2)}) collective-permute-start(bf16[32,4096]{1,0:T(8,128)(2,1)} %copy-done.6), channel_id=1, source_target_pairs={{0,14},{1,15},{2,0},{3,1},{4,2},{5,3},{6,4},{7,5},{8,6},{9,7},{10,... | collective-permute-start | bytes 786440 | tf_op jit(solution)/shard_map/ppermute | solution.py:258
  57.9 1.0 constant_dynamic-update-slice_fusion.6
  58.9 4.3 %collective-permute-done.8 = bf16[32,4096]{1,0:T(8,128)(2,1)S(1)} collective-permute-done((bf16[32,4096]{1,0:T(8,128)(2,1)}, bf16[32,4096]{1,0:T(8,128)(2,1)S(1)}, u32[]{:S(2)}, u32[]{:S(2)}) %collective-permute-start.8) | collective-permute-done | bytes 262176 | tf_op jit(solution)/shard_map/ppermute | solution.py:258
  63.2 0.0 collective-permute-start.9
  63.2 0.0 collective-permute-done.11
  63.2 2.7 %collective-permute-start.12 = (bf16[32,4096]{1,0:T(8,128)(2,1)S(1)}, bf16[32,4096]{1,0:T(8,128)(2,1)S(1)}, u32[]{:S(2)}, u32[]{:S(2)}) collective-permute-start(bf16[32,4096]{1,0:T(8,128)(2,1)S(1)} %collective-permute-done.11), channel_id=1, source_target_pairs={{0,14},{1,15},{2,0},{3,1},{4,2},{5,3},{6,4},{7,5},{8,6},{9,7},{10,... | collective-permute-start | bytes 786440 | tf_op jit(solution)/shard_map/ppermute | solution.py:258
  65.9 4.2 %collective-permute-done.9 = bf16[32,4096]{1,0:T(8,128)(2,1)S(1)} collective-permute-done((bf16[32,4096]{1,0:T(8,128)(2,1)S(1)}, bf16[32,4096]{1,0:T(8,128)(2,1)S(1)}, u32[]{:S(2)}, u32[]{:S(2)}) %collective-permute-start.9) | collective-permute-done | bytes 262176 | tf_op jit(solution)/shard_map/ppermute | solution.py:258
  70.1 6.7 %collective-permute-done.10 = bf16[32,4096]{1,0:T(8,128)(2,1)S(1)} collective-permute-done((bf16[32,4096]{1,0:T(8,128)(2,1)S(1)}, bf16[32,4096]{1,0:T(8,128)(2,1)S(1)}, u32[]{:S(2)}, u32[]{:S(2)}) %collective-permute-start.10) | collective-permute-done | bytes 262176 | tf_op jit(solution)/shard_map/ppermute | solution.py:258
  76.9 1.3 %copy-done.1 = bf16[256,4096]{1,0:T(8,128)(2,1)} copy-done((bf16[256,4096]{1,0:T(8,128)(2,1)}, bf16[256,4096]{1,0:T(8,128)(2,1)S(1)}, u32[]{:S(2)}) %copy-start.1) | copy-done | bytes 2097176
  78.3 2.8 %all-to-all-done.1 = bf16[16,32,16,128]{3,2,1,0:T(8,128)(2,1)S(1)} async-done(((bf16[16,32,16,128]{3,2,1,0:T(8,128)(2,1)}), bf16[16,32,16,128]{3,2,1,0:T(8,128)(2,1)S(1)}, u32[]{:S(2)}, u32[]{:S(2)}) %all-to-all-start.1) | async-done | bytes 2097184 | tf_op jit(solution)/shard_map/all_to_all | solution.py:279
  81.0 0.9 front.1
  81.9 0.1 reshape.137
  82.0 3.0 %collective-permute-start.13 = (bf16[2,4096]{1,0:T(2,128)(2,1)S(1)}, bf16[2,4096]{1,0:T(2,128)(2,1)S(1)}, u32[]{:S(2)}, u32[]{:S(2)}) collective-permute-start(bf16[2,4096]{1,0:T(2,128)(2,1)S(1)} %reshape.137), channel_id=1, source_target_pairs={{0,1},{1,0},{2,3},{3,2},{4,5},{5,4},{6,7},{7,6},{8,9},{9,8},{10,11... | collective-permute-start | bytes 49160 | tf_op jit(solution)/shard_map/ppermute | solution.py:289
  85.0 1.6 %copy-done.2 = bf16[256,4096]{1,0:T(8,128)(2,1)S(1)} copy-done((bf16[256,4096]{1,0:T(8,128)(2,1)S(1)}, bf16[256,4096]{1,0:T(8,128)(2,1)}, u32[]{:S(2)}) %copy-start.2) | copy-done | bytes 2097176
  86.6 0.1 stage.1.queries_ref
  86.9 1.3 %raw.1 = f32[8,4,128]{2,1,0:T(4,128)} custom-call(s32[1]{0:T(128)} %bitcast.19.place_ref, bf16[4,4096]{1,0:T(4,128)(2,1)S(1)} %pad_maximum_fusion.1.grads_ref, bf16[256,4096]{1,0:T(8,128)(2,1)S(1)} %stage.1.queries_ref), custom_call_target="tpu_custom_call" | custom-call | tf_op jit(solution)/shard_map/raw/pallas_call | solution.py:96
  88.2 8.2 %all-to-all-start.2 = ((f32[8,4,128]{2,1,0:T(4,128)}), f32[8,4,128]{2,1,0:T(4,128)S(1)}, u32[]{:S(2)}, u32[]{:S(2)}) async-start(f32[8,4,128]{2,1,0:T(4,128)} %raw.1), calls=%async_computation.2 | async-start | bytes 32768 | tf_op jit(solution)/shard_map/all_to_all | solution.py:300
  96.4 2.7 %fusion.5 = (f32[128]{0:T(128)S(1)}, f32[128]{0:T(128)S(1)}) fusion(bf16[1,128,8192]{2,1,0:T(8,128)(2,1)} %param.9, f32[8192]{0:T(1024)S(1)} %bitcast.54, bf16[128,8192]{1,0:T(8,128)(2,1)S(1)} %bitcast.45), kind=kLoop, calls=%fused_computation.11 | loop fusion | flops 7339776 | bytes 4228096 | tf_op jit(solution)/shard_map/reduce_sum | solution.py:216
  99.1 3.9 %all-to-all-done.2.parts_ref = f32[8,4,128]{2,1,0:T(4,128)S(1)} async-done(((f32[8,4,128]{2,1,0:T(4,128)}), f32[8,4,128]{2,1,0:T(4,128)S(1)}, u32[]{:S(2)}, u32[]{:S(2)}) %all-to-all-start.2) | async-done | bytes 16416 | tf_op jit(solution)/shard_map/all_to_all | solution.py:300
  103.0 0.7 fold.1
  103.8 3.5 %all-to-all-start.3 = ((f32[16,16,128]{2,1,0:T(8,128)}), f32[16,16,128]{2,1,0:T(8,128)S(1)}, u32[]{:S(2)}, u32[]{:S(2)}) async-start(f32[16,16,128]{2,1,0:T(8,128)} %fold.1), calls=%async_computation.3 | async-start | bytes 262144 | tf_op jit(solution)/shard_map/all_to_all | solution.py:306
  107.3 4.6 %fusion.9 = bf16[1,128,8192]{2,1,0:T(8,128)(2,1)} fusion(bf16[128,8192]{1,0:T(8,128)(2,1)S(1)} %bitcast.46, bf16[1,128,8192]{2,1,0:T(8,128)(2,1)} %param.9, f32[128]{0:T(128)S(1)} %broadcast_multiply_fusion, f32[128]{0:T(128)S(1)} %get-tuple-element.33, f32[8192]{0:T(1024)S(1)} %bitcast.55, f32[128]{0:T(128)S(1)} %get-tuple-element.32), kind=kLoop, calls=%fused_computation.15 | loop fusion | flops 9437184 | bytes 6325760 | tf_op jit(solution)/shard_map/broadcast_in_dim | solution.py:312
  111.9 2.2 %all-to-all-done.3.parts_ref = f32[16,16,128]{2,1,0:T(8,128)S(1)} async-done(((f32[16,16,128]{2,1,0:T(8,128)}), f32[16,16,128]{2,1,0:T(8,128)S(1)}, u32[]{:S(2)}, u32[]{:S(2)}) %all-to-all-start.3) | async-done | bytes 131104 | tf_op jit(solution)/shard_map/all_to_all | solution.py:306
  114.1 0.7 scores.1
  (34 shorter events, 0.3 us)
Async XLA Ops:
  0.6 10.8 %copy-start = (s32[2]{0:T(128)S(1)}, s32[2]{0:T(128)}, u32[]{:S(2)}) copy-start(s32[2]{0:T(128)} %param.12) | copy-start | bytes 28
  0.6 12.5 %collective-permute-start.2 = (f32[64,128]{1,0:T(8,128)}, f32[64,128]{1,0:T(8,128)S(1)}, u32[]{:S(2)}, u32[]{:S(2)}) collective-permute-start(f32[64,128]{1,0:T(8,128)} %bitcast.50), channel_id=1, source_target_pairs={{0,48},{16,0},{32,16},{48,32},{64,112},{80,64},{96,80},{112,96},{1... | collective-permute-start | bytes 98312 | tf_op jit(solution)/shard_map/ppermute | solution.py:242
  4.0 9.1 %collective-permute-start.1 = (f32[64,128]{1,0:T(8,128)}, f32[64,128]{1,0:T(8,128)S(1)}, u32[]{:S(2)}, u32[]{:S(2)}) collective-permute-start(f32[64,128]{1,0:T(8,128)} %bitcast.51), channel_id=1, source_target_pairs={{0,32},{16,48},{32,0},{48,16},{64,96},{80,112},{96,64},{112,80},{1... | collective-permute-start | bytes 98312 | tf_op jit(solution)/shard_map/ppermute | solution.py:242
  4.6 8.6 %collective-permute-start = (f32[64,128]{1,0:T(8,128)}, f32[64,128]{1,0:T(8,128)S(1)}, u32[]{:S(2)}, u32[]{:S(2)}) collective-permute-start(f32[64,128]{1,0:T(8,128)} %bitcast.52), channel_id=1, source_target_pairs={{0,16},{16,32},{32,48},{48,0},{64,80},{80,96},{96,112},{112,64},{1... | collective-permute-start | bytes 98312 | tf_op jit(solution)/shard_map/ppermute | solution.py:242
  5.2 8.0 %copy-start.4 = (f32[1,8192]{1,0:T(1,128)S(1)}, f32[1,8192]{1,0:T(1,128)}, u32[]{:S(2)}) copy-start(f32[1,8192]{1,0:T(1,128)} %param.10) | copy-start | bytes 98308
  5.2 8.0 %copy-start.5 = (bf16[1,32,4096]{2,1,0:T(8,128)(2,1)S(1)}, bf16[1,32,4096]{2,1,0:T(8,128)(2,1)}, u32[]{:S(2)}) copy-start(bf16[1,32,4096]{2,1,0:T(8,128)(2,1)} %param.15) | copy-start | bytes 786436
  5.2 34.1 %all-to-all-start = ((bf16[16,32,16,128]{3,2,1,0:T(8,128)(2,1)}), bf16[16,32,16,128]{3,2,1,0:T(8,128)(2,1)S(1)}, u32[]{:S(2)}, u32[]{:S(2)}) async-start(bf16[16,32,16,128]{3,2,1,0:T(8,128)(2,1)} %bitcast.49), calls=%async_computation | async-start | bytes 4194304 | tf_op jit(solution)/shard_map/all_to_all | solution.py:269
  13.2 16.8 %collective-permute-start.3 = (bf16[32,4096]{1,0:T(8,128)(2,1)S(1)}, bf16[32,4096]{1,0:T(8,128)(2,1)S(1)}, u32[]{:S(2)}, u32[]{:S(2)}) collective-permute-start(bf16[32,4096]{1,0:T(8,128)(2,1)S(1)} %bitcast.56), channel_id=1, source_target_pairs={{0,2},{1,3},{2,4},{3,5},{4,6},{5,7},{6,8},{7,9},{8,10},{9,11},{10,... | collective-permute-start | bytes 786440 | tf_op jit(solution)/shard_map/ppermute | solution.py:258
  14.9 15.9 %collective-permute-start.4 = (bf16[32,4096]{1,0:T(8,128)(2,1)S(1)}, bf16[32,4096]{1,0:T(8,128)(2,1)S(1)}, u32[]{:S(2)}, u32[]{:S(2)}) collective-permute-start(bf16[32,4096]{1,0:T(8,128)(2,1)S(1)} %bitcast.57), channel_id=1, source_target_pairs={{0,14},{1,15},{2,0},{3,1},{4,2},{5,3},{6,4},{7,5},{8,6},{9,7},{10,... | collective-permute-start | bytes 786440 | tf_op jit(solution)/shard_map/ppermute | solution.py:258
  18.9 21.5 %collective-permute-start.5 = (f32[4,64,128]{2,1,0:T(8,128)S(1)}, f32[4,64,128]{2,1,0:T(8,128)S(1)}, u32[]{:S(2)}, u32[]{:S(2)}) collective-permute-start(f32[4,64,128]{2,1,0:T(8,128)S(1)} %pad_maximum_fusion.refs_0_), channel_id=1, source_target_pairs={{0,64},{16,80},{32,96},{48,112},{64,128},{80,144},{96,160},{112,17... | collective-permute-start | bytes 393224 | tf_op jit(solution)/shard_map/ppermute | solution.py:242
  20.3 21.0 %collective-permute-start.6 = (f32[4,64,128]{2,1,0:T(8,128)S(1)}, f32[4,64,128]{2,1,0:T(8,128)S(1)}, u32[]{:S(2)}, u32[]{:S(2)}) collective-permute-start(f32[4,64,128]{2,1,0:T(8,128)S(1)} %pad_maximum_fusion.refs_0_), channel_id=1, source_target_pairs={{0,128},{16,144},{32,160},{48,176},{64,192},{80,208},{96,224},{112... | collective-permute-start | bytes 393224 | tf_op jit(solution)/shard_map/ppermute | solution.py:242
  22.7 18.6 %collective-permute-start.7 = (f32[4,64,128]{2,1,0:T(8,128)S(1)}, f32[4,64,128]{2,1,0:T(8,128)S(1)}, u32[]{:S(2)}, u32[]{:S(2)}) collective-permute-start(f32[4,64,128]{2,1,0:T(8,128)S(1)} %pad_maximum_fusion.refs_0_), channel_id=1, source_target_pairs={{0,192},{16,208},{32,224},{48,240},{64,0},{80,16},{96,32},{112,48}... | collective-permute-start | bytes 393224 | tf_op jit(solution)/shard_map/ppermute | solution.py:242
  30.0 0.7 copy-start.8
  30.8 14.9 %copy-start.6 = (bf16[32,4096]{1,0:T(8,128)(2,1)}, bf16[32,4096]{1,0:T(8,128)(2,1)S(1)}, u32[]{:S(2)}) copy-start(bf16[32,4096]{1,0:T(8,128)(2,1)S(1)} %collective-permute-done.4) | copy-start | bytes 786436
  45.7 35.3 %all-to-all-start.1 = ((bf16[16,32,16,128]{3,2,1,0:T(8,128)(2,1)}), bf16[16,32,16,128]{3,2,1,0:T(8,128)(2,1)S(1)}, u32[]{:S(2)}, u32[]{:S(2)}) async-start(bf16[16,32,16,128]{3,2,1,0:T(8,128)(2,1)} %chain_all.1), calls=%async_computation.1 | async-start | bytes 4194304 | tf_op jit(solution)/shard_map/all_to_all | solution.py:279
  52.1 24.8 %copy-start.7 = (bf16[32,4096]{1,0:T(8,128)(2,1)S(1)}, bf16[32,4096]{1,0:T(8,128)(2,1)}, u32[]{:S(2)}) copy-start(bf16[32,4096]{1,0:T(8,128)(2,1)} %copy-done.6) | copy-start | bytes 786436
  52.1 28.9 %copy-start.3 = (bf16[1,64,8192]{2,1,0:T(8,128)(2,1)S(1)}, bf16[1,64,8192]{2,1,0:T(8,128)(2,1)}, u32[]{:S(2)}) copy-start(bf16[1,64,8192]{2,1,0:T(8,128)(2,1)} %param.14) | copy-start | bytes 3145732
  52.2 11.0 %collective-permute-start.8 = (bf16[32,4096]{1,0:T(8,128)(2,1)}, bf16[32,4096]{1,0:T(8,128)(2,1)S(1)}, u32[]{:S(2)}, u32[]{:S(2)}) collective-permute-start(bf16[32,4096]{1,0:T(8,128)(2,1)} %copy-done.8), channel_id=1, source_target_pairs={{0,2},{1,3},{2,4},{3,5},{4,6},{5,7},{6,8},{7,9},{8,10},{9,11},{10,... | collective-permute-start | bytes 786440 | tf_op jit(solution)/shard_map/ppermute | solution.py:258
  53.9 9.3 %collective-permute-start.11 = (bf16[32,4096]{1,0:T(8,128)(2,1)}, bf16[32,4096]{1,0:T(8,128)(2,1)S(1)}, u32[]{:S(2)}, u32[]{:S(2)}) collective-permute-start(bf16[32,4096]{1,0:T(8,128)(2,1)} %copy-done.6), channel_id=1, source_target_pairs={{0,14},{1,15},{2,0},{3,1},{4,2},{5,3},{6,4},{7,5},{8,6},{9,7},{10,... | collective-permute-start | bytes 786440 | tf_op jit(solution)/shard_map/ppermute | solution.py:258
  63.2 6.9 %collective-permute-start.9 = (bf16[32,4096]{1,0:T(8,128)(2,1)S(1)}, bf16[32,4096]{1,0:T(8,128)(2,1)S(1)}, u32[]{:S(2)}, u32[]{:S(2)}) collective-permute-start(bf16[32,4096]{1,0:T(8,128)(2,1)S(1)} %collective-permute-done.8), channel_id=1, source_target_pairs={{0,2},{1,3},{2,4},{3,5},{4,6},{5,7},{6,8},{7,9},{8,10},{9,11},{10,... | collective-permute-start | bytes 786440 | tf_op jit(solution)/shard_map/ppermute | solution.py:258
  63.2 13.6 %collective-permute-start.12 = (bf16[32,4096]{1,0:T(8,128)(2,1)S(1)}, bf16[32,4096]{1,0:T(8,128)(2,1)S(1)}, u32[]{:S(2)}, u32[]{:S(2)}) collective-permute-start(bf16[32,4096]{1,0:T(8,128)(2,1)S(1)} %collective-permute-done.11), channel_id=1, source_target_pairs={{0,14},{1,15},{2,0},{3,1},{4,2},{5,3},{6,4},{7,5},{8,6},{9,7},{10,... | collective-permute-start | bytes 786440 | tf_op jit(solution)/shard_map/ppermute | solution.py:258
  70.1 6.7 %collective-permute-start.10 = (bf16[32,4096]{1,0:T(8,128)(2,1)S(1)}, bf16[32,4096]{1,0:T(8,128)(2,1)S(1)}, u32[]{:S(2)}, u32[]{:S(2)}) collective-permute-start(bf16[32,4096]{1,0:T(8,128)(2,1)S(1)} %collective-permute-done.9), channel_id=1, source_target_pairs={{0,2},{1,3},{2,4},{3,5},{4,6},{5,7},{6,8},{7,9},{8,10},{9,11},{10,... | collective-permute-start | bytes 786440 | tf_op jit(solution)/shard_map/ppermute | solution.py:258
  76.9 1.3 %copy-start.1 = (bf16[256,4096]{1,0:T(8,128)(2,1)}, bf16[256,4096]{1,0:T(8,128)(2,1)S(1)}, u32[]{:S(2)}) copy-start(bf16[256,4096]{1,0:T(8,128)(2,1)S(1)} %constant_dynamic-update-slice_fusion.queries_ref) | copy-start | bytes 6291460
  82.0 4.8 %collective-permute-start.13 = (bf16[2,4096]{1,0:T(2,128)(2,1)S(1)}, bf16[2,4096]{1,0:T(2,128)(2,1)S(1)}, u32[]{:S(2)}, u32[]{:S(2)}) collective-permute-start(bf16[2,4096]{1,0:T(2,128)(2,1)S(1)} %reshape.137), channel_id=1, source_target_pairs={{0,1},{1,0},{2,3},{3,2},{4,5},{5,4},{6,7},{7,6},{8,9},{9,8},{10,11... | collective-permute-start | bytes 49160 | tf_op jit(solution)/shard_map/ppermute | solution.py:289
  85.0 1.6 %copy-start.2 = (bf16[256,4096]{1,0:T(8,128)(2,1)S(1)}, bf16[256,4096]{1,0:T(8,128)(2,1)}, u32[]{:S(2)}) copy-start(bf16[256,4096]{1,0:T(8,128)(2,1)} %copy-done.1) | copy-start | bytes 6291460
  88.2 14.8 %all-to-all-start.2 = ((f32[8,4,128]{2,1,0:T(4,128)}), f32[8,4,128]{2,1,0:T(4,128)S(1)}, u32[]{:S(2)}, u32[]{:S(2)}) async-start(f32[8,4,128]{2,1,0:T(4,128)} %raw.1), calls=%async_computation.2 | async-start | bytes 32768 | tf_op jit(solution)/shard_map/all_to_all | solution.py:300
  103.8 10.3 %all-to-all-start.3 = ((f32[16,16,128]{2,1,0:T(8,128)}), f32[16,16,128]{2,1,0:T(8,128)S(1)}, u32[]{:S(2)}, u32[]{:S(2)}) async-start(f32[16,16,128]{2,1,0:T(8,128)} %fold.1), calls=%async_computation.3 | async-start | bytes 262144 | tf_op jit(solution)/shard_map/all_to_all | solution.py:306

commit v6 on v5

--- a/solution.py
+++ b/solution.py
@@ -54,8 +54,13 @@
     def mean(v):
         v = jnp.sum(v, axis=0)
         v = v[:8] + v[8:]
-        v = jnp.sum(v, axis=-1, keepdims=True) / width
-        return jnp.broadcast_to(jnp.concatenate([v, v], axis=0), (SUBLANES, LANES))
+        parts = []
+        for _ in range(3):
+            parts.append(v.astype(jnp.bfloat16))
+            v = v - parts[-1].astype(jnp.float32)
+        ones = jnp.ones((3 * LANES, LANES), jnp.bfloat16)
+        v = jnp.dot(jnp.concatenate(parts, axis=1), ones, preferred_element_type=jnp.float32) / width
+        return jnp.concatenate([v, v], axis=0)
 
     zero = jnp.zeros((step, SUBLANES, LANES), jnp.float32)
     for s in range(sections - 1, 0, -1):

time: 115 us -> 115 us (level)
  no operation moved by 1% of the time
where the time goes in v6:
time: 115 us
  starting transfers between devices  51 us (44%)
  waiting for transfers between devices  34.6 us (30%)
  other arithmetic  8.46 us (7%)
  Pallas kernels  8.07 us (7%)
  matrix products  6.16 us (5%)
  local copies, waits for them, and re-layouts  5.51 us (5%)
    ppermute x7, waiting for transfers between devices, around(): lax.ppermute(value, 'dp', [(i, (i + 2 * steps) % ranks) for i in range(ra...  15.2 us
    ppermute x7, starting transfers between devices, around(): lax.ppermute(value, 'dp', [(i, (i + 2 * steps) % ranks) for i in range(ra...  14.2 us
    ppermute x6, starting transfers between devices, moved(): return lax.ppermute(value, 'section', pairs)  9.44 us
    all_to_all x1, waiting for transfers between devices, shards(): recv = lax.all_to_all(to_tiles(resid_first), 'section', 0, 0)  8.51 us
    all_to_all x1, starting transfers between devices, shards(): raw = lax.all_to_all(raw, 'dp', 0, 0, axis_index_groups=same_core)  8.18 us
    all_to_all x1, starting transfers between devices, shards(): lax.all_to_all(grads, 'section', 0, 0)  6.43 us
    all_to_all x1, starting transfers between devices, shards(): recv = lax.all_to_all(to_tiles(resid_first), 'section', 0, 0)  6.21 us
    dot_general x1, matrix products, shards(): jnp.einsum('tf,rf->tr', hidden_acts[0], proj_in[0], preferred_element_typ...  6.16 us
  transfers between devices with their start and end apart: 18, of which 9 were waited for; matrix products, arithmetic and copies ran while one was open for 14% of the time, Pallas kernels for 0%

profile of v6, /device:TPU:1, one launch (start us, length us, event | category | flops | bytes accessed | tf_op | source)
XLA Modules:
  0.0 114.7 jit_solution(5075306315796907236)
XLA Ops:
  0.6 0.0 copy-start
  0.6 3.4 %collective-permute-start.2 = (f32[64,128]{1,0:T(8,128)}, f32[64,128]{1,0:T(8,128)S(1)}, u32[]{:S(2)}, u32[]{:S(2)}) collective-permute-start(f32[64,128]{1,0:T(8,128)} %bitcast.50), channel_id=1, source_target_pairs={{0,48},{16,0},{32,16},{48,32},{64,112},{80,64},{96,80},{112,96},{1... | collective-permute-start | bytes 98312 | tf_op jit(solution)/shard_map/ppermute | solution.py:247
  4.0 0.5 collective-permute-start.1
  4.6 0.6 collective-permute-start
  5.2 6.2 %all-to-all-start = ((bf16[16,32,16,128]{3,2,1,0:T(8,128)(2,1)}), bf16[16,32,16,128]{3,2,1,0:T(8,128)(2,1)S(1)}, u32[]{:S(2)}, u32[]{:S(2)}) async-start(bf16[16,32,16,128]{3,2,1,0:T(8,128)(2,1)} %bitcast.49), calls=%async_computation | async-start | bytes 4194304 | tf_op jit(solution)/shard_map/all_to_all | solution.py:274
  11.4 0.6 gather_fusion
  12.1 1.0 dynamic-slice_select_fusion
  13.1 0.0 collective-permute-done
  13.2 1.7 %collective-permute-start.3 = (bf16[32,4096]{1,0:T(8,128)(2,1)S(1)}, bf16[32,4096]{1,0:T(8,128)(2,1)S(1)}, u32[]{:S(2)}, u32[]{:S(2)}) collective-permute-start(bf16[32,4096]{1,0:T(8,128)(2,1)S(1)} %bitcast.56), channel_id=1, source_target_pairs={{0,2},{1,3},{2,4},{3,5},{4,6},{5,7},{6,8},{7,9},{8,10},{9,11},{10,... | collective-permute-start | bytes 786440 | tf_op jit(solution)/shard_map/ppermute | solution.py:263
  14.9 4.0 %collective-permute-start.4 = (bf16[32,4096]{1,0:T(8,128)(2,1)S(1)}, bf16[32,4096]{1,0:T(8,128)(2,1)S(1)}, u32[]{:S(2)}, u32[]{:S(2)}) collective-permute-start(bf16[32,4096]{1,0:T(8,128)(2,1)S(1)} %bitcast.57), channel_id=1, source_target_pairs={{0,14},{1,15},{2,0},{3,1},{4,2},{5,3},{6,4},{7,5},{8,6},{9,7},{10,... | collective-permute-start | bytes 786440 | tf_op jit(solution)/shard_map/ppermute | solution.py:263
  18.9 1.4 %collective-permute-start.5 = (f32[4,64,128]{2,1,0:T(8,128)S(1)}, f32[4,64,128]{2,1,0:T(8,128)S(1)}, u32[]{:S(2)}, u32[]{:S(2)}) collective-permute-start(f32[4,64,128]{2,1,0:T(8,128)S(1)} %pad_maximum_fusion.refs_0_), channel_id=1, source_target_pairs={{0,64},{16,80},{32,96},{48,112},{64,128},{80,144},{96,160},{112,17... | collective-permute-start | bytes 393224 | tf_op jit(solution)/shard_map/ppermute | solution.py:247
  20.3 2.4 %collective-permute-start.6 = (f32[4,64,128]{2,1,0:T(8,128)S(1)}, f32[4,64,128]{2,1,0:T(8,128)S(1)}, u32[]{:S(2)}, u32[]{:S(2)}) collective-permute-start(f32[4,64,128]{2,1,0:T(8,128)S(1)} %pad_maximum_fusion.refs_0_), channel_id=1, source_target_pairs={{0,128},{16,144},{32,160},{48,176},{64,192},{80,208},{96,224},{112... | collective-permute-start | bytes 393224 | tf_op jit(solution)/shard_map/ppermute | solution.py:247
  22.7 1.2 %collective-permute-start.7 = (f32[4,64,128]{2,1,0:T(8,128)S(1)}, f32[4,64,128]{2,1,0:T(8,128)S(1)}, u32[]{:S(2)}, u32[]{:S(2)}) collective-permute-start(f32[4,64,128]{2,1,0:T(8,128)S(1)} %pad_maximum_fusion.refs_0_), channel_id=1, source_target_pairs={{0,192},{16,208},{32,224},{48,240},{64,0},{80,16},{96,32},{112,48}... | collective-permute-start | bytes 393224 | tf_op jit(solution)/shard_map/ppermute | solution.py:247
  23.9 6.2 %fusion.10.side_in_ref = bf16[128,64]{1,0:T(8,128)(2,1)S(1)} fusion(bf16[1,64,28672]{2,1,0:T(8,128)(2,1)} %param.13, bf16[1,128,28672]{2,1,0:T(8,128)(2,1)} %param.8), kind=kOutput, calls=%fused_computation.16 | convolution fusion | flops 469770240 | bytes 11026432 | tf_op jit(solution)/shard_map/tf,rf->tr/dot_general | solution.py:256
  30.0 0.0 collective-permute-done.3
  30.0 0.7 copy-done.8
  30.7 0.0 collective-permute-done.4
  30.8 8.5 %all-to-all-done.recv_ref = bf16[16,32,16,128]{3,2,1,0:T(8,128)(2,1)S(1)} async-done(((bf16[16,32,16,128]{3,2,1,0:T(8,128)(2,1)}), bf16[16,32,16,128]{3,2,1,0:T(8,128)(2,1)S(1)}, u32[]{:S(2)}, u32[]{:S(2)}) %all-to-all-start) | async-done | bytes 2097184 | tf_op jit(solution)/shard_map/all_to_all | solution.py:274
  39.3 1.2 %collective-permute-done.5.refs_1_ = f32[4,64,128]{2,1,0:T(8,128)S(1)} collective-permute-done((f32[4,64,128]{2,1,0:T(8,128)S(1)}, f32[4,64,128]{2,1,0:T(8,128)S(1)}, u32[]{:S(2)}, u32[]{:S(2)}) %collective-permute-start.5) | collective-permute-done | bytes 131104 | tf_op jit(solution)/shard_map/ppermute | solution.py:247
  40.4 0.8 collective-permute-done.6.refs_2_
  41.3 4.3 %chain_all.1 = bf16[16,32,16,128]{3,2,1,0:T(8,128)(2,1)} custom-call(s32[1]{0:T(128)} %bitcast.place_ref, bf16[16,32,16,128]{3,2,1,0:T(8,128)(2,1)S(1)} %all-to-all-done.recv_ref, bf16[32,16,128]{2,1,0:T(8,128)(2,1)S(1)} %bitcast.48, f32[4,64,128]{2,1,0:T(8,128)S(1)} %pad_maximum_fusion.refs_0_, f32[4,64,128]{2,1,0:T(8,128)S(1)} %collective-permute-done.5.refs_1_, ...), custom_call_target="tpu_custom_call" | custom-call | tf_op jit(solution)/shard_map/chain_all/pallas_call | solution.py:118
  45.6 6.4 %all-to-all-start.1 = ((bf16[16,32,16,128]{3,2,1,0:T(8,128)(2,1)}), bf16[16,32,16,128]{3,2,1,0:T(8,128)(2,1)S(1)}, u32[]{:S(2)}, u32[]{:S(2)}) async-start(bf16[16,32,16,128]{3,2,1,0:T(8,128)(2,1)} %chain_all.1), calls=%async_computation.1 | async-start | bytes 4194304 | tf_op jit(solution)/shard_map/all_to_all | solution.py:284
  52.0 0.0 copy-start.3
  52.1 1.7 %collective-permute-start.8 = (bf16[32,4096]{1,0:T(8,128)(2,1)}, bf16[32,4096]{1,0:T(8,128)(2,1)S(1)}, u32[]{:S(2)}, u32[]{:S(2)}) collective-permute-start(bf16[32,4096]{1,0:T(8,128)(2,1)} %copy-done.8), channel_id=1, source_target_pairs={{0,2},{1,3},{2,4},{3,5},{4,6},{5,7},{6,8},{7,9},{8,10},{9,11},{10,... | collective-permute-start | bytes 786440 | tf_op jit(solution)/shard_map/ppermute | solution.py:263
  53.8 4.0 %collective-permute-start.11 = (bf16[32,4096]{1,0:T(8,128)(2,1)}, bf16[32,4096]{1,0:T(8,128)(2,1)S(1)}, u32[]{:S(2)}, u32[]{:S(2)}) collective-permute-start(bf16[32,4096]{1,0:T(8,128)(2,1)} %copy-done.6), channel_id=1, source_target_pairs={{0,14},{1,15},{2,0},{3,1},{4,2},{5,3},{6,4},{7,5},{8,6},{9,7},{10,... | collective-permute-start | bytes 786440 | tf_op jit(solution)/shard_map/ppermute | solution.py:263
  57.8 1.0 constant_dynamic-update-slice_fusion.6
  58.8 4.3 %collective-permute-done.8 = bf16[32,4096]{1,0:T(8,128)(2,1)S(1)} collective-permute-done((bf16[32,4096]{1,0:T(8,128)(2,1)}, bf16[32,4096]{1,0:T(8,128)(2,1)S(1)}, u32[]{:S(2)}, u32[]{:S(2)}) %collective-permute-start.8) | collective-permute-done | bytes 262176 | tf_op jit(solution)/shard_map/ppermute | solution.py:263
  63.1 0.0 collective-permute-start.9
  63.1 0.0 collective-permute-done.11
  63.1 2.7 %collective-permute-start.12 = (bf16[32,4096]{1,0:T(8,128)(2,1)S(1)}, bf16[32,4096]{1,0:T(8,128)(2,1)S(1)}, u32[]{:S(2)}, u32[]{:S(2)}) collective-permute-start(bf16[32,4096]{1,0:T(8,128)(2,1)S(1)} %collective-permute-done.11), channel_id=1, source_target_pairs={{0,14},{1,15},{2,0},{3,1},{4,2},{5,3},{6,4},{7,5},{8,6},{9,7},{10,... | collective-permute-start | bytes 786440 | tf_op jit(solution)/shard_map/ppermute | solution.py:263
  65.8 4.2 %collective-permute-done.9 = bf16[32,4096]{1,0:T(8,128)(2,1)S(1)} collective-permute-done((bf16[32,4096]{1,0:T(8,128)(2,1)S(1)}, bf16[32,4096]{1,0:T(8,128)(2,1)S(1)}, u32[]{:S(2)}, u32[]{:S(2)}) %collective-permute-start.9) | collective-permute-done | bytes 262176 | tf_op jit(solution)/shard_map/ppermute | solution.py:263
  70.0 6.7 %collective-permute-done.10 = bf16[32,4096]{1,0:T(8,128)(2,1)S(1)} collective-permute-done((bf16[32,4096]{1,0:T(8,128)(2,1)S(1)}, bf16[32,4096]{1,0:T(8,128)(2,1)S(1)}, u32[]{:S(2)}, u32[]{:S(2)}) %collective-permute-start.10) | collective-permute-done | bytes 262176 | tf_op jit(solution)/shard_map/ppermute | solution.py:263
  76.8 1.3 %copy-done.1 = bf16[256,4096]{1,0:T(8,128)(2,1)} copy-done((bf16[256,4096]{1,0:T(8,128)(2,1)}, bf16[256,4096]{1,0:T(8,128)(2,1)S(1)}, u32[]{:S(2)}) %copy-start.1) | copy-done | bytes 2097176
  78.1 2.8 %all-to-all-done.1 = bf16[16,32,16,128]{3,2,1,0:T(8,128)(2,1)S(1)} async-done(((bf16[16,32,16,128]{3,2,1,0:T(8,128)(2,1)}), bf16[16,32,16,128]{3,2,1,0:T(8,128)(2,1)S(1)}, u32[]{:S(2)}, u32[]{:S(2)}) %all-to-all-start.1) | async-done | bytes 2097184 | tf_op jit(solution)/shard_map/all_to_all | solution.py:284
  80.9 0.9 front.1
  81.8 0.1 reshape.137
  81.9 3.0 %collective-permute-start.13 = (bf16[2,4096]{1,0:T(2,128)(2,1)S(1)}, bf16[2,4096]{1,0:T(2,128)(2,1)S(1)}, u32[]{:S(2)}, u32[]{:S(2)}) collective-permute-start(bf16[2,4096]{1,0:T(2,128)(2,1)S(1)} %reshape.137), channel_id=1, source_target_pairs={{0,1},{1,0},{2,3},{3,2},{4,5},{5,4},{6,7},{7,6},{8,9},{9,8},{10,11... | collective-permute-start | bytes 49160 | tf_op jit(solution)/shard_map/ppermute | solution.py:294
  84.9 1.6 %copy-done.2 = bf16[256,4096]{1,0:T(8,128)(2,1)S(1)} copy-done((bf16[256,4096]{1,0:T(8,128)(2,1)S(1)}, bf16[256,4096]{1,0:T(8,128)(2,1)}, u32[]{:S(2)}) %copy-start.2) | copy-done | bytes 2097176
  86.5 0.1 stage.1.queries_ref
  86.7 1.3 %raw.1 = f32[8,4,128]{2,1,0:T(4,128)} custom-call(s32[1]{0:T(128)} %bitcast.19.place_ref, bf16[4,4096]{1,0:T(4,128)(2,1)S(1)} %pad_maximum_fusion.1.grads_ref, bf16[256,4096]{1,0:T(8,128)(2,1)S(1)} %stage.1.queries_ref), custom_call_target="tpu_custom_call" | custom-call | tf_op jit(solution)/shard_map/raw/pallas_call | solution.py:101
  88.1 8.2 %all-to-all-start.2 = ((f32[8,4,128]{2,1,0:T(4,128)}), f32[8,4,128]{2,1,0:T(4,128)S(1)}, u32[]{:S(2)}, u32[]{:S(2)}) async-start(f32[8,4,128]{2,1,0:T(4,128)} %raw.1), calls=%async_computation.2 | async-start | bytes 32768 | tf_op jit(solution)/shard_map/all_to_all | solution.py:305
  96.3 2.7 %fusion.5 = (f32[128]{0:T(128)S(1)}, f32[128]{0:T(128)S(1)}) fusion(bf16[1,128,8192]{2,1,0:T(8,128)(2,1)} %param.9, f32[8192]{0:T(1024)S(1)} %bitcast.54, bf16[128,8192]{1,0:T(8,128)(2,1)S(1)} %bitcast.45), kind=kLoop, calls=%fused_computation.11 | loop fusion | flops 7339776 | bytes 4228096 | tf_op jit(solution)/shard_map/reduce_sum | solution.py:221
  99.0 3.9 %all-to-all-done.2.parts_ref = f32[8,4,128]{2,1,0:T(4,128)S(1)} async-done(((f32[8,4,128]{2,1,0:T(4,128)}), f32[8,4,128]{2,1,0:T(4,128)S(1)}, u32[]{:S(2)}, u32[]{:S(2)}) %all-to-all-start.2) | async-done | bytes 16416 | tf_op jit(solution)/shard_map/all_to_all | solution.py:305
  102.9 0.7 fold.1
  103.6 3.5 %all-to-all-start.3 = ((f32[16,16,128]{2,1,0:T(8,128)}), f32[16,16,128]{2,1,0:T(8,128)S(1)}, u32[]{:S(2)}, u32[]{:S(2)}) async-start(f32[16,16,128]{2,1,0:T(8,128)} %fold.1), calls=%async_computation.3 | async-start | bytes 262144 | tf_op jit(solution)/shard_map/all_to_all | solution.py:311
  107.2 4.6 %fusion.9 = bf16[1,128,8192]{2,1,0:T(8,128)(2,1)} fusion(bf16[128,8192]{1,0:T(8,128)(2,1)S(1)} %bitcast.46, bf16[1,128,8192]{2,1,0:T(8,128)(2,1)} %param.9, f32[128]{0:T(128)S(1)} %broadcast_multiply_fusion, f32[128]{0:T(128)S(1)} %get-tuple-element.33, f32[8192]{0:T(1024)S(1)} %bitcast.55, f32[128]{0:T(128)S(1)} %get-tuple-element.32), kind=kLoop, calls=%fused_computation.15 | loop fusion | flops 9437184 | bytes 6325760 | tf_op jit(solution)/shard_map/broadcast_in_dim | solution.py:317
  111.8 2.2 %all-to-all-done.3.parts_ref = f32[16,16,128]{2,1,0:T(8,128)S(1)} async-done(((f32[16,16,128]{2,1,0:T(8,128)}), f32[16,16,128]{2,1,0:T(8,128)S(1)}, u32[]{:S(2)}, u32[]{:S(2)}) %all-to-all-start.3) | async-done | bytes 131104 | tf_op jit(solution)/shard_map/all_to_all | solution.py:311
  114.0 0.7 scores.1
  (34 shorter events, 0.3 us)
Async XLA Ops:
  0.6 10.8 %copy-start = (s32[2]{0:T(128)S(1)}, s32[2]{0:T(128)}, u32[]{:S(2)}) copy-start(s32[2]{0:T(128)} %param.12) | copy-start | bytes 28
  0.6 12.5 %collective-permute-start.2 = (f32[64,128]{1,0:T(8,128)}, f32[64,128]{1,0:T(8,128)S(1)}, u32[]{:S(2)}, u32[]{:S(2)}) collective-permute-start(f32[64,128]{1,0:T(8,128)} %bitcast.50), channel_id=1, source_target_pairs={{0,48},{16,0},{32,16},{48,32},{64,112},{80,64},{96,80},{112,96},{1... | collective-permute-start | bytes 98312 | tf_op jit(solution)/shard_map/ppermute | solution.py:247
  4.0 9.1 %collective-permute-start.1 = (f32[64,128]{1,0:T(8,128)}, f32[64,128]{1,0:T(8,128)S(1)}, u32[]{:S(2)}, u32[]{:S(2)}) collective-permute-start(f32[64,128]{1,0:T(8,128)} %bitcast.51), channel_id=1, source_target_pairs={{0,32},{16,48},{32,0},{48,16},{64,96},{80,112},{96,64},{112,80},{1... | collective-permute-start | bytes 98312 | tf_op jit(solution)/shard_map/ppermute | solution.py:247
  4.6 8.6 %collective-permute-start = (f32[64,128]{1,0:T(8,128)}, f32[64,128]{1,0:T(8,128)S(1)}, u32[]{:S(2)}, u32[]{:S(2)}) collective-permute-start(f32[64,128]{1,0:T(8,128)} %bitcast.52), channel_id=1, source_target_pairs={{0,16},{16,32},{32,48},{48,0},{64,80},{80,96},{96,112},{112,64},{1... | collective-permute-start | bytes 98312 | tf_op jit(solution)/shard_map/ppermute | solution.py:247
  5.2 8.0 %copy-start.4 = (f32[1,8192]{1,0:T(1,128)S(1)}, f32[1,8192]{1,0:T(1,128)}, u32[]{:S(2)}) copy-start(f32[1,8192]{1,0:T(1,128)} %param.10) | copy-start | bytes 98308
  5.2 8.0 %copy-start.5 = (bf16[1,32,4096]{2,1,0:T(8,128)(2,1)S(1)}, bf16[1,32,4096]{2,1,0:T(8,128)(2,1)}, u32[]{:S(2)}) copy-start(bf16[1,32,4096]{2,1,0:T(8,128)(2,1)} %param.15) | copy-start | bytes 786436
  5.2 34.1 %all-to-all-start = ((bf16[16,32,16,128]{3,2,1,0:T(8,128)(2,1)}), bf16[16,32,16,128]{3,2,1,0:T(8,128)(2,1)S(1)}, u32[]{:S(2)}, u32[]{:S(2)}) async-start(bf16[16,32,16,128]{3,2,1,0:T(8,128)(2,1)} %bitcast.49), calls=%async_computation | async-start | bytes 4194304 | tf_op jit(solution)/shard_map/all_to_all | solution.py:274
  13.2 16.8 %collective-permute-start.3 = (bf16[32,4096]{1,0:T(8,128)(2,1)S(1)}, bf16[32,4096]{1,0:T(8,128)(2,1)S(1)}, u32[]{:S(2)}, u32[]{:S(2)}) collective-permute-start(bf16[32,4096]{1,0:T(8,128)(2,1)S(1)} %bitcast.56), channel_id=1, source_target_pairs={{0,2},{1,3},{2,4},{3,5},{4,6},{5,7},{6,8},{7,9},{8,10},{9,11},{10,... | collective-permute-start | bytes 786440 | tf_op jit(solution)/shard_map/ppermute | solution.py:263
  14.9 15.9 %collective-permute-start.4 = (bf16[32,4096]{1,0:T(8,128)(2,1)S(1)}, bf16[32,4096]{1,0:T(8,128)(2,1)S(1)}, u32[]{:S(2)}, u32[]{:S(2)}) collective-permute-start(bf16[32,4096]{1,0:T(8,128)(2,1)S(1)} %bitcast.57), channel_id=1, source_target_pairs={{0,14},{1,15},{2,0},{3,1},{4,2},{5,3},{6,4},{7,5},{8,6},{9,7},{10,... | collective-permute-start | bytes 786440 | tf_op jit(solution)/shard_map/ppermute | solution.py:263
  18.9 21.5 %collective-permute-start.5 = (f32[4,64,128]{2,1,0:T(8,128)S(1)}, f32[4,64,128]{2,1,0:T(8,128)S(1)}, u32[]{:S(2)}, u32[]{:S(2)}) collective-permute-start(f32[4,64,128]{2,1,0:T(8,128)S(1)} %pad_maximum_fusion.refs_0_), channel_id=1, source_target_pairs={{0,64},{16,80},{32,96},{48,112},{64,128},{80,144},{96,160},{112,17... | collective-permute-start | bytes 393224 | tf_op jit(solution)/shard_map/ppermute | solution.py:247
  20.3 21.0 %collective-permute-start.6 = (f32[4,64,128]{2,1,0:T(8,128)S(1)}, f32[4,64,128]{2,1,0:T(8,128)S(1)}, u32[]{:S(2)}, u32[]{:S(2)}) collective-permute-start(f32[4,64,128]{2,1,0:T(8,128)S(1)} %pad_maximum_fusion.refs_0_), channel_id=1, source_target_pairs={{0,128},{16,144},{32,160},{48,176},{64,192},{80,208},{96,224},{112... | collective-permute-start | bytes 393224 | tf_op jit(solution)/shard_map/ppermute | solution.py:247
  22.7 18.6 %collective-permute-start.7 = (f32[4,64,128]{2,1,0:T(8,128)S(1)}, f32[4,64,128]{2,1,0:T(8,128)S(1)}, u32[]{:S(2)}, u32[]{:S(2)}) collective-permute-start(f32[4,64,128]{2,1,0:T(8,128)S(1)} %pad_maximum_fusion.refs_0_), channel_id=1, source_target_pairs={{0,192},{16,208},{32,224},{48,240},{64,0},{80,16},{96,32},{112,48}... | collective-permute-start | bytes 393224 | tf_op jit(solution)/shard_map/ppermute | solution.py:247
  30.0 0.7 copy-start.8
  30.8 14.8 %copy-start.6 = (bf16[32,4096]{1,0:T(8,128)(2,1)}, bf16[32,4096]{1,0:T(8,128)(2,1)S(1)}, u32[]{:S(2)}) copy-start(bf16[32,4096]{1,0:T(8,128)(2,1)S(1)} %collective-permute-done.4) | copy-start | bytes 786436
  45.6 35.3 %all-to-all-start.1 = ((bf16[16,32,16,128]{3,2,1,0:T(8,128)(2,1)}), bf16[16,32,16,128]{3,2,1,0:T(8,128)(2,1)S(1)}, u32[]{:S(2)}, u32[]{:S(2)}) async-start(bf16[16,32,16,128]{3,2,1,0:T(8,128)(2,1)} %chain_all.1), calls=%async_computation.1 | async-start | bytes 4194304 | tf_op jit(solution)/shard_map/all_to_all | solution.py:284
  52.0 24.8 %copy-start.7 = (bf16[32,4096]{1,0:T(8,128)(2,1)S(1)}, bf16[32,4096]{1,0:T(8,128)(2,1)}, u32[]{:S(2)}) copy-start(bf16[32,4096]{1,0:T(8,128)(2,1)} %copy-done.6) | copy-start | bytes 786436
  52.0 28.9 %copy-start.3 = (bf16[1,64,8192]{2,1,0:T(8,128)(2,1)S(1)}, bf16[1,64,8192]{2,1,0:T(8,128)(2,1)}, u32[]{:S(2)}) copy-start(bf16[1,64,8192]{2,1,0:T(8,128)(2,1)} %param.14) | copy-start | bytes 3145732
  52.1 11.0 %collective-permute-start.8 = (bf16[32,4096]{1,0:T(8,128)(2,1)}, bf16[32,4096]{1,0:T(8,128)(2,1)S(1)}, u32[]{:S(2)}, u32[]{:S(2)}) collective-permute-start(bf16[32,4096]{1,0:T(8,128)(2,1)} %copy-done.8), channel_id=1, source_target_pairs={{0,2},{1,3},{2,4},{3,5},{4,6},{5,7},{6,8},{7,9},{8,10},{9,11},{10,... | collective-permute-start | bytes 786440 | tf_op jit(solution)/shard_map/ppermute | solution.py:263
  53.8 9.3 %collective-permute-start.11 = (bf16[32,4096]{1,0:T(8,128)(2,1)}, bf16[32,4096]{1,0:T(8,128)(2,1)S(1)}, u32[]{:S(2)}, u32[]{:S(2)}) collective-permute-start(bf16[32,4096]{1,0:T(8,128)(2,1)} %copy-done.6), channel_id=1, source_target_pairs={{0,14},{1,15},{2,0},{3,1},{4,2},{5,3},{6,4},{7,5},{8,6},{9,7},{10,... | collective-permute-start | bytes 786440 | tf_op jit(solution)/shard_map/ppermute | solution.py:263
  63.1 6.9 %collective-permute-start.9 = (bf16[32,4096]{1,0:T(8,128)(2,1)S(1)}, bf16[32,4096]{1,0:T(8,128)(2,1)S(1)}, u32[]{:S(2)}, u32[]{:S(2)}) collective-permute-start(bf16[32,4096]{1,0:T(8,128)(2,1)S(1)} %collective-permute-done.8), channel_id=1, source_target_pairs={{0,2},{1,3},{2,4},{3,5},{4,6},{5,7},{6,8},{7,9},{8,10},{9,11},{10,... | collective-permute-start | bytes 786440 | tf_op jit(solution)/shard_map/ppermute | solution.py:263
  63.1 13.6 %collective-permute-start.12 = (bf16[32,4096]{1,0:T(8,128)(2,1)S(1)}, bf16[32,4096]{1,0:T(8,128)(2,1)S(1)}, u32[]{:S(2)}, u32[]{:S(2)}) collective-permute-start(bf16[32,4096]{1,0:T(8,128)(2,1)S(1)} %collective-permute-done.11), channel_id=1, source_target_pairs={{0,14},{1,15},{2,0},{3,1},{4,2},{5,3},{6,4},{7,5},{8,6},{9,7},{10,... | collective-permute-start | bytes 786440 | tf_op jit(solution)/shard_map/ppermute | solution.py:263
  69.9 6.7 %collective-permute-start.10 = (bf16[32,4096]{1,0:T(8,128)(2,1)S(1)}, bf16[32,4096]{1,0:T(8,128)(2,1)S(1)}, u32[]{:S(2)}, u32[]{:S(2)}) collective-permute-start(bf16[32,4096]{1,0:T(8,128)(2,1)S(1)} %collective-permute-done.9), channel_id=1, source_target_pairs={{0,2},{1,3},{2,4},{3,5},{4,6},{5,7},{6,8},{7,9},{8,10},{9,11},{10,... | collective-permute-start | bytes 786440 | tf_op jit(solution)/shard_map/ppermute | solution.py:263
  76.8 1.3 %copy-start.1 = (bf16[256,4096]{1,0:T(8,128)(2,1)}, bf16[256,4096]{1,0:T(8,128)(2,1)S(1)}, u32[]{:S(2)}) copy-start(bf16[256,4096]{1,0:T(8,128)(2,1)S(1)} %constant_dynamic-update-slice_fusion.queries_ref) | copy-start | bytes 6291460
  81.9 4.8 %collective-permute-start.13 = (bf16[2,4096]{1,0:T(2,128)(2,1)S(1)}, bf16[2,4096]{1,0:T(2,128)(2,1)S(1)}, u32[]{:S(2)}, u32[]{:S(2)}) collective-permute-start(bf16[2,4096]{1,0:T(2,128)(2,1)S(1)} %reshape.137), channel_id=1, source_target_pairs={{0,1},{1,0},{2,3},{3,2},{4,5},{5,4},{6,7},{7,6},{8,9},{9,8},{10,11... | collective-permute-start | bytes 49160 | tf_op jit(solution)/shard_map/ppermute | solution.py:294
  84.9 1.6 %copy-start.2 = (bf16[256,4096]{1,0:T(8,128)(2,1)S(1)}, bf16[256,4096]{1,0:T(8,128)(2,1)}, u32[]{:S(2)}) copy-start(bf16[256,4096]{1,0:T(8,128)(2,1)} %copy-done.1) | copy-start | bytes 6291460
  88.1 14.8 %all-to-all-start.2 = ((f32[8,4,128]{2,1,0:T(4,128)}), f32[8,4,128]{2,1,0:T(4,128)S(1)}, u32[]{:S(2)}, u32[]{:S(2)}) async-start(f32[8,4,128]{2,1,0:T(4,128)} %raw.1), calls=%async_computation.2 | async-start | bytes 32768 | tf_op jit(solution)/shard_map/all_to_all | solution.py:305
  103.6 10.3 %all-to-all-start.3 = ((f32[16,16,128]{2,1,0:T(8,128)}), f32[16,16,128]{2,1,0:T(8,128)S(1)}, u32[]{:S(2)}, u32[]{:S(2)}) async-start(f32[16,16,128]{2,1,0:T(8,128)} %fold.1), calls=%async_computation.3 | async-start | bytes 262144 | tf_op jit(solution)/shard_map/all_to_all | solution.py:311
